TPU v7x, 32 devices: a whole 2x2x4 slice. The times are simulated.
32 devices in a mesh: groups: 2 (over x), ao: 16 (over z, y, core).
Axes of the slice: x: 2, y: 2, z: 4, core: 2. Of those that a mesh axis runs over, the one named last changes fastest.
Arguments:
- tiles: bfloat16 [64, 128, 128, 128], P('ao', None, 'groups'), parts along dimension 2, may hold values from -6 to 6
- pairs: int32 [64, 2], replicated, may hold values from 0 to 63, as said below
- occ_coef: bfloat16 [6144, 8], replicated, may hold values from -0.3125 to 0.3125
- vir_coef: bfloat16 [6144, 4864], P(None, 'ao'), may hold values from -0.078125 to 0.078125
Outputs:
- pair_ints: bfloat16 [4864, 1024], P('ao', 'groups'), parts along dimension 1
There are 2 independent parts, one for each index of `groups`. A program takes and returns all parts, laid end to end along the dimension named above; an argument that names none is the same for every part. Nothing has to cross between parts.
Inputs may be any that keep to these rules, and one draw needn't show every extreme that they name: `pairs`: device d of ao holds tiles d * 4 to (d + 1) * 4 - 1. The column groups of one device's tiles are 4 consecutive groups (modulo 64); the row group of a tile differs from its column group by at most 3, cyclically.
All inputs are finite; a program needn't handle non-finite values.
Results may differ from a plain program's by a relative error of at most 0.0056.
Values may be sent and summed in bfloat16 or wider, within the bound.
No kernel may reach another device: no remote copies, remote signals or barrier semaphores. Data moves between devices by JAX's collectives and lax.ppermute only.
A program may use at most 128 MiB of HBM per device.

v0:
```python
import jax
import jax.numpy as jnp
from jax import lax
from jax.sharding import PartitionSpec as P

NGROUP = 64
AO_GROUP = 96


def on_device(tiles, pairs, occ_coef, vir_coef):
    count_dev = tiles.shape[0]
    tile_edge = tiles.shape[1]
    ri_width = tiles.shape[2]
    occ_batch = occ_coef.shape[1]
    col_width = occ_batch * ri_width
    device_index = lax.axis_index("ao")
    my_pairs = lax.dynamic_slice_in_dim(pairs, device_index * count_dev, count_dev, 0)
    group_coef = occ_coef.reshape(NGROUP, AO_GROUP, occ_batch)
    coef_rows = group_coef[my_pairs[:, 0]]
    coef_rows = jnp.pad(coef_rows, ((0, 0), (0, tile_edge - AO_GROUP), (0, 0)))
    half_full = jnp.einsum("tri,trqc->tciq", coef_rows, tiles, preferred_element_type=jnp.float32)
    half_ints = half_full[:, :AO_GROUP].reshape(count_dev, AO_GROUP, col_width).astype(jnp.bfloat16)
    received = lax.all_to_all(half_ints, "ao", split_axis=2, concat_axis=0, tiled=True)
    select = (pairs[:, 1][None, :] == jnp.arange(NGROUP)[:, None]).astype(jnp.bfloat16)
    column_sum = jnp.einsum("gt,tck->gck", select, received, preferred_element_type=jnp.float32)
    column_sum = column_sum.reshape(NGROUP * AO_GROUP, received.shape[2]).astype(jnp.bfloat16)
    x_own = lax.all_to_all(column_sum, "ao", split_axis=0, concat_axis=1, tiled=True)
    product = lax.dot_general(
        vir_coef,
        lax.all_gather(x_own, "ao", axis=0, tiled=True),
        (((0,), (0,)), ((), ())),
        preferred_element_type=jnp.float32,
    )
    return product.astype(jnp.bfloat16)


def solution(mesh):
    return jax.shard_map(
        on_device,
        mesh=mesh,
        in_specs=(P("ao", None, "groups", None), P(), P(), P(None, "ao")),
        out_specs=P("ao", "groups"),
        check_vma=False,
    )
```

profile of v0, /device:TPU:0, one launch (start us, length us, event | category | flops | bytes accessed | tf_op | source)
XLA Modules:
  0.0 135.8 jit_solution(5112329516828948614)
XLA Ops:
  6.5 0.7 constant_dynamic-slice_fusion
  7.3 1.1 reshape.12
  8.4 0.1 copy.15
  8.5 0.6 gather_fusion
  9.0 0.0 copy-start
  9.0 7.9 %fusion.5 = bf16[4,128,8,64]{1,2,3,0:T(8,128)(2,1)S(1)} fusion(bf16[4,128,64,128]{3,2,1,0:T(8,128)(2,1)} %param.4, bf16[4,96,8]{1,2,0:T(8,128)(2,1)S(1)} %gather_fusion), kind=kOutput, calls=%fused_computation.5 | convolution fusion | flops 67371008 | bytes 8919040 | tf_op jit(solution)/shard_map/tri,trqc->tciq/dot_general | solution.py:21
  16.9 0.1 copy.17
  17.0 1.2 copy.18
  18.2 7.4 %all-to-all-start = ((bf16[4,96,512]{1,0,2:T(4,128)(2,1)}), bf16[4,96,512]{1,0,2:T(4,128)(2,1)S(1)}, u32[]{:S(2)}, u32[]{:S(2)}) async-start(bf16[4,96,512]{1,0,2:T(4,128)(2,1)} %copy.18), calls=%async_computation | async-start | bytes 1048576 | tf_op jit(solution)/shard_map/all_to_all | solution.py:23
  25.6 0.0 all-gather.2.cloned.1.call-start
  25.7 0.0 copy-done
  25.7 14.4 %all-to-all-done = bf16[4,96,512]{1,0,2:T(4,128)(2,1)S(1)} async-done(((bf16[4,96,512]{1,0,2:T(4,128)(2,1)}), bf16[4,96,512]{1,0,2:T(4,128)(2,1)S(1)}, u32[]{:S(2)}, u32[]{:S(2)}) %all-to-all-start) | async-done | bytes 393248 | tf_op jit(solution)/shard_map/all_to_all | solution.py:23
  40.1 0.1 copy.19
  40.2 0.4 copy.20
  40.6 0.3 convolution_convert_fusion
  40.9 0.4 convert_element_type.22
  41.2 0.1 copy.21
  41.3 16.2 %all_to_all.34 = bf16[16,384,32]{1,2,0:T(8,128)(2,1)} all-to-all(bf16[16,384,32]{1,2,0:T(8,128)(2,1)S(1)} %copy.21), channel_id=1, replica_groups=mesh['groups'=2,'ao'=16] {'ao'}, dimensions={0} | all-to-all | bytes 786432 | tf_op jit(solution)/shard_map/all_to_all | solution.py:27
  57.5 0.0 all-gather.2.cloned.1.call-update
  57.5 64.7 %all-gather.2.cloned.1.call-done = bf16[6144,512]{0,1:T(8,128)(2,1)} async-done(((bf16[384,512]{0,1:T(8,128)(2,1)}), bf16[6144,512]{0,1:T(8,128)(2,1)}) %all-gather.2.cloned.1.call-update) | async-done | bytes 6291472 | tf_op jit(solution)/shard_map/all_gather | solution.py:30
  122.2 6.7 %fusion.8 = bf16[304,512]{1,0:T(8,128)(2,1)} fusion(bf16[6144,512]{0,1:T(8,128)(2,1)} %all-gather.2.cloned.1.call-done, bf16[6144,304]{0,1:T(8,128)(2,1)} %param.7), kind=kOutput, calls=%fused_computation.7 | convolution fusion | flops 1912758272 | bytes 10338304 | tf_op jit(solution)/shard_map/dot_general | solution.py:28
  (3 shorter events, 0.0 us)
Async XLA Ops:
  9.0 16.6 %copy-start = (s32[64,2]{0,1:T(2,128)S(1)}, s32[64,2]{0,1:T(2,128)}, u32[]{:S(2)}) copy-start(s32[64,2]{0,1:T(2,128)} %param.5) | copy-start | bytes 1540
  18.2 21.9 %all-to-all-start = ((bf16[4,96,512]{1,0,2:T(4,128)(2,1)}), bf16[4,96,512]{1,0,2:T(4,128)(2,1)S(1)}, u32[]{:S(2)}, u32[]{:S(2)}) async-start(bf16[4,96,512]{1,0,2:T(4,128)(2,1)} %copy.18), calls=%async_computation | async-start | bytes 1048576 | tf_op jit(solution)/shard_map/all_to_all | solution.py:23
  25.6 96.6 %all-gather.2.cloned.1.call-start = ((), (), s32[]{:S(2)}) async-start(), calls=%async_computation.2 | async-start | bytes 6684672 | tf_op jit(solution)/shard_map/all_gather | solution.py:30
Sparse Core Ops, SparseCore 0:
  57.7 64.4 all-gather.1
where the time goes:
time: 136 us
  waiting for transfers between devices  79.1 us (58%)
  blocking collectives  16.2 us (12%)
  matrix products  14.9 us (11%)
  between operations  13.5 us (10%)
  starting transfers between devices  7.43 us (5%)
  local copies, waits for them, and re-layouts  4.7 us (3%)
    all_gather x1, waiting for transfers between devices, on_device(): lax.all_gather(x_own, 'ao', axis=0, tiled=True)  64.7 us
    all_to_all x1, blocking collectives, on_device(): lax.all_to_all(column_sum, 'ao', split_axis=0, concat_axis=1, tiled=True)  16.2 us
    all_to_all x1, waiting for transfers between devices, on_device(): lax.all_to_all(half_ints, 'ao', split_axis=2, concat_axis=0, tiled=True)  14.4 us
    dot_general x1, matrix products, on_device(): jnp.einsum('tri,trqc->tciq', coef_rows, tiles, preferred_element_type=jnp...  7.87 us
    all_to_all x1, starting transfers between devices, on_device(): lax.all_to_all(half_ints, 'ao', split_axis=2, concat_axis=0, tiled=True)  7.39 us
    dot_general x1, matrix products, on_device(): lax.dot_general(vir_coef, lax.all_gather(x_own, 'ao', axis=0, tiled=True)...  6.72 us
  transfers between devices with their start and end apart: 2, of which 2 were waited for; matrix products, arithmetic and copies ran while one was open for 0% of the time, Pallas kernels for 0%

commit v1 on v0

v1 whole, which is shorter than its diff:
```python
import functools

import jax
import jax.numpy as jnp
from jax import lax
from jax.experimental import pallas as pl
from jax.experimental.pallas import tpu as pltpu
from jax.sharding import PartitionSpec as P

NGROUP = 64
AO_GROUP = 96
LANES = 128
QB = 16
CHUNKS = 2
VMEM_LIMIT = 48 * 1024 * 1024


def first_group(pairs, dev, count):
    cols = [pairs[1, dev * count + j] for j in range(count)]
    first = cols[0]
    for col in cols[1:]:
        before = lax.rem(col + (NGROUP - 1), NGROUP)
        is_first = functools.reduce(jnp.logical_and, [other != before for other in cols])
        first = jnp.where(is_first, col, first)
    before = lax.rem(cols[0] + (NGROUP - 1), NGROUP)
    is_first = functools.reduce(jnp.logical_and, [other != before for other in cols])
    return jnp.where(is_first, cols[0], first)


def tile_of_slot(pairs, dev, count, slot):
    wanted = lax.rem(first_group(pairs, dev, count) + slot, NGROUP)
    found = jnp.int32(0)
    for j in range(1, count):
        found = jnp.where(pairs[1, dev * count + j] == wanted, j, found)
    return found


def half_kernel(count, occ_batch, pairs, me, occ_ref, tile_ref, out_ref, spread, held):
    slot = pl.program_id(0)
    width = AO_GROUP * QB
    q_chunk = tile_ref.shape[2]

    @pl.when(slot == 0)
    def _():
        row = lax.broadcasted_iota(jnp.int32, (LANES, width), 0)
        lane = lax.broadcasted_iota(jnp.int32, (LANES, width), 1)
        spread[...] = (lane // QB == row).astype(jnp.bfloat16)

    tile = tile_of_slot(pairs, me[0], count, slot)
    offset = pairs[0, me[0] * count + tile] * AO_GROUP
    start = pl.multiple_of(offset // LANES * LANES, LANES)
    last = occ_ref.shape[1] - LANES
    after = pl.multiple_of(jnp.minimum(start + LANES, last), LANES)
    shift = offset - start
    low = occ_ref[:, pl.ds(start, LANES)].astype(jnp.float32)
    high = occ_ref[:, pl.ds(after, LANES)].astype(jnp.float32)
    turn = lax.rem(LANES - shift, LANES)
    low, high = pltpu.roll(low, turn, 1), pltpu.roll(high, turn, 1)
    lane = lax.broadcasted_iota(jnp.int32, low.shape, 1)
    coef = jnp.where(lane < LANES - shift, low, high).astype(jnp.bfloat16)
    wide = jnp.dot(coef, spread[...], preferred_element_type=jnp.float32)
    wide = jnp.broadcast_to(wide[:, None, :], (occ_batch, QB, width))
    q_row = lax.broadcasted_iota(jnp.int32, wide.shape, 1)
    q_col = lax.broadcasted_iota(jnp.int32, wide.shape, 2) % QB
    kron = jnp.where(q_row == q_col, wide, 0.0).reshape(occ_batch * QB, width).astype(jnp.bfloat16)
    for block in range(q_chunk // QB):
        part = tile_ref[0, :, block * QB : (block + 1) * QB, :].reshape(width, LANES)
        half = jnp.dot(kron, part, preferred_element_type=jnp.float32)
        held[slot, :, block * QB : (block + 1) * QB, :] = half.reshape(occ_batch, QB, LANES)

    @pl.when(slot == count - 1)
    def _():
        rows = occ_batch * q_chunk
        lane = lax.broadcasted_iota(jnp.int32, (rows, LANES), 1)
        pieces = [held[s].reshape(rows, LANES) for s in range(count)]
        for out in range(count * AO_GROUP // LANES):
            value = None
            for s in range(count):
                begin, end = s * AO_GROUP - out * LANES, (s + 1) * AO_GROUP - out * LANES
                if end <= 0 or begin >= LANES:
                    continue
                turned = pieces[s] if begin % LANES == 0 else pltpu.roll(pieces[s], begin % LANES, 1)
                value = turned if value is None else jnp.where(lane < begin, value, turned)
            out_ref[:, out * LANES : (out + 1) * LANES] = value.astype(out_ref.dtype)


def half_chunk(pairs, me, occ, tiles, chunk):
    count, ri_width = tiles.shape[0], tiles.shape[2]
    occ_batch = occ.shape[0]
    q_chunk = ri_width // CHUNKS
    rows, columns = occ_batch * q_chunk, count * AO_GROUP
    return pl.pallas_call(
        functools.partial(half_kernel, count, occ_batch),
        grid_spec=pltpu.PrefetchScalarGridSpec(
            num_scalar_prefetch=2,
            grid=(count,),
            in_specs=[
                pl.BlockSpec(occ.shape, lambda s, pairs, me: (0, 0)),
                pl.BlockSpec(
                    (1, AO_GROUP, q_chunk, LANES),
                    lambda s, pairs, me: (tile_of_slot(pairs, me[0], count, s), 0, chunk, 0),
                ),
            ],
            out_specs=pl.BlockSpec((rows, columns), lambda s, pairs, me: (0, 0)),
            scratch_shapes=[
                pltpu.VMEM((LANES, AO_GROUP * QB), jnp.bfloat16),
                pltpu.VMEM((count, occ_batch, q_chunk, LANES), jnp.float32),
            ],
        ),
        out_shape=jax.ShapeDtypeStruct((rows, columns), jnp.bfloat16),
        compiler_params=pltpu.CompilerParams(vmem_limit_bytes=VMEM_LIMIT),
        cost_estimate=pl.CostEstimate(
            flops=2 * rows * columns * AO_GROUP * QB, bytes_accessed=tiles.size, transcendentals=0
        ),
        name="half_transform",
    )(pairs, me, occ, tiles)


def chip_of(place, chips):
    return jnp.where(place < chips // 2, 2 * place, 2 * (chips - 1 - place) + 1)


def place_of(chip, chips):
    return jnp.where(lax.rem(chip, 2) == 0, chip // 2, chips - 1 - chip // 2)


def source_chip(chip, step, chips):
    away = (step + 1) // 2
    away = jnp.where(lax.rem(step, 2) == 1, chips - away, away)
    return chip_of(lax.rem(place_of(chip, chips) + away, chips), chips)


def window_kernel(count, chips, pairs, me, vir_ref, own_ref, other_ref):
    step = pl.program_id(0)
    chip, core = me[0] // 2, lax.rem(me[0], 2)
    source = source_chip(chip, step, chips)
    tiles_all = vir_ref.shape[1] // LANES
    for dev, out_ref in ((2 * source + core, own_ref), (2 * source + 1 - core, other_ref)):
        offset = first_group(pairs, dev, count) * AO_GROUP
        start = offset // LANES
        shift = offset - start * LANES
        turn = lax.rem(LANES - shift, LANES)
        lane = lax.broadcasted_iota(jnp.int32, (vir_ref.shape[0], LANES), 1)
        before = None
        for j in range(count * AO_GROUP // LANES + 1):
            at = pl.multiple_of(lax.rem(start + j, tiles_all) * LANES, LANES)
            turned = pltpu.roll(vir_ref[:, pl.ds(at, LANES)].astype(jnp.float32), turn, 1)
            if before is not None:
                value = jnp.where(lane < LANES - shift, before, turned)
                out_ref[:, (j - 1) * LANES : j * LANES] = value.astype(out_ref.dtype)
            before = turned


def windows(pairs, me, vir, count, chips):
    rows, columns = vir.shape[0], count * AO_GROUP
    shape = jax.ShapeDtypeStruct((rows, chips * columns), vir.dtype)
    spec = pl.BlockSpec((rows, columns), lambda k, pairs, me: (0, k))
    return pl.pallas_call(
        functools.partial(window_kernel, count, chips),
        grid_spec=pltpu.PrefetchScalarGridSpec(
            num_scalar_prefetch=2,
            grid=(chips,),
            in_specs=[pl.BlockSpec(vir.shape, lambda k, pairs, me: (0, 0))],
            out_specs=[spec, spec],
        ),
        out_shape=[shape, shape],
        compiler_params=pltpu.CompilerParams(vmem_limit_bytes=VMEM_LIMIT),
        cost_estimate=pl.CostEstimate(flops=0, bytes_accessed=6 * vir.size, transcendentals=0),
        name="vir_windows",
    )(pairs, me, vir)


def join_kernel(occ_batch, *refs):
    out_ref = refs[-1]
    sums = [refs[c][...] + refs[CHUNKS + c][...] for c in range(CHUNKS)]
    q_chunk = sums[0].shape[1] // occ_batch
    rows = sums[0].shape[0]
    lane = lax.broadcasted_iota(jnp.int32, (rows, LANES), 1)
    per_tile = LANES // q_chunk
    for out in range(out_ref.shape[1] // LANES):
        value = None
        for piece in range(per_tile):
            i, c = divmod(out * per_tile + piece, CHUNKS)
            tile, at = divmod(i * q_chunk, LANES)
            part = sums[c][:, tile * LANES : (tile + 1) * LANES]
            turn = (piece * q_chunk - at) % LANES
            part = part if turn == 0 else pltpu.roll(part, turn, 1)
            value = part if value is None else jnp.where(lane < piece * q_chunk, value, part)
        out_ref[:, out * LANES : (out + 1) * LANES] = value.astype(out_ref.dtype)


def join(own, received, occ_batch):
    rows, columns = own[0].shape
    return pl.pallas_call(
        functools.partial(join_kernel, occ_batch),
        out_shape=jax.ShapeDtypeStruct((rows, CHUNKS * columns), jnp.bfloat16),
        compiler_params=pltpu.CompilerParams(vmem_limit_bytes=VMEM_LIMIT),
        name="join_cores",
    )(*own, *received)


def on_device(chips, tiles, pairs, occ_coef, vir_coef):
    count = tiles.shape[0]
    occ_batch = occ_coef.shape[1]
    columns = count * AO_GROUP
    me = lax.axis_index("ao").astype(jnp.int32).reshape(1)
    pairs, occ, vir = pairs.T, occ_coef.T, vir_coef.T

    ring = [2 * p if p < chips // 2 else 2 * (chips - 1 - p) + 1 for p in range(chips)]
    forward = [(2 * ring[p] + c, 2 * ring[(p + 1) % chips] + c) for p in range(chips) for c in (0, 1)]
    backward = [(b, a) for a, b in forward]
    across = [(d, d ^ 1) for d in range(2 * chips)]

    ahead = [half_chunk(pairs, me, occ, tiles, c) for c in range(CHUNKS)]
    behind = list(ahead)
    own_w, other_w = windows(pairs, me, vir, count, chips)
    other_w = lax.ppermute(other_w, "ao", across)

    sums = [[None, None] for _ in range(CHUNKS)]

    def use(c, step, block):
        for which, w in enumerate((own_w, other_w)):
            term = lax.dot_general(
                w[:, step * columns : (step + 1) * columns],
                block,
                (((1,), (1,)), ((), ())),
                preferred_element_type=jnp.float32,
            )
            sums[c][which] = term if sums[c][which] is None else sums[c][which] + term

    for c in range(CHUNKS):
        use(c, 0, ahead[c])
    for away in range(1, chips // 2):
        for c in range(CHUNKS):
            ahead[c] = lax.ppermute(ahead[c], "ao", forward)
            behind[c] = lax.ppermute(behind[c], "ao", backward)
        for c in range(CHUNKS):
            use(c, 2 * away - 1, ahead[c])
            use(c, 2 * away, behind[c])
    for c in range(CHUNKS):
        last = lax.ppermute(ahead[c], "ao", forward) if c < CHUNKS // 2 else lax.ppermute(behind[c], "ao", backward)
        use(c, chips - 1, last)

    received = [lax.ppermute(sums[c][1], "ao", across) for c in range(CHUNKS)]
    return join([sums[c][0] for c in range(CHUNKS)], received, occ_batch)


def solution(mesh):
    return jax.shard_map(
        functools.partial(on_device, mesh.shape["ao"] // 2),
        mesh=mesh,
        in_specs=(P("ao", None, "groups", None), P(), P(), P(None, "ao")),
        out_specs=P("ao", "groups"),
        check_vma=False,
    )
```

time: 136 us -> 55 us (0.40)
  waiting for transfers between devices: 79.1 us -> 10.9 us
  Pallas kernels: 0 us -> 17.5 us
  blocking collectives: 16.2 us -> 0 us
  between operations: 13.5 us -> 0.34 us
  starting transfers between devices: 7.43 us -> 15.8 us
  matrix products: 14.9 us -> 8.52 us
  local copies, waits for them, and re-layouts: 4.7 us -> 1.57 us
    all_gather x1 -> x0, waiting for transfers between devices: 64.7 us -> none  [on_device(): lax.all_gather(x_own, 'ao', axis=0, tiled=True)]
    pallas_call x0 -> x4, Pallas kernels: none -> 17.5 us  [the longest x2 10.6 us: half_chunk(): pl.pallas_call(functools.partial(half_kernel, count, occ_batch), grid_spe...]
    all_to_all x1 -> x0, blocking collectives: 16.2 us -> none  [on_device(): lax.all_to_all(column_sum, 'ao', split_axis=0, concat_axis=1, tiled=True)]
    ppermute x0 -> x17, starting transfers between devices: none -> 15.8 us  [the longest x6 12.3 us: on_device(): behind[c] = lax.ppermute(behind[c], 'ao', backward)]
    all_to_all x1 -> x0, waiting for transfers between devices: 14.4 us -> none  [on_device(): lax.all_to_all(half_ints, 'ao', split_axis=2, concat_axis=0, tiled=True)]
    ppermute x0 -> x17, waiting for transfers between devices: none -> 10.9 us  [the longest x6 5.83 us: on_device(): behind[c] = lax.ppermute(behind[c], 'ao', backward)]
    all_to_all x1 -> x0, starting transfers between devices: 7.39 us -> none  [on_device(): lax.all_to_all(half_ints, 'ao', split_axis=2, concat_axis=0, tiled=True)]
    dot_general x3 -> x32, matrix products: 14.9 us -> 8.52 us  [use(): lax.dot_general(w[:, step * columns:(step + 1) * columns], block, (((1,),...]
  transfers between devices with their start and end apart: 2 -> 17, of which waited for: 2 -> 6; matrix products, arithmetic and copies ran while one was open for 0% -> 16% of each run, Pallas kernels for 0% -> 20%
where the time goes in v1:
time: 55 us; the launch traced here: 54.7 us
  Pallas kernels  17.5 us (32%)
  starting transfers between devices  15.8 us (29%)
  waiting for transfers between devices  10.9 us (20%)
  matrix products  8.52 us (15%)
  local copies, waits for them, and re-layouts  1.57 us (3%)
    ppermute x6, starting transfers between devices, on_device(): behind[c] = lax.ppermute(behind[c], 'ao', backward)  12.3 us
    pallas_call x2, Pallas kernels, half_chunk(): pl.pallas_call(functools.partial(half_kernel, count, occ_batch), grid_spe...  10.6 us
    dot_general x32, matrix products, use(): lax.dot_general(w[:, step * columns:(step + 1) * columns], block, (((1,),...  8.52 us
    ppermute x6, waiting for transfers between devices, on_device(): behind[c] = lax.ppermute(behind[c], 'ao', backward)  5.83 us
    pallas_call x1, Pallas kernels, windows(): pl.pallas_call(functools.partial(window_kernel, count, chips), grid_spec=...  5.82 us
    ppermute x6, waiting for transfers between devices, on_device(): ahead[c] = lax.ppermute(ahead[c], 'ao', forward)  3.6 us
    ppermute x1, starting transfers between devices, on_device(): lax.ppermute(behind[c], 'ao', backward)  1.79 us
    unnamed x4, local copies, waits for them, and re-layouts  1.57 us
  transfers between devices with their start and end apart: 17, of which 6 were waited for; matrix products, arithmetic and copies ran while one was open for 16% of the time, Pallas kernels for 20%

profile of v1, /device:TPU:0, one launch (start us, length us, event | category | flops | bytes accessed | tf_op | source)
XLA Modules:
  0.0 54.7 jit_solution(6890579449073287794)
XLA Ops:
  0.0 0.9 %copy-done = bf16[6144,8]{0,1:T(8,128)(2,1)S(1)} copy-done((bf16[6144,8]{0,1:T(8,128)(2,1)S(1)}, bf16[6144,8]{0,1:T(8,128)(2,1)}, u32[]{:S(2)}) %copy-start) | copy-done | bytes 98328
  0.9 0.7 %copy-done.1 = s32[64,2]{0,1:T(2,128)S(1)} copy-done((s32[64,2]{0,1:T(2,128)S(1)}, s32[64,2]{0,1:T(2,128)}, u32[]{:S(2)}) %copy-start.1) | copy-done | bytes 536
  1.6 5.3 %half_transform.3 = bf16[256,384]{1,0:T(8,128)(2,1)S(1)} custom-call(s32[2,64]{1,0:T(2,128)S(1)} %bitcast.38, s32[1]{0:T(128)} %bitcast.1.me, bf16[8,6144]{1,0:T(8,128)(2,1)S(1)} %bitcast.36, bf16[4,128,64,128]{3,2,1,0:T(8,128)(2,1)} %tile_ref.3), custom_call_target="tpu_custom_call" | custom-call | flops 301989888 | bytes 4194304 | tf_op jit(solution)/shard_map/half_transform/pallas_call | solution.py:92
  6.9 3.0 %collective-permute-start.8 = (bf16[256,384]{1,0:T(8,128)(2,1)S(1)}, bf16[256,384]{1,0:T(8,128)(2,1)S(1)}, u32[]{:S(2)}, u32[]{:S(2)}) collective-permute-start(bf16[256,384]{1,0:T(8,128)(2,1)S(1)} %half_transform.3), channel_id=1, source_target_pairs={{4,0},{5,1},{8,4},{9,5},{12,8},{13,9},{14,12},{15,13},{10,14},{11,... | collective-permute-start | bytes 589832 | tf_op jit(solution)/shard_map/ppermute | solution.py:236
  10.0 5.3 %half_transform.2 = bf16[256,384]{1,0:T(8,128)(2,1)S(1)} custom-call(s32[2,64]{1,0:T(2,128)S(1)} %bitcast.39, s32[1]{0:T(128)} %bitcast.1.me, bf16[8,6144]{1,0:T(8,128)(2,1)S(1)} %bitcast.37, bf16[4,128,64,128]{3,2,1,0:T(8,128)(2,1)} %tile_ref.3), custom_call_target="tpu_custom_call" | custom-call | flops 301989888 | bytes 4194304 | tf_op jit(solution)/shard_map/half_transform/pallas_call | solution.py:92
  15.4 1.9 %collective-permute-start.1 = (bf16[256,384]{1,0:T(8,128)(2,1)S(1)}, bf16[256,384]{1,0:T(8,128)(2,1)S(1)}, u32[]{:S(2)}, u32[]{:S(2)}) collective-permute-start(bf16[256,384]{1,0:T(8,128)(2,1)S(1)} %half_transform.2), channel_id=1, source_target_pairs={{4,0},{5,1},{8,4},{9,5},{12,8},{13,9},{14,12},{15,13},{10,14},{11,... | collective-permute-start | bytes 589832 | tf_op jit(solution)/shard_map/ppermute | solution.py:236
  17.4 5.8 %vir_windows.1 = (bf16[304,3072]{1,0:T(8,128)(2,1)S(1)}, bf16[304,3072]{1,0:T(8,128)(2,1)S(1)}) custom-call(s32[2,64]{1,0:T(2,128)S(1)} %bitcast.40, s32[1]{0:T(128)} %bitcast.1.me, bf16[304,6144]{1,0:T(8,128)(2,1)} %bitcast.41), custom_call_target="tpu_custom_call" | custom-call | bytes 11206656 | tf_op jit(solution)/shard_map/vir_windows/pallas_call | solution.py:158
  23.3 0.3 fusion.52
  23.6 0.3 fusion.54
  23.9 1.9 %collective-permute-start.10 = (bf16[256,384]{1,0:T(8,128)(2,1)S(1)}, bf16[256,384]{1,0:T(8,128)(2,1)S(1)}, u32[]{:S(2)}, u32[]{:S(2)}) collective-permute-start(bf16[256,384]{1,0:T(8,128)(2,1)S(1)} %collective-permute-done.8), channel_id=1, source_target_pairs={{4,0},{5,1},{8,4},{9,5},{12,8},{13,9},{14,12},{15,13},{10,14},{11,... | collective-permute-start | bytes 589832 | tf_op jit(solution)/shard_map/ppermute | solution.py:236
  26.0 1.9 %collective-permute-start.3 = (bf16[256,384]{1,0:T(8,128)(2,1)S(1)}, bf16[256,384]{1,0:T(8,128)(2,1)S(1)}, u32[]{:S(2)}, u32[]{:S(2)}) collective-permute-start(bf16[256,384]{1,0:T(8,128)(2,1)S(1)} %collective-permute-done.1), channel_id=1, source_target_pairs={{4,0},{5,1},{8,4},{9,5},{12,8},{13,9},{14,12},{15,13},{10,14},{11,... | collective-permute-start | bytes 589832 | tf_op jit(solution)/shard_map/ppermute | solution.py:236
  28.0 0.3 convolution_add_fusion.12
  28.3 0.3 convolution_add_fusion.11
  28.6 0.3 convolution_add_fusion.17
  28.8 0.3 convolution_add_fusion.16
  29.1 2.6 %collective-permute-done.10 = bf16[256,384]{1,0:T(8,128)(2,1)S(1)} collective-permute-done((bf16[256,384]{1,0:T(8,128)(2,1)S(1)}, bf16[256,384]{1,0:T(8,128)(2,1)S(1)}, u32[]{:S(2)}, u32[]{:S(2)}) %collective-permute-start.10) | collective-permute-done | bytes 196640 | tf_op jit(solution)/shard_map/ppermute | solution.py:236
  31.7 1.8 %collective-permute-start.12 = (bf16[256,384]{1,0:T(8,128)(2,1)S(1)}, bf16[256,384]{1,0:T(8,128)(2,1)S(1)}, u32[]{:S(2)}, u32[]{:S(2)}) collective-permute-start(bf16[256,384]{1,0:T(8,128)(2,1)S(1)} %collective-permute-done.10), channel_id=1, source_target_pairs={{4,0},{5,1},{8,4},{9,5},{12,8},{13,9},{14,12},{15,13},{10,14},{11,... | collective-permute-start | bytes 589832 | tf_op jit(solution)/shard_map/ppermute | solution.py:236
  33.8 0.3 collective-permute-start.11
  34.1 1.9 %collective-permute-done.3 = bf16[256,384]{1,0:T(8,128)(2,1)S(1)} collective-permute-done((bf16[256,384]{1,0:T(8,128)(2,1)S(1)}, bf16[256,384]{1,0:T(8,128)(2,1)S(1)}, u32[]{:S(2)}, u32[]{:S(2)}) %collective-permute-start.3) | collective-permute-done | bytes 196640 | tf_op jit(solution)/shard_map/ppermute | solution.py:236
  35.9 1.8 %collective-permute-start.5 = (bf16[256,384]{1,0:T(8,128)(2,1)S(1)}, bf16[256,384]{1,0:T(8,128)(2,1)S(1)}, u32[]{:S(2)}, u32[]{:S(2)}) collective-permute-start(bf16[256,384]{1,0:T(8,128)(2,1)S(1)} %collective-permute-done.3), channel_id=1, source_target_pairs={{4,0},{5,1},{8,4},{9,5},{12,8},{13,9},{14,12},{15,13},{10,14},{11,... | collective-permute-start | bytes 589832 | tf_op jit(solution)/shard_map/ppermute | solution.py:236
  38.0 0.3 fusion.44
  38.2 0.3 fusion.7
  38.5 0.3 fusion.9
  38.8 1.3 %collective-permute-done.12 = bf16[256,384]{1,0:T(8,128)(2,1)S(1)} collective-permute-done((bf16[256,384]{1,0:T(8,128)(2,1)S(1)}, bf16[256,384]{1,0:T(8,128)(2,1)S(1)}, u32[]{:S(2)}, u32[]{:S(2)}) %collective-permute-start.12) | collective-permute-done | bytes 196640 | tf_op jit(solution)/shard_map/ppermute | solution.py:236
  40.1 1.8 %collective-permute-start.13 = (bf16[256,384]{1,0:T(8,128)(2,1)S(1)}, bf16[256,384]{1,0:T(8,128)(2,1)S(1)}, u32[]{:S(2)}, u32[]{:S(2)}) collective-permute-start(bf16[256,384]{1,0:T(8,128)(2,1)S(1)} %collective-permute-done.12), channel_id=1, source_target_pairs={{4,0},{5,1},{8,4},{9,5},{12,8},{13,9},{14,12},{15,13},{10,14},{11,... | collective-permute-start | bytes 589832 | tf_op jit(solution)/shard_map/ppermute | solution.py:241
  41.9 3.5 %collective-permute-done.4 = bf16[256,384]{1,0:T(8,128)(2,1)S(1)} collective-permute-done((bf16[256,384]{1,0:T(8,128)(2,1)S(1)}, bf16[256,384]{1,0:T(8,128)(2,1)S(1)}, u32[]{:S(2)}, u32[]{:S(2)}) %collective-permute-start.4) | collective-permute-done | bytes 196640 | tf_op jit(solution)/shard_map/ppermute | solution.py:235
  45.5 0.4 collective-permute-start.6
  45.9 0.3 fusion.38
  46.2 0.3 fusion.8
  46.5 0.3 fusion.36
  46.8 0.3 fusion.6
  47.0 0.3 fusion.24
  47.6 0.3 fusion.18
  48.1 0.3 fusion.2
  48.4 0.3 fusion.1
  48.7 0.3 fusion
  49.0 0.3 convolution_add_fusion
  49.3 0.3 fusion.26
  49.6 0.3 fusion.30
  49.9 0.3 fusion.20
  50.4 0.3 fusion.5
  50.7 0.3 fusion.4
  50.9 0.3 fusion.3
  51.2 0.5 collective-permute-done.6
  52.1 0.3 convolution_add_fusion.8.refs_1_
  52.4 0.3 convolution_add_fusion.13.refs_0_
  52.6 1.0 %collective-permute-done.15.refs_2_ = f32[304,256]{1,0:T(8,128)S(1)} collective-permute-done((f32[304,256]{1,0:T(8,128)S(1)}, f32[304,256]{1,0:T(8,128)S(1)}, u32[]{:S(2)}, u32[]{:S(2)}) %collective-permute-start.15) | collective-permute-done | bytes 311328 | tf_op jit(solution)/shard_map/ppermute | solution.py:244
  53.6 1.0 %join_cores.1 = bf16[304,512]{1,0:T(8,128)(2,1)} custom-call(f32[304,256]{1,0:T(8,128)S(1)} %convolution_add_fusion.13.refs_0_, f32[304,256]{1,0:T(8,128)S(1)} %convolution_add_fusion.8.refs_1_, f32[304,256]{1,0:T(8,128)S(1)} %collective-permute-done.15.refs_2_, f32[304,256]{1,0:T(8,128)S(1)} %collective-permute-done.16.refs_3_), custom_call_target="tpu_custom_call" | custom-call | tf_op jit(solution)/shard_map/join_cores/pallas_call | solution.py:194
  (26 shorter events, 2.4 us)
Async XLA Ops:
  0.0 0.9 %copy-start = (bf16[6144,8]{0,1:T(8,128)(2,1)S(1)}, bf16[6144,8]{0,1:T(8,128)(2,1)}, u32[]{:S(2)}) copy-start(bf16[6144,8]{0,1:T(8,128)(2,1)} %param.6) | copy-start | bytes 294916
  0.9 0.7 %copy-start.1 = (s32[64,2]{0,1:T(2,128)S(1)}, s32[64,2]{0,1:T(2,128)}, u32[]{:S(2)}) copy-start(s32[64,2]{0,1:T(2,128)} %param.5) | copy-start | bytes 1540
  6.9 17.0 %collective-permute-start.8 = (bf16[256,384]{1,0:T(8,128)(2,1)S(1)}, bf16[256,384]{1,0:T(8,128)(2,1)S(1)}, u32[]{:S(2)}, u32[]{:S(2)}) collective-permute-start(bf16[256,384]{1,0:T(8,128)(2,1)S(1)} %half_transform.3), channel_id=1, source_target_pairs={{4,0},{5,1},{8,4},{9,5},{12,8},{13,9},{14,12},{15,13},{10,14},{11,... | collective-permute-start | bytes 589832 | tf_op jit(solution)/shard_map/ppermute | solution.py:236
  9.9 15.9 %collective-permute-start.7 = (bf16[256,384]{1,0:T(8,128)(2,1)S(1)}, bf16[256,384]{1,0:T(8,128)(2,1)S(1)}, u32[]{:S(2)}, u32[]{:S(2)}) collective-permute-start(bf16[256,384]{1,0:T(8,128)(2,1)S(1)} %half_transform.3), channel_id=1, source_target_pairs={{0,4},{1,5},{4,8},{5,9},{8,12},{9,13},{12,14},{13,15},{14,10},{15,... | collective-permute-start | bytes 589832 | tf_op jit(solution)/shard_map/ppermute | solution.py:235
  15.4 10.6 %collective-permute-start.1 = (bf16[256,384]{1,0:T(8,128)(2,1)S(1)}, bf16[256,384]{1,0:T(8,128)(2,1)S(1)}, u32[]{:S(2)}, u32[]{:S(2)}) collective-permute-start(bf16[256,384]{1,0:T(8,128)(2,1)S(1)} %half_transform.2), channel_id=1, source_target_pairs={{4,0},{5,1},{8,4},{9,5},{12,8},{13,9},{14,12},{15,13},{10,14},{11,... | collective-permute-start | bytes 589832 | tf_op jit(solution)/shard_map/ppermute | solution.py:236
  17.3 10.6 %collective-permute-start = (bf16[256,384]{1,0:T(8,128)(2,1)S(1)}, bf16[256,384]{1,0:T(8,128)(2,1)S(1)}, u32[]{:S(2)}, u32[]{:S(2)}) collective-permute-start(bf16[256,384]{1,0:T(8,128)(2,1)S(1)} %half_transform.2), channel_id=1, source_target_pairs={{0,4},{1,5},{4,8},{5,9},{8,12},{9,13},{12,14},{13,15},{14,10},{15,... | collective-permute-start | bytes 589832 | tf_op jit(solution)/shard_map/ppermute | solution.py:235
  23.3 23.8 %collective-permute-start.14 = (bf16[304,3072]{1,0:T(8,128)(2,1)S(1)}, bf16[304,3072]{1,0:T(8,128)(2,1)S(1)}, u32[]{:S(2)}, u32[]{:S(2)}) collective-permute-start(bf16[304,3072]{1,0:T(8,128)(2,1)S(1)} %get-tuple-element.8), channel_id=1, source_target_pairs={{0,1},{1,0},{2,3},{3,2},{4,5},{5,4},{6,7},{7,6},{8,9},{9,8},{10,11... | collective-permute-start | bytes 5603336 | tf_op jit(solution)/shard_map/ppermute | solution.py:217
  23.9 7.8 %collective-permute-start.10 = (bf16[256,384]{1,0:T(8,128)(2,1)S(1)}, bf16[256,384]{1,0:T(8,128)(2,1)S(1)}, u32[]{:S(2)}, u32[]{:S(2)}) collective-permute-start(bf16[256,384]{1,0:T(8,128)(2,1)S(1)} %collective-permute-done.8), channel_id=1, source_target_pairs={{4,0},{5,1},{8,4},{9,5},{12,8},{13,9},{14,12},{15,13},{10,14},{11,... | collective-permute-start | bytes 589832 | tf_op jit(solution)/shard_map/ppermute | solution.py:236
  25.8 8.0 %collective-permute-start.9 = (bf16[256,384]{1,0:T(8,128)(2,1)S(1)}, bf16[256,384]{1,0:T(8,128)(2,1)S(1)}, u32[]{:S(2)}, u32[]{:S(2)}) collective-permute-start(bf16[256,384]{1,0:T(8,128)(2,1)S(1)} %collective-permute-done.7), channel_id=1, source_target_pairs={{0,4},{1,5},{4,8},{5,9},{8,12},{9,13},{12,14},{13,15},{14,10},{15,... | collective-permute-start | bytes 589832 | tf_op jit(solution)/shard_map/ppermute | solution.py:235
  26.0 10.0 %collective-permute-start.3 = (bf16[256,384]{1,0:T(8,128)(2,1)S(1)}, bf16[256,384]{1,0:T(8,128)(2,1)S(1)}, u32[]{:S(2)}, u32[]{:S(2)}) collective-permute-start(bf16[256,384]{1,0:T(8,128)(2,1)S(1)} %collective-permute-done.1), channel_id=1, source_target_pairs={{4,0},{5,1},{8,4},{9,5},{12,8},{13,9},{14,12},{15,13},{10,14},{11,... | collective-permute-start | bytes 589832 | tf_op jit(solution)/shard_map/ppermute | solution.py:236
  27.9 9.9 %collective-permute-start.2 = (bf16[256,384]{1,0:T(8,128)(2,1)S(1)}, bf16[256,384]{1,0:T(8,128)(2,1)S(1)}, u32[]{:S(2)}, u32[]{:S(2)}) collective-permute-start(bf16[256,384]{1,0:T(8,128)(2,1)S(1)} %collective-permute-done), channel_id=1, source_target_pairs={{0,4},{1,5},{4,8},{5,9},{8,12},{9,13},{12,14},{13,15},{14,10},{15,... | collective-permute-start | bytes 589832 | tf_op jit(solution)/shard_map/ppermute | solution.py:235
  31.7 8.4 %collective-permute-start.12 = (bf16[256,384]{1,0:T(8,128)(2,1)S(1)}, bf16[256,384]{1,0:T(8,128)(2,1)S(1)}, u32[]{:S(2)}, u32[]{:S(2)}) collective-permute-start(bf16[256,384]{1,0:T(8,128)(2,1)S(1)} %collective-permute-done.10), channel_id=1, source_target_pairs={{4,0},{5,1},{8,4},{9,5},{12,8},{13,9},{14,12},{15,13},{10,14},{11,... | collective-permute-start | bytes 589832 | tf_op jit(solution)/shard_map/ppermute | solution.py:236
  33.8 12.9 %collective-permute-start.11 = (bf16[256,384]{1,0:T(8,128)(2,1)S(1)}, bf16[256,384]{1,0:T(8,128)(2,1)S(1)}, u32[]{:S(2)}, u32[]{:S(2)}) collective-permute-start(bf16[256,384]{1,0:T(8,128)(2,1)S(1)} %collective-permute-done.9), channel_id=1, source_target_pairs={{0,4},{1,5},{4,8},{5,9},{8,12},{9,13},{12,14},{13,15},{14,10},{15,... | collective-permute-start | bytes 589832 | tf_op jit(solution)/shard_map/ppermute | solution.py:235
  35.9 10.0 %collective-permute-start.5 = (bf16[256,384]{1,0:T(8,128)(2,1)S(1)}, bf16[256,384]{1,0:T(8,128)(2,1)S(1)}, u32[]{:S(2)}, u32[]{:S(2)}) collective-permute-start(bf16[256,384]{1,0:T(8,128)(2,1)S(1)} %collective-permute-done.3), channel_id=1, source_target_pairs={{4,0},{5,1},{8,4},{9,5},{12,8},{13,9},{14,12},{15,13},{10,14},{11,... | collective-permute-start | bytes 589832 | tf_op jit(solution)/shard_map/ppermute | solution.py:236
  37.8 7.7 %collective-permute-start.4 = (bf16[256,384]{1,0:T(8,128)(2,1)S(1)}, bf16[256,384]{1,0:T(8,128)(2,1)S(1)}, u32[]{:S(2)}, u32[]{:S(2)}) collective-permute-start(bf16[256,384]{1,0:T(8,128)(2,1)S(1)} %collective-permute-done.2), channel_id=1, source_target_pairs={{0,4},{1,5},{4,8},{5,9},{8,12},{9,13},{12,14},{13,15},{14,10},{15,... | collective-permute-start | bytes 589832 | tf_op jit(solution)/shard_map/ppermute | solution.py:235
  40.1 8.8 %collective-permute-start.13 = (bf16[256,384]{1,0:T(8,128)(2,1)S(1)}, bf16[256,384]{1,0:T(8,128)(2,1)S(1)}, u32[]{:S(2)}, u32[]{:S(2)}) collective-permute-start(bf16[256,384]{1,0:T(8,128)(2,1)S(1)} %collective-permute-done.12), channel_id=1, source_target_pairs={{4,0},{5,1},{8,4},{9,5},{12,8},{13,9},{14,12},{15,13},{10,14},{11,... | collective-permute-start | bytes 589832 | tf_op jit(solution)/shard_map/ppermute | solution.py:241
  45.5 6.2 %collective-permute-start.6 = (bf16[256,384]{1,0:T(8,128)(2,1)S(1)}, bf16[256,384]{1,0:T(8,128)(2,1)S(1)}, u32[]{:S(2)}, u32[]{:S(2)}) collective-permute-start(bf16[256,384]{1,0:T(8,128)(2,1)S(1)} %collective-permute-done.4), channel_id=1, source_target_pairs={{0,4},{1,5},{4,8},{5,9},{8,12},{9,13},{12,14},{13,15},{14,10},{15,... | collective-permute-start | bytes 589832 | tf_op jit(solution)/shard_map/ppermute | solution.py:241
  49.2 3.4 %collective-permute-start.16 = (f32[304,256]{1,0:T(8,128)S(1)}, f32[304,256]{1,0:T(8,128)S(1)}, u32[]{:S(2)}, u32[]{:S(2)}) collective-permute-start(f32[304,256]{1,0:T(8,128)S(1)} %convolution_add_fusion), channel_id=1, source_target_pairs={{0,1},{1,0},{2,3},{3,2},{4,5},{5,4},{6,7},{7,6},{8,9},{9,8},{10,11... | collective-permute-start | bytes 933896 | tf_op jit(solution)/shard_map/ppermute | solution.py:244
  52.0 1.7 %collective-permute-start.15 = (f32[304,256]{1,0:T(8,128)S(1)}, f32[304,256]{1,0:T(8,128)S(1)}, u32[]{:S(2)}, u32[]{:S(2)}) collective-permute-start(f32[304,256]{1,0:T(8,128)S(1)} %convolution_add_fusion.4), channel_id=1, source_target_pairs={{0,1},{1,0},{2,3},{3,2},{4,5},{5,4},{6,7},{7,6},{8,9},{9,8},{10,11... | collective-permute-start | bytes 933896 | tf_op jit(solution)/shard_map/ppermute | solution.py:244

commit v2 on v0

v2 whole, which is shorter than its diff:
```python
import functools

import jax
import jax.numpy as jnp
from jax import lax
from jax.experimental import pallas as pl
from jax.experimental.pallas import tpu as pltpu
from jax.sharding import PartitionSpec as P

NGROUP = 64
AO_GROUP = 96
LANES = 128
QB = 16
PAIR = 2
VMEM_LIMIT = 56 * 1024 * 1024


def occupied_rows(occ_ref, offset):
    start = pl.multiple_of((offset // LANES) * LANES, LANES)
    after = pl.multiple_of(jnp.minimum(start + LANES, occ_ref.shape[1] - LANES), LANES)
    shift = offset - start
    turn = lax.rem(LANES - shift, LANES)
    low = pltpu.roll(occ_ref[:, pl.ds(start, LANES)].astype(jnp.float32), turn, 1)
    high = pltpu.roll(occ_ref[:, pl.ds(after, LANES)].astype(jnp.float32), turn, 1)
    lane = lax.broadcasted_iota(jnp.int32, low.shape, 1)
    return jnp.where(lane < LANES - shift, low, high)


def half_kernel(me, pairs_hbm, occ_hbm, tiles_ref, out_ref, pairs, occ, held_tiles, kron, held, sems):
    count, ri_width = tiles_ref.shape[0], tiles_ref.shape[2]
    occ_batch = occ_hbm.shape[0]
    width = AO_GROUP * QB
    pairs_copy = pltpu.make_async_copy(pairs_hbm, pairs, sems.at[count])
    occ_copy = pltpu.make_async_copy(occ_hbm, occ, sems.at[count + 1])
    pairs_copy.start()
    occ_copy.start()
    copies = [
        pltpu.make_async_copy(tiles_ref.at[t, pl.ds(0, AO_GROUP)], held_tiles.at[t], sems.at[t]) for t in range(count)
    ]
    for copy in copies:
        copy.start()
    row = lax.broadcasted_iota(jnp.int32, (LANES, width), 0)
    lane = lax.broadcasted_iota(jnp.int32, (LANES, width), 1)
    spread = jnp.where(jnp.right_shift(lane, QB.bit_length() - 1) == row, 1.0, 0.0).astype(jnp.bfloat16)
    q_row = lax.broadcasted_iota(jnp.int32, (QB, width), 0)
    q_col = jnp.bitwise_and(lax.broadcasted_iota(jnp.int32, (QB, width), 1), QB - 1)
    diagonal = q_row == q_col
    pairs_copy.wait()
    occ_copy.wait()
    first = me[0] * count
    coef = [occupied_rows(occ, pairs[0, first + t] * AO_GROUP) for t in range(count)]
    coef = jnp.concatenate(coef, 0).astype(jnp.bfloat16)
    wide = jnp.dot(coef, spread, preferred_element_type=jnp.float32)
    for t in range(count):
        for i in range(occ_batch):
            rows = jnp.broadcast_to(wide[t * occ_batch + i : t * occ_batch + i + 1], (QB, width))
            kron[t, i * QB : (i + 1) * QB, :] = jnp.where(diagonal, rows, 0.0).astype(jnp.bfloat16)
    for t in range(count):
        copies[t].wait()
        for b in range(0, ri_width // QB, PAIR):
            parts = [held_tiles[t, :, (b + k) * QB : (b + k + 1) * QB, :].reshape(width, LANES) for k in range(PAIR)]
            half = jnp.dot(kron[t], jnp.concatenate(parts, 1), preferred_element_type=jnp.float32)
            for k in range(PAIR):
                part = half[:, k * LANES : (k + 1) * LANES].reshape(occ_batch, QB, LANES)
                held[t, :, (b + k) * QB : (b + k + 1) * QB, :] = part
    rows = occ_batch * ri_width
    lane = lax.broadcasted_iota(jnp.int32, (rows, LANES), 1)
    pieces = []
    for s in range(count):
        tile = jnp.int32(0)
        for j in range(1, count):
            tile = jnp.where(lax.rem(pairs[1, first + j], count) == s, j, tile)
        pieces.append(held[tile].reshape(rows, LANES))
    for out in range(count * AO_GROUP // LANES):
        value = None
        for s in range(count):
            begin, end = s * AO_GROUP - out * LANES, (s + 1) * AO_GROUP - out * LANES
            if end <= 0 or begin >= LANES:
                continue
            turned = pieces[s] if begin % LANES == 0 else pltpu.roll(pieces[s], begin % LANES, 1)
            value = turned if value is None else jnp.where(lane < begin, value, turned)
        out_ref[:, out * LANES : (out + 1) * LANES] = value.astype(out_ref.dtype)


def half_transform(me, pairs, occ, tiles):
    count, ri_width = tiles.shape[0], tiles.shape[2]
    occ_batch = occ.shape[0]
    width = AO_GROUP * QB
    rows, columns = occ_batch * ri_width, count * AO_GROUP
    return pl.pallas_call(
        half_kernel,
        in_specs=[pl.BlockSpec(memory_space=pltpu.SMEM)] + [pl.BlockSpec(memory_space=pl.ANY)] * 3,
        out_specs=pl.BlockSpec(memory_space=pltpu.VMEM),
        out_shape=jax.ShapeDtypeStruct((rows, columns), jnp.bfloat16),
        scratch_shapes=[
            pltpu.SMEM(pairs.shape, jnp.int32),
            pltpu.VMEM(occ.shape, jnp.bfloat16),
            pltpu.VMEM((count, AO_GROUP, ri_width, LANES), jnp.bfloat16),
            pltpu.VMEM((count, occ_batch * QB, width), jnp.bfloat16),
            pltpu.VMEM((count, occ_batch, ri_width, LANES), jnp.float32),
            pltpu.SemaphoreType.DMA((count + 2,)),
        ],
        compiler_params=pltpu.CompilerParams(vmem_limit_bytes=VMEM_LIMIT),
        cost_estimate=pl.CostEstimate(
            flops=2 * rows * columns * width, bytes_accessed=2 * tiles.size, transcendentals=0
        ),
        name="half_transform",
    )(me, pairs, occ, tiles)


def chip_at(place, chips):
    place = lax.rem(place + chips, chips)
    return jnp.where(place < chips // 2, 2 * place, 2 * (chips - 1 - place) + 1)


def place_of(chip, chips):
    return jnp.where(lax.rem(chip, 2) == 0, chip // 2, chips - 1 - chip // 2)


def take_windows(count, pairs, vir_ref, dev, write):
    columns = count * AO_GROUP
    panels = vir_ref.shape[1] // columns
    cols = [pairs[1, dev * count + j] for j in range(count)]
    first = cols[0]
    for col in cols:
        before = lax.rem(col + (NGROUP - 1), NGROUP)
        is_first = functools.reduce(jnp.logical_and, [other != before for other in cols])
        first = jnp.where(is_first, col, first)
    panel = first // count
    bound = lax.rem(first, count) * AO_GROUP
    low = pl.multiple_of(panel * columns, LANES)
    high = pl.multiple_of(lax.rem(panel + 1, panels) * columns, LANES)
    for j in range(columns // LANES):
        lane = lax.broadcasted_iota(jnp.int32, (vir_ref.shape[0], LANES), 1) + j * LANES
        here = vir_ref[:, pl.ds(pl.multiple_of(low + j * LANES, LANES), LANES)]
        there = vir_ref[:, pl.ds(pl.multiple_of(high + j * LANES, LANES), LANES)]
        write(j, jnp.where(lane >= bound, here, there))


def window_kernel(count, chips, me, pairs, own_ref, other_ref, both_ref, last_ref):
    chip, core = me[0] // 2, lax.rem(me[0], 2)
    place = place_of(chip, chips)
    behind = 2 * core - 1
    rows, columns = own_ref.shape[0], count * AO_GROUP
    for k in range(chips - 1):
        source = chip_at(place + behind * ((k + 1) // 2), chips)
        dev = 2 * source + (core if k == 0 or k % 2 == 1 else 1 - core)
        for half, vir_ref in enumerate((own_ref, other_ref)):

            def write(j, value, k=k, half=half):
                at = k * columns + j * LANES
                both_ref[half * rows : (half + 1) * rows, at : at + LANES] = value

            take_windows(count, pairs, vir_ref, dev, write)
    source = chip_at(place + chips // 2, chips)
    for k, dev in enumerate((2 * source + core, 2 * source + 1 - core)):

        def write(j, value, k=k):
            at = k * columns + j * LANES
            last_ref[:, at : at + LANES] = value

        take_windows(count, pairs, own_ref, dev, write)


def windows(me, pairs, vir, other_vir, count, chips):
    rows, columns = vir.shape[0], count * AO_GROUP
    smem, vmem = pl.BlockSpec(memory_space=pltpu.SMEM), pl.BlockSpec(memory_space=pltpu.VMEM)
    return pl.pallas_call(
        functools.partial(window_kernel, count, chips),
        in_specs=[smem, smem, vmem, vmem],
        out_specs=[vmem, vmem],
        out_shape=[
            jax.ShapeDtypeStruct((2 * rows, (chips - 1) * columns), vir.dtype),
            jax.ShapeDtypeStruct((rows, 2 * columns), vir.dtype),
        ],
        compiler_params=pltpu.CompilerParams(vmem_limit_bytes=VMEM_LIMIT),
        cost_estimate=pl.CostEstimate(flops=0, bytes_accessed=8 * vir.size, transcendentals=0),
        name="vir_windows",
    )(me, pairs, vir, other_vir)


def product(vir, block):
    return lax.dot_general(vir, block, (((1,), (1,)), ((), ())), preferred_element_type=jnp.float32)


def on_device(chips, tiles, pairs, occ_coef, vir_coef):
    count = tiles.shape[0]
    columns = count * AO_GROUP
    me = lax.axis_index("ao").astype(jnp.int32).reshape(1)
    pairs, occ, vir = pairs.T, occ_coef.T, vir_coef.T
    rows = vir.shape[0]

    ring = [2 * p if p < chips // 2 else 2 * (chips - 1 - p) + 1 for p in range(chips)]
    links = [(ring[p], ring[(p + 1) % chips]) for p in range(chips)]
    onward = [(2 * a, 2 * b) for a, b in links] + [(2 * b + 1, 2 * a + 1) for a, b in links]
    across = [(d, d ^ 1) for d in range(2 * chips)]

    own = half_transform(me, pairs, occ, tiles)
    both_w, last_w = windows(me, pairs, vir, lax.ppermute(vir, "ao", across), count, chips)
    travelling = [own, lax.ppermute(own, "ao", across)]
    sums = product(both_w[:, :columns], own)
    for hop in range(1, chips // 2):
        for which in range(2):
            travelling[which] = lax.ppermute(travelling[which], "ao", onward)
            k = 2 * hop - 1 + which
            sums = sums + product(both_w[:, k * columns : (k + 1) * columns], travelling[which])
    received = lax.ppermute(sums[rows:], "ao", across)
    last = lax.ppermute(travelling[0], "ao", onward)
    total = sums[:rows] + received + product(last_w[:, :columns], last)
    total = total + product(last_w[:, columns:], lax.ppermute(last, "ao", across))
    return total.astype(jnp.bfloat16)


def solution(mesh):
    return jax.shard_map(
        functools.partial(on_device, mesh.shape["ao"] // 2),
        mesh=mesh,
        in_specs=(P("ao", None, "groups", None), P(), P(), P(None, "ao")),
        out_specs=P("ao", "groups"),
        check_vma=False,
    )
```

time: 136 us -> 52.9 us (0.39)
  waiting for transfers between devices: 79.1 us -> 17.4 us
  blocking collectives: 16.2 us -> 0 us
  between operations: 13.5 us -> 0.13 us
  Pallas kernels: 0 us -> 11.4 us
  starting transfers between devices: 7.43 us -> 16.1 us
  matrix products: 14.9 us -> 7.3 us
  local copies, waits for them, and re-layouts: 4.7 us -> 0.42 us
    all_gather x1 -> x0, waiting for transfers between devices: 64.7 us -> none  [on_device(): lax.all_gather(x_own, 'ao', axis=0, tiled=True)]
    ppermute x0 -> x11, waiting for transfers between devices: none -> 17.4 us  [the longest x6 9.85 us: on_device(): travelling[which] = lax.ppermute(travelling[which], 'ao', onward)]
    all_to_all x1 -> x0, blocking collectives: 16.2 us -> none  [on_device(): lax.all_to_all(column_sum, 'ao', split_axis=0, concat_axis=1, tiled=True)]
    ppermute x0 -> x11, starting transfers between devices: none -> 16.1 us  [the longest x6 13.8 us: on_device(): travelling[which] = lax.ppermute(travelling[which], 'ao', onward)]
    all_to_all x1 -> x0, waiting for transfers between devices: 14.4 us -> none  [on_device(): lax.all_to_all(half_ints, 'ao', split_axis=2, concat_axis=0, tiled=True)]
    pallas_call x0 -> x2, Pallas kernels: none -> 11.4 us  [the longest x1 7.11 us: windows(): pl.pallas_call(functools.partial(window_kernel, count, chips), in_specs=[...]
    dot_general x3 -> x9, matrix products: 14.9 us -> 7.3 us  [product(): lax.dot_general(vir, block, (((1,), (1,)), ((), ())), preferred_element_t...]
    all_to_all x1 -> x0, starting transfers between devices: 7.39 us -> none  [on_device(): lax.all_to_all(half_ints, 'ao', split_axis=2, concat_axis=0, tiled=True)]
  transfers between devices with their start and end apart: 2 -> 11, of which waited for: 2 -> 6; matrix products, arithmetic and copies ran while one was open for 0% -> 11% of each run, Pallas kernels for 0% -> 22%
where the time goes in v2:
time: 52.9 us; the launch traced here: 52.7 us
  waiting for transfers between devices  17.4 us (33%)
  starting transfers between devices  16.1 us (30%)
  Pallas kernels  11.4 us (22%)
  matrix products  7.3 us (14%)
    ppermute x6, starting transfers between devices, on_device(): travelling[which] = lax.ppermute(travelling[which], 'ao', onward)  13.8 us
    ppermute x6, waiting for transfers between devices, on_device(): travelling[which] = lax.ppermute(travelling[which], 'ao', onward)  9.85 us
    dot_general x9, matrix products, product(): lax.dot_general(vir, block, (((1,), (1,)), ((), ())), preferred_element_t...  7.3 us
    pallas_call x1, Pallas kernels, windows(): pl.pallas_call(functools.partial(window_kernel, count, chips), in_specs=[...  7.11 us
    ppermute x1, waiting for transfers between devices, on_device(): last = lax.ppermute(travelling[0], 'ao', onward)  6.2 us
    pallas_call x1, Pallas kernels, half_transform(): pl.pallas_call(half_kernel, in_specs=[pl.BlockSpec(memory_space=pltpu.SME...  4.25 us
    ppermute x1, starting transfers between devices, on_device(): last = lax.ppermute(travelling[0], 'ao', onward)  1.62 us
    ppermute x1, waiting for transfers between devices, on_device(): lax.ppermute(last, 'ao', across)  1.35 us
  transfers between devices with their start and end apart: 11, of which 6 were waited for; matrix products, arithmetic and copies ran while one was open for 11% of the time, Pallas kernels for 22%

profile of v2, /device:TPU:0, one launch (start us, length us, event | category | flops | bytes accessed | tf_op | source)
XLA Modules:
  0.0 52.7 jit_solution(1711029138193461972)
XLA Ops:
  0.0 0.5 collective-permute-start
  0.5 4.2 %half_transform.1 = bf16[512,384]{1,0:T(8,128)(2,1)} custom-call(s32[1]{0:T(128)} %bitcast.me, s32[2,64]{1,0:T(2,128)} %bitcast.16, bf16[8,6144]{1,0:T(8,128)(2,1)} %bitcast.15, bf16[4,128,64,128]{3,2,1,0:T(8,128)(2,1)} %tiles_ref.1), custom_call_target="tpu_custom_call" | custom-call | flops 603979776 | bytes 8388608 | tf_op jit(solution)/shard_map/half_transform/pallas_call | solution.py:90
  4.7 0.1 collective-permute-start.2
  4.8 3.0 %collective-permute-start.1 = (bf16[512,384]{1,0:T(8,128)(2,1)}, bf16[512,384]{1,0:T(8,128)(2,1)S(1)}, u32[]{:S(2)}, u32[]{:S(2)}) collective-permute-start(bf16[512,384]{1,0:T(8,128)(2,1)} %half_transform.1), channel_id=1, source_target_pairs={{0,4},{4,8},{8,12},{12,14},{14,10},{10,6},{6,2},{2,0},{5,1},{9,5},... | collective-permute-start | bytes 1179656 | tf_op jit(solution)/shard_map/ppermute | solution.py:204
  7.9 0.0 collective-permute-done.2
  7.9 2.4 %collective-permute-start.3 = (bf16[512,384]{1,0:T(8,128)(2,1)S(1)}, bf16[512,384]{1,0:T(8,128)(2,1)S(1)}, u32[]{:S(2)}, u32[]{:S(2)}) collective-permute-start(bf16[512,384]{1,0:T(8,128)(2,1)S(1)} %collective-permute-done.2), channel_id=1, source_target_pairs={{0,4},{4,8},{8,12},{12,14},{14,10},{10,6},{6,2},{2,0},{5,1},{9,5},... | collective-permute-start | bytes 1179656 | tf_op jit(solution)/shard_map/ppermute | solution.py:204
  10.3 3.5 %collective-permute-done.1 = bf16[512,384]{1,0:T(8,128)(2,1)S(1)} collective-permute-done((bf16[512,384]{1,0:T(8,128)(2,1)}, bf16[512,384]{1,0:T(8,128)(2,1)S(1)}, u32[]{:S(2)}, u32[]{:S(2)}) %collective-permute-start.1) | collective-permute-done | bytes 393248 | tf_op jit(solution)/shard_map/ppermute | solution.py:204
  13.8 2.1 %collective-permute-start.4 = (bf16[512,384]{1,0:T(8,128)(2,1)S(1)}, bf16[512,384]{1,0:T(8,128)(2,1)S(1)}, u32[]{:S(2)}, u32[]{:S(2)}) collective-permute-start(bf16[512,384]{1,0:T(8,128)(2,1)S(1)} %collective-permute-done.1), channel_id=1, source_target_pairs={{0,4},{4,8},{8,12},{12,14},{14,10},{10,6},{6,2},{2,0},{5,1},{9,5},... | collective-permute-start | bytes 1179656 | tf_op jit(solution)/shard_map/ppermute | solution.py:204
  15.8 2.1 %collective-permute-done.3 = bf16[512,384]{1,0:T(8,128)(2,1)S(1)} collective-permute-done((bf16[512,384]{1,0:T(8,128)(2,1)S(1)}, bf16[512,384]{1,0:T(8,128)(2,1)S(1)}, u32[]{:S(2)}, u32[]{:S(2)}) %collective-permute-start.3) | collective-permute-done | bytes 393248 | tf_op jit(solution)/shard_map/ppermute | solution.py:204
  18.0 2.1 %collective-permute-start.5 = (bf16[512,384]{1,0:T(8,128)(2,1)S(1)}, bf16[512,384]{1,0:T(8,128)(2,1)S(1)}, u32[]{:S(2)}, u32[]{:S(2)}) collective-permute-start(bf16[512,384]{1,0:T(8,128)(2,1)S(1)} %collective-permute-done.3), channel_id=1, source_target_pairs={{0,4},{4,8},{8,12},{12,14},{14,10},{10,6},{6,2},{2,0},{5,1},{9,5},... | collective-permute-start | bytes 1179656 | tf_op jit(solution)/shard_map/ppermute | solution.py:204
  20.1 2.1 %collective-permute-done.4 = bf16[512,384]{1,0:T(8,128)(2,1)S(1)} collective-permute-done((bf16[512,384]{1,0:T(8,128)(2,1)S(1)}, bf16[512,384]{1,0:T(8,128)(2,1)S(1)}, u32[]{:S(2)}, u32[]{:S(2)}) %collective-permute-start.4) | collective-permute-done | bytes 393248 | tf_op jit(solution)/shard_map/ppermute | solution.py:204
  22.2 2.1 %collective-permute-start.6 = (bf16[512,384]{1,0:T(8,128)(2,1)S(1)}, bf16[512,384]{1,0:T(8,128)(2,1)S(1)}, u32[]{:S(2)}, u32[]{:S(2)}) collective-permute-start(bf16[512,384]{1,0:T(8,128)(2,1)S(1)} %collective-permute-done.4), channel_id=1, source_target_pairs={{0,4},{4,8},{8,12},{12,14},{14,10},{10,6},{6,2},{2,0},{5,1},{9,5},... | collective-permute-start | bytes 1179656 | tf_op jit(solution)/shard_map/ppermute | solution.py:204
  24.3 2.1 %collective-permute-done.5 = bf16[512,384]{1,0:T(8,128)(2,1)S(1)} collective-permute-done((bf16[512,384]{1,0:T(8,128)(2,1)S(1)}, bf16[512,384]{1,0:T(8,128)(2,1)S(1)}, u32[]{:S(2)}, u32[]{:S(2)}) %collective-permute-start.5) | collective-permute-done | bytes 393248 | tf_op jit(solution)/shard_map/ppermute | solution.py:204
  26.4 2.1 %collective-permute-start.7 = (bf16[512,384]{1,0:T(8,128)(2,1)S(1)}, bf16[512,384]{1,0:T(8,128)(2,1)S(1)}, u32[]{:S(2)}, u32[]{:S(2)}) collective-permute-start(bf16[512,384]{1,0:T(8,128)(2,1)S(1)} %collective-permute-done.5), channel_id=1, source_target_pairs={{0,4},{4,8},{8,12},{12,14},{14,10},{10,6},{6,2},{2,0},{5,1},{9,5},... | collective-permute-start | bytes 1179656 | tf_op jit(solution)/shard_map/ppermute | solution.py:204
  28.5 0.0 collective-permute-done.other_ref
  28.5 7.1 %vir_windows.1 = (bf16[608,2688]{1,0:T(8,128)(2,1)}, bf16[304,768]{1,0:T(8,128)(2,1)}) custom-call(s32[1]{0:T(128)} %bitcast.me, s32[2,64]{1,0:T(2,128)} %bitcast.17, bf16[304,6144]{1,0:T(8,128)(2,1)} %bitcast.14, bf16[304,6144]{1,0:T(8,128)(2,1)} %collective-permute-done.other_ref), custom_call_target="tpu_custom_call" | custom-call | bytes 14942208 | tf_op jit(solution)/shard_map/vir_windows/pallas_call | solution.py:168
  35.6 0.0 copy-start.1
  35.6 1.6 %fusion.10 = f32[608,512]{1,0:T(8,128)S(1)} fusion(bf16[512,384]{1,0:T(8,128)(2,1)S(1)} %collective-permute-done.1, bf16[608,2688]{1,0:T(8,128)(2,1)} %get-tuple-element.7), kind=kOutput, calls=%fused_computation.17 | convolution fusion | flops 239075328 | bytes 2105344 | tf_op jit(solution)/shard_map/dot_general | solution.py:183
  37.2 0.0 copy-done.1
  37.2 0.0 copy-start
  37.2 1.7 %convolution_add_fusion.3 = f32[608,512]{1,0:T(8,128)S(1)} fusion(f32[608,512]{1,0:T(8,128)S(1)} %fusion.10, bf16[512,384]{1,0:T(8,128)(2,1)S(1)} %copy-done.1, bf16[608,2688]{1,0:T(8,128)(2,1)} %get-tuple-element.7), kind=kOutput, calls=%fused_computation.3 | convolution fusion | flops 239386624 | bytes 3350528 | tf_op jit(solution)/shard_map/dot_general | solution.py:183
  38.9 0.4 copy-done
  39.3 0.5 fusion.7
  39.8 0.5 fusion
  40.3 0.0 collective-permute-done.6
  40.3 0.5 fusion.4
  40.8 0.5 fusion.1
  41.4 0.0 collective-permute-done.7
  41.4 0.5 convolution_add_fusion
  41.9 0.0 copy-start.2
  42.0 0.1 collective-permute-start.8
  42.0 1.6 %collective-permute-start.9 = (bf16[512,384]{1,0:T(8,128)(2,1)S(1)}, bf16[512,384]{1,0:T(8,128)(2,1)S(1)}, u32[]{:S(2)}, u32[]{:S(2)}) collective-permute-start(bf16[512,384]{1,0:T(8,128)(2,1)S(1)} %collective-permute-done.6), channel_id=1, source_target_pairs={{0,4},{4,8},{8,12},{12,14},{14,10},{10,6},{6,2},{2,0},{5,1},{9,5},... | collective-permute-start | bytes 1179656 | tf_op jit(solution)/shard_map/ppermute | solution.py:208
  43.7 6.2 %collective-permute-done.9 = bf16[512,384]{1,0:T(8,128)(2,1)S(1)} collective-permute-done((bf16[512,384]{1,0:T(8,128)(2,1)S(1)}, bf16[512,384]{1,0:T(8,128)(2,1)S(1)}, u32[]{:S(2)}, u32[]{:S(2)}) %collective-permute-start.9) | collective-permute-done | bytes 393248 | tf_op jit(solution)/shard_map/ppermute | solution.py:208
  49.9 0.0 collective-permute-start.10
  49.9 0.0 collective-permute-done.8
  49.9 0.0 copy-done.2
  49.9 0.4 convolution_add_fusion.5
  50.3 1.3 %collective-permute-done.10 = bf16[512,384]{1,0:T(8,128)(2,1)S(1)} collective-permute-done((bf16[512,384]{1,0:T(8,128)(2,1)S(1)}, bf16[512,384]{1,0:T(8,128)(2,1)S(1)}, u32[]{:S(2)}, u32[]{:S(2)}) %collective-permute-start.10) | collective-permute-done | bytes 393248 | tf_op jit(solution)/shard_map/ppermute | solution.py:210
  51.6 1.1 %fusion.2 = bf16[304,512]{1,0:T(8,128)(2,1)} fusion(f32[304,512]{1,0:T(8,128)S(1)} %convolution_add_fusion.5, bf16[512,384]{1,0:T(8,128)(2,1)S(1)} %collective-permute-done.10, bf16[304,768]{1,0:T(8,128)(2,1)S(1)} %copy-done.2), kind=kOutput, calls=%fused_computation.8 | convolution fusion | flops 119848960 | bytes 1560576 | tf_op jit(solution)/shard_map/dot_general | solution.py:183
  (1 shorter events, 0.0 us)
Async XLA Ops:
  0.0 28.5 %collective-permute-start = (bf16[304,6144]{1,0:T(8,128)(2,1)}, bf16[304,6144]{1,0:T(8,128)(2,1)}, u32[]{:S(2)}, u32[]{:S(2)}) collective-permute-start(bf16[304,6144]{1,0:T(8,128)(2,1)} %bitcast.13), channel_id=1, source_target_pairs={{0,1},{1,0},{2,3},{3,2},{4,5},{5,4},{6,7},{7,6},{8,9},{9,8},{10,11... | collective-permute-start | bytes 11206664 | tf_op jit(solution)/shard_map/ppermute | solution.py:199
  4.7 3.1 %collective-permute-start.2 = (bf16[512,384]{1,0:T(8,128)(2,1)}, bf16[512,384]{1,0:T(8,128)(2,1)S(1)}, u32[]{:S(2)}, u32[]{:S(2)}) collective-permute-start(bf16[512,384]{1,0:T(8,128)(2,1)} %half_transform.1), channel_id=1, source_target_pairs={{0,1},{1,0},{2,3},{3,2},{4,5},{5,4},{6,7},{7,6},{8,9},{9,8},{10,11... | collective-permute-start | bytes 1179656 | tf_op jit(solution)/shard_map/ppermute | solution.py:200
  4.8 8.9 %collective-permute-start.1 = (bf16[512,384]{1,0:T(8,128)(2,1)}, bf16[512,384]{1,0:T(8,128)(2,1)S(1)}, u32[]{:S(2)}, u32[]{:S(2)}) collective-permute-start(bf16[512,384]{1,0:T(8,128)(2,1)} %half_transform.1), channel_id=1, source_target_pairs={{0,4},{4,8},{8,12},{12,14},{14,10},{10,6},{6,2},{2,0},{5,1},{9,5},... | collective-permute-start | bytes 1179656 | tf_op jit(solution)/shard_map/ppermute | solution.py:204
  7.9 10.1 %collective-permute-start.3 = (bf16[512,384]{1,0:T(8,128)(2,1)S(1)}, bf16[512,384]{1,0:T(8,128)(2,1)S(1)}, u32[]{:S(2)}, u32[]{:S(2)}) collective-permute-start(bf16[512,384]{1,0:T(8,128)(2,1)S(1)} %collective-permute-done.2), channel_id=1, source_target_pairs={{0,4},{4,8},{8,12},{12,14},{14,10},{10,6},{6,2},{2,0},{5,1},{9,5},... | collective-permute-start | bytes 1179656 | tf_op jit(solution)/shard_map/ppermute | solution.py:204
  13.8 8.4 %collective-permute-start.4 = (bf16[512,384]{1,0:T(8,128)(2,1)S(1)}, bf16[512,384]{1,0:T(8,128)(2,1)S(1)}, u32[]{:S(2)}, u32[]{:S(2)}) collective-permute-start(bf16[512,384]{1,0:T(8,128)(2,1)S(1)} %collective-permute-done.1), channel_id=1, source_target_pairs={{0,4},{4,8},{8,12},{12,14},{14,10},{10,6},{6,2},{2,0},{5,1},{9,5},... | collective-permute-start | bytes 1179656 | tf_op jit(solution)/shard_map/ppermute | solution.py:204
  18.0 8.4 %collective-permute-start.5 = (bf16[512,384]{1,0:T(8,128)(2,1)S(1)}, bf16[512,384]{1,0:T(8,128)(2,1)S(1)}, u32[]{:S(2)}, u32[]{:S(2)}) collective-permute-start(bf16[512,384]{1,0:T(8,128)(2,1)S(1)} %collective-permute-done.3), channel_id=1, source_target_pairs={{0,4},{4,8},{8,12},{12,14},{14,10},{10,6},{6,2},{2,0},{5,1},{9,5},... | collective-permute-start | bytes 1179656 | tf_op jit(solution)/shard_map/ppermute | solution.py:204
  22.2 18.1 %collective-permute-start.6 = (bf16[512,384]{1,0:T(8,128)(2,1)S(1)}, bf16[512,384]{1,0:T(8,128)(2,1)S(1)}, u32[]{:S(2)}, u32[]{:S(2)}) collective-permute-start(bf16[512,384]{1,0:T(8,128)(2,1)S(1)} %collective-permute-done.4), channel_id=1, source_target_pairs={{0,4},{4,8},{8,12},{12,14},{14,10},{10,6},{6,2},{2,0},{5,1},{9,5},... | collective-permute-start | bytes 1179656 | tf_op jit(solution)/shard_map/ppermute | solution.py:204
  26.4 15.0 %collective-permute-start.7 = (bf16[512,384]{1,0:T(8,128)(2,1)S(1)}, bf16[512,384]{1,0:T(8,128)(2,1)S(1)}, u32[]{:S(2)}, u32[]{:S(2)}) collective-permute-start(bf16[512,384]{1,0:T(8,128)(2,1)S(1)} %collective-permute-done.5), channel_id=1, source_target_pairs={{0,4},{4,8},{8,12},{12,14},{14,10},{10,6},{6,2},{2,0},{5,1},{9,5},... | collective-permute-start | bytes 1179656 | tf_op jit(solution)/shard_map/ppermute | solution.py:204
  35.6 1.6 %copy-start.1 = (bf16[512,384]{1,0:T(8,128)(2,1)S(1)}, bf16[512,384]{1,0:T(8,128)(2,1)}, u32[]{:S(2)}) copy-start(bf16[512,384]{1,0:T(8,128)(2,1)} %half_transform.1) | copy-start | bytes 1179652
  37.2 2.1 %copy-start = (bf16[608,2688]{1,0:T(8,128)(2,1)S(1)}, bf16[608,2688]{1,0:T(8,128)(2,1)}, u32[]{:S(2)}) copy-start(bf16[608,2688]{1,0:T(8,128)(2,1)} %get-tuple-element.7) | copy-start | bytes 9805828
  41.9 8.0 %copy-start.2 = (bf16[304,768]{1,0:T(8,128)(2,1)S(1)}, bf16[304,768]{1,0:T(8,128)(2,1)}, u32[]{:S(2)}) copy-start(bf16[304,768]{1,0:T(8,128)(2,1)} %get-tuple-element.8) | copy-start | bytes 1400836
  42.0 7.9 %collective-permute-start.8 = (f32[304,512]{1,0:T(8,128)S(1)}, f32[304,512]{1,0:T(8,128)S(1)}, u32[]{:S(2)}, u32[]{:S(2)}) collective-permute-start(f32[304,512]{1,0:T(8,128)S(1)} %slice.45), channel_id=1, source_target_pairs={{0,1},{1,0},{2,3},{3,2},{4,5},{5,4},{6,7},{7,6},{8,9},{9,8},{10,11... | collective-permute-start | bytes 1867784 | tf_op jit(solution)/shard_map/ppermute | solution.py:207
  42.0 7.8 %collective-permute-start.9 = (bf16[512,384]{1,0:T(8,128)(2,1)S(1)}, bf16[512,384]{1,0:T(8,128)(2,1)S(1)}, u32[]{:S(2)}, u32[]{:S(2)}) collective-permute-start(bf16[512,384]{1,0:T(8,128)(2,1)S(1)} %collective-permute-done.6), channel_id=1, source_target_pairs={{0,4},{4,8},{8,12},{12,14},{14,10},{10,6},{6,2},{2,0},{5,1},{9,5},... | collective-permute-start | bytes 1179656 | tf_op jit(solution)/shard_map/ppermute | solution.py:208
  49.9 1.7 %collective-permute-start.10 = (bf16[512,384]{1,0:T(8,128)(2,1)S(1)}, bf16[512,384]{1,0:T(8,128)(2,1)S(1)}, u32[]{:S(2)}, u32[]{:S(2)}) collective-permute-start(bf16[512,384]{1,0:T(8,128)(2,1)S(1)} %collective-permute-done.9), channel_id=1, source_target_pairs={{0,1},{1,0},{2,3},{3,2},{4,5},{5,4},{6,7},{7,6},{8,9},{9,8},{10,11... | collective-permute-start | bytes 1179656 | tf_op jit(solution)/shard_map/ppermute | solution.py:210

commit v3 on v2

--- a/solution.py
+++ b/solution.py
@@ -12,7 +12,8 @@
 LANES = 128
 QB = 16
 PAIR = 2
-VMEM_LIMIT = 56 * 1024 * 1024
+HALF_VMEM = 56 * 1024 * 1024
+WINDOW_VMEM = 24 * 1024 * 1024
 
 
 def occupied_rows(occ_ref, offset):
@@ -100,7 +101,7 @@
             pltpu.VMEM((count, occ_batch, ri_width, LANES), jnp.float32),
             pltpu.SemaphoreType.DMA((count + 2,)),
         ],
-        compiler_params=pltpu.CompilerParams(vmem_limit_bytes=VMEM_LIMIT),
+        compiler_params=pltpu.CompilerParams(vmem_limit_bytes=HALF_VMEM),
         cost_estimate=pl.CostEstimate(
             flops=2 * rows * columns * width, bytes_accessed=2 * tiles.size, transcendentals=0
         ),
@@ -131,10 +132,12 @@
     low = pl.multiple_of(panel * columns, LANES)
     high = pl.multiple_of(lax.rem(panel + 1, panels) * columns, LANES)
     for j in range(columns // LANES):
-        lane = lax.broadcasted_iota(jnp.int32, (vir_ref.shape[0], LANES), 1) + j * LANES
+        lane = lax.broadcasted_iota(jnp.int32, (QB, LANES), 1) + j * LANES
+        keep = jnp.where(lane >= bound, 1.0, 0.0)
         here = vir_ref[:, pl.ds(pl.multiple_of(low + j * LANES, LANES), LANES)]
         there = vir_ref[:, pl.ds(pl.multiple_of(high + j * LANES, LANES), LANES)]
-        write(j, jnp.where(lane >= bound, here, there))
+        keep, drop = keep[:1].astype(jnp.bfloat16), (1.0 - keep[:1]).astype(jnp.bfloat16)
+        write(j, here * keep + there * drop)
 
 
 def window_kernel(count, chips, me, pairs, own_ref, other_ref, both_ref, last_ref):
@@ -173,7 +176,7 @@
             jax.ShapeDtypeStruct((2 * rows, (chips - 1) * columns), vir.dtype),
             jax.ShapeDtypeStruct((rows, 2 * columns), vir.dtype),
         ],
-        compiler_params=pltpu.CompilerParams(vmem_limit_bytes=VMEM_LIMIT),
+        compiler_params=pltpu.CompilerParams(vmem_limit_bytes=WINDOW_VMEM),
         cost_estimate=pl.CostEstimate(flops=0, bytes_accessed=8 * vir.size, transcendentals=0),
         name="vir_windows",
     )(me, pairs, vir, other_vir)
@@ -197,15 +200,36 @@
 
     own = half_transform(me, pairs, occ, tiles)
     both_w, last_w = windows(me, pairs, vir, lax.ppermute(vir, "ao", across), count, chips)
-    travelling = [own, lax.ppermute(own, "ao", across)]
-    sums = product(both_w[:, :columns], own)
-    for hop in range(1, chips // 2):
-        for which in range(2):
-            travelling[which] = lax.ppermute(travelling[which], "ao", onward)
-            k = 2 * hop - 1 + which
-            sums = sums + product(both_w[:, k * columns : (k + 1) * columns], travelling[which])
+    blocks = [own]
+    sums, summed = None, 0
+
+    def add_to(sums, k):
+        term = product(both_w[:, k * columns : (k + 1) * columns], blocks[k])
+        return term if sums is None else sums + term
+
+    for message in range(1, chips):
+        if message == 1:
+            block = own
+        elif message == 2:
+            block = lax.ppermute(own, "ao", across)
+        else:
+            block = blocks[message - 2]
+        if message == 3:
+            block, both_w, last_w = lax.optimization_barrier((block, both_w, last_w))
+        elif message > 3:
+            while summed < message - 2:
+                sums = add_to(sums, summed)
+                summed += 1
+            block, sums = lax.optimization_barrier((block, sums))
+        block = lax.ppermute(block, "ao", onward)
+        if message < chips - 1:
+            blocks.append(block)
+        else:
+            last = block
+    while summed < len(blocks):
+        sums = add_to(sums, summed)
+        summed += 1
     received = lax.ppermute(sums[rows:], "ao", across)
-    last = lax.ppermute(travelling[0], "ao", onward)
     total = sums[:rows] + received + product(last_w[:, :columns], last)
     total = total + product(last_w[:, columns:], lax.ppermute(last, "ao", across))
     return total.astype(jnp.bfloat16)

time: 52.9 us -> 42.2 us (0.80)
  waiting for transfers between devices: 17.4 us -> 11.7 us
  Pallas kernels: 11.4 us -> 8.62 us
  matrix products: 7.3 us -> 5.06 us
  other arithmetic: 0 us -> 0.78 us
    ppermute x8, waiting for transfers between devices: 16.1 us -> 10.4 us  [the longest x7 10.4 us: on_device(): block = lax.ppermute(block, 'ao', onward)]
    pallas_call x1, Pallas kernels: 7.11 us -> 4.24 us  [windows(): pl.pallas_call(functools.partial(window_kernel, count, chips), in_specs=[...]
    dot_general x9, matrix products: 7.3 us -> 5.06 us  [product(): lax.dot_general(vir, block, (((1,), (1,)), ((), ())), preferred_element_t...]
    add x0 -> x3, other arithmetic: none -> 0.78 us  [add_to(): return term if sums is None else sums + term]
  transfers between devices with their start and end apart: 11 -> 11, of which waited for: 6 -> 7; matrix products, arithmetic and copies ran while one was open for 11% -> 11% of each run, Pallas kernels for 22% -> 20%
where the time goes in v3:
time: 42.2 us; the launch traced here: 42.1 us
  starting transfers between devices  15.7 us (37%)
  waiting for transfers between devices  11.7 us (28%)
  Pallas kernels  8.62 us (20%)
  matrix products  5.06 us (12%)
  other arithmetic  0.78 us (2%)
    ppermute x7, starting transfers between devices, on_device(): block = lax.ppermute(block, 'ao', onward)  15 us
    ppermute x7, waiting for transfers between devices, on_device(): block = lax.ppermute(block, 'ao', onward)  10.4 us
    dot_general x9, matrix products, product(): lax.dot_general(vir, block, (((1,), (1,)), ((), ())), preferred_element_t...  5.06 us
    pallas_call x1, Pallas kernels, half_transform(): pl.pallas_call(half_kernel, in_specs=[pl.BlockSpec(memory_space=pltpu.SME...  4.39 us
    pallas_call x1, Pallas kernels, windows(): pl.pallas_call(functools.partial(window_kernel, count, chips), in_specs=[...  4.24 us
    ppermute x1, waiting for transfers between devices, on_device(): lax.ppermute(last, 'ao', across)  1.35 us
  transfers between devices with their start and end apart: 11, of which 7 were waited for; matrix products, arithmetic and copies ran while one was open for 11% of the time, Pallas kernels for 20%

profile of v3, /device:TPU:0, one launch (start us, length us, event | category | flops | bytes accessed | tf_op | source)
XLA Modules:
  0.0 42.1 jit_solution(7652242695239189623)
XLA Ops:
  0.0 0.5 %collective-permute-start.1 = (bf16[304,6144]{1,0:T(8,128)(2,1)}, bf16[304,6144]{1,0:T(8,128)(2,1)}, u32[]{:S(2)}, u32[]{:S(2)}) collective-permute-start(bf16[304,6144]{1,0:T(8,128)(2,1)} %bitcast.13), channel_id=1, source_target_pairs={{0,1},{1,0},{2,3},{3,2},{4,5},{5,4},{6,7},{7,6},{8,9},{9,8},{10,11... | collective-permute-start | bytes 11206664 | tf_op jit(solution)/shard_map/ppermute | solution.py:202
  0.5 0.0 copy-start
  0.5 0.0 copy-start.1
  0.5 4.4 %half_transform.1 = bf16[512,384]{1,0:T(8,128)(2,1)} custom-call(s32[1]{0:T(128)} %bitcast.me, s32[2,64]{1,0:T(2,128)} %bitcast.15, bf16[8,6144]{1,0:T(8,128)(2,1)} %bitcast.17, bf16[4,128,64,128]{3,2,1,0:T(8,128)(2,1)} %tiles_ref.1), custom_call_target="tpu_custom_call" | custom-call | flops 603979776 | bytes 8388608 | tf_op jit(solution)/shard_map/half_transform/pallas_call | solution.py:91
  4.9 0.1 collective-permute-start.3
  5.0 3.0 %collective-permute-start = (bf16[512,384]{1,0:T(8,128)(2,1)}, bf16[512,384]{1,0:T(8,128)(2,1)S(1)}, u32[]{:S(2)}, u32[]{:S(2)}) collective-permute-start(bf16[512,384]{1,0:T(8,128)(2,1)} %half_transform.1), channel_id=1, source_target_pairs={{0,4},{4,8},{8,12},{12,14},{14,10},{10,6},{6,2},{2,0},{5,1},{9,5},... | collective-permute-start | bytes 1179656 | tf_op jit(solution)/shard_map/ppermute | solution.py:224
  8.0 0.0 collective-permute-done.3
  8.0 2.3 %collective-permute-start.4 = (bf16[512,384]{1,0:T(8,128)(2,1)S(1)}, bf16[512,384]{1,0:T(8,128)(2,1)S(1)}, u32[]{:S(2)}, u32[]{:S(2)}) collective-permute-start(bf16[512,384]{1,0:T(8,128)(2,1)S(1)} %collective-permute-done.3), channel_id=1, source_target_pairs={{0,4},{4,8},{8,12},{12,14},{14,10},{10,6},{6,2},{2,0},{5,1},{9,5},... | collective-permute-start | bytes 1179656 | tf_op jit(solution)/shard_map/ppermute | solution.py:224
  10.3 0.0 collective-permute-done.1.other_ref
  10.3 0.0 copy-done
  10.3 0.0 copy-done.1
  10.3 4.2 %vir_windows.1 = (bf16[608,2688]{1,0:T(8,128)(2,1)S(1)}, bf16[304,768]{1,0:T(8,128)(2,1)S(1)}) custom-call(s32[1]{0:T(128)} %bitcast.me, s32[2,64]{1,0:T(2,128)S(1)} %bitcast.16, bf16[304,6144]{1,0:T(8,128)(2,1)S(1)} %bitcast.14, bf16[304,6144]{1,0:T(8,128)(2,1)} %collective-permute-done.1.other_ref), custom_call_target="tpu_custom_call" | custom-call | bytes 14942208 | tf_op jit(solution)/shard_map/vir_windows/pallas_call | solution.py:171
  14.6 0.0 copy-start.2
  14.6 0.0 collective-permute-done
  14.6 1.6 %collective-permute-start.2 = (bf16[512,384]{1,0:T(8,128)(2,1)S(1)}, bf16[512,384]{1,0:T(8,128)(2,1)S(1)}, u32[]{:S(2)}, u32[]{:S(2)}) collective-permute-start(bf16[512,384]{1,0:T(8,128)(2,1)S(1)} %collective-permute-done), channel_id=1, source_target_pairs={{0,4},{4,8},{8,12},{12,14},{14,10},{10,6},{6,2},{2,0},{5,1},{9,5},... | collective-permute-start | bytes 1179656 | tf_op jit(solution)/shard_map/ppermute | solution.py:224
  16.2 0.5 %fusion.14 = f32[608,512]{1,0:T(8,128)S(1)} fusion(bf16[512,384]{1,0:T(8,128)(2,1)S(1)} %collective-permute-done, bf16[608,2688]{1,0:T(8,128)(2,1)S(1)} %get-tuple-element.21), kind=kOutput, calls=%fused_computation.16 | convolution fusion | flops 239075328 | bytes 2105344 | tf_op jit(solution)/shard_map/dot_general | solution.py:186
  16.7 0.0 copy-done.2
  16.7 0.5 %convolution_add_fusion = f32[608,512]{1,0:T(8,128)S(1)} fusion(f32[608,512]{1,0:T(8,128)S(1)} %fusion.14, bf16[512,384]{1,0:T(8,128)(2,1)S(1)} %copy-done.2, bf16[608,2688]{1,0:T(8,128)(2,1)S(1)} %get-tuple-element.21), kind=kOutput, calls=%fused_computation | convolution fusion | flops 239386624 | bytes 3350528 | tf_op jit(solution)/shard_map/dot_general | solution.py:186
  17.3 0.9 %collective-permute-done.4 = bf16[512,384]{1,0:T(8,128)(2,1)S(1)} collective-permute-done((bf16[512,384]{1,0:T(8,128)(2,1)S(1)}, bf16[512,384]{1,0:T(8,128)(2,1)S(1)}, u32[]{:S(2)}, u32[]{:S(2)}) %collective-permute-start.4) | collective-permute-done | bytes 393248 | tf_op jit(solution)/shard_map/ppermute | solution.py:224
  18.1 2.1 %collective-permute-start.6 = (bf16[512,384]{1,0:T(8,128)(2,1)S(1)}, bf16[512,384]{1,0:T(8,128)(2,1)S(1)}, u32[]{:S(2)}, u32[]{:S(2)}) collective-permute-start(bf16[512,384]{1,0:T(8,128)(2,1)S(1)} %collective-permute-done.4), channel_id=1, source_target_pairs={{0,4},{4,8},{8,12},{12,14},{14,10},{10,6},{6,2},{2,0},{5,1},{9,5},... | collective-permute-start | bytes 1179656 | tf_op jit(solution)/shard_map/ppermute | solution.py:224
  20.2 0.5 %fusion.12 = f32[608,512]{1,0:T(8,128)S(1)} fusion(bf16[512,384]{1,0:T(8,128)(2,1)S(1)} %collective-permute-done.4, bf16[608,2688]{1,0:T(8,128)(2,1)S(1)} %get-tuple-element.21), kind=kOutput, calls=%fused_computation.14 | convolution fusion | flops 239075328 | bytes 2105344 | tf_op jit(solution)/shard_map/dot_general | solution.py:186
  20.7 0.3 add.28
  21.0 1.4 %collective-permute-done.2 = bf16[512,384]{1,0:T(8,128)(2,1)S(1)} collective-permute-done((bf16[512,384]{1,0:T(8,128)(2,1)S(1)}, bf16[512,384]{1,0:T(8,128)(2,1)S(1)}, u32[]{:S(2)}, u32[]{:S(2)}) %collective-permute-start.2) | collective-permute-done | bytes 393248 | tf_op jit(solution)/shard_map/ppermute | solution.py:224
  22.4 2.0 %collective-permute-start.5 = (bf16[512,384]{1,0:T(8,128)(2,1)S(1)}, bf16[512,384]{1,0:T(8,128)(2,1)S(1)}, u32[]{:S(2)}, u32[]{:S(2)}) collective-permute-start(bf16[512,384]{1,0:T(8,128)(2,1)S(1)} %collective-permute-done.2), channel_id=1, source_target_pairs={{0,4},{4,8},{8,12},{12,14},{14,10},{10,6},{6,2},{2,0},{5,1},{9,5},... | collective-permute-start | bytes 1179656 | tf_op jit(solution)/shard_map/ppermute | solution.py:224
  24.4 0.5 %fusion.10 = f32[608,512]{1,0:T(8,128)S(1)} fusion(bf16[512,384]{1,0:T(8,128)(2,1)S(1)} %collective-permute-done.2, bf16[608,2688]{1,0:T(8,128)(2,1)S(1)} %get-tuple-element.21), kind=kOutput, calls=%fused_computation.12 | convolution fusion | flops 239075328 | bytes 2105344 | tf_op jit(solution)/shard_map/dot_general | solution.py:186
  24.9 0.3 add.29
  25.2 1.4 %collective-permute-done.6 = bf16[512,384]{1,0:T(8,128)(2,1)S(1)} collective-permute-done((bf16[512,384]{1,0:T(8,128)(2,1)S(1)}, bf16[512,384]{1,0:T(8,128)(2,1)S(1)}, u32[]{:S(2)}, u32[]{:S(2)}) %collective-permute-start.6) | collective-permute-done | bytes 393248 | tf_op jit(solution)/shard_map/ppermute | solution.py:224
  26.6 2.0 %collective-permute-start.7 = (bf16[512,384]{1,0:T(8,128)(2,1)S(1)}, bf16[512,384]{1,0:T(8,128)(2,1)S(1)}, u32[]{:S(2)}, u32[]{:S(2)}) collective-permute-start(bf16[512,384]{1,0:T(8,128)(2,1)S(1)} %collective-permute-done.6), channel_id=1, source_target_pairs={{0,4},{4,8},{8,12},{12,14},{14,10},{10,6},{6,2},{2,0},{5,1},{9,5},... | collective-permute-start | bytes 1179656 | tf_op jit(solution)/shard_map/ppermute | solution.py:224
  28.6 0.5 %fusion.8 = f32[608,512]{1,0:T(8,128)S(1)} fusion(bf16[512,384]{1,0:T(8,128)(2,1)S(1)} %collective-permute-done.6, bf16[608,2688]{1,0:T(8,128)(2,1)S(1)} %get-tuple-element.21), kind=kOutput, calls=%fused_computation.10 | convolution fusion | flops 239075328 | bytes 2105344 | tf_op jit(solution)/shard_map/dot_general | solution.py:186
  29.1 0.3 add.30
  29.4 1.4 %collective-permute-done.5 = bf16[512,384]{1,0:T(8,128)(2,1)S(1)} collective-permute-done((bf16[512,384]{1,0:T(8,128)(2,1)S(1)}, bf16[512,384]{1,0:T(8,128)(2,1)S(1)}, u32[]{:S(2)}, u32[]{:S(2)}) %collective-permute-start.5) | collective-permute-done | bytes 393248 | tf_op jit(solution)/shard_map/ppermute | solution.py:224
  30.8 2.0 %collective-permute-start.9 = (bf16[512,384]{1,0:T(8,128)(2,1)S(1)}, bf16[512,384]{1,0:T(8,128)(2,1)S(1)}, u32[]{:S(2)}, u32[]{:S(2)}) collective-permute-start(bf16[512,384]{1,0:T(8,128)(2,1)S(1)} %collective-permute-done.5), channel_id=1, source_target_pairs={{0,4},{4,8},{8,12},{12,14},{14,10},{10,6},{6,2},{2,0},{5,1},{9,5},... | collective-permute-start | bytes 1179656 | tf_op jit(solution)/shard_map/ppermute | solution.py:224
  32.8 0.5 %fusion.6 = f32[608,512]{1,0:T(8,128)S(1)} fusion(bf16[512,384]{1,0:T(8,128)(2,1)S(1)} %collective-permute-done.5, bf16[608,2688]{1,0:T(8,128)(2,1)S(1)} %get-tuple-element.21), kind=kOutput, calls=%fused_computation.8 | convolution fusion | flops 239075328 | bytes 2105344 | tf_op jit(solution)/shard_map/dot_general | solution.py:186
  33.4 1.7 %collective-permute-done.7 = bf16[512,384]{1,0:T(8,128)(2,1)S(1)} collective-permute-done((bf16[512,384]{1,0:T(8,128)(2,1)S(1)}, bf16[512,384]{1,0:T(8,128)(2,1)S(1)}, u32[]{:S(2)}, u32[]{:S(2)}) %collective-permute-start.7) | collective-permute-done | bytes 393248 | tf_op jit(solution)/shard_map/ppermute | solution.py:224
  35.0 0.5 %add_add_fusion = f32[608,512]{1,0:T(8,128)S(1)} fusion(f32[608,512]{1,0:T(8,128)S(1)} %add.30, f32[608,512]{1,0:T(8,128)S(1)} %fusion.6, bf16[512,384]{1,0:T(8,128)(2,1)S(1)} %collective-permute-done.7, bf16[608,2688]{1,0:T(8,128)(2,1)S(1)} %get-tuple-element.21), kind=kOutput, calls=%fused_computation.2 | convolution fusion | flops 239697920 | bytes 4595712 | tf_op jit(solution)/shard_map/dot_general | solution.py:186
  35.6 0.1 collective-permute-start.8
  35.7 3.6 %collective-permute-done.9 = bf16[512,384]{1,0:T(8,128)(2,1)S(1)} collective-permute-done((bf16[512,384]{1,0:T(8,128)(2,1)S(1)}, bf16[512,384]{1,0:T(8,128)(2,1)S(1)}, u32[]{:S(2)}, u32[]{:S(2)}) %collective-permute-start.9) | collective-permute-done | bytes 393248 | tf_op jit(solution)/shard_map/ppermute | solution.py:224
  39.3 0.0 collective-permute-start.10
  39.3 0.4 fusion.18
  39.6 0.0 collective-permute-done.8
  39.6 1.4 %collective-permute-done.10 = bf16[512,384]{1,0:T(8,128)(2,1)S(1)} collective-permute-done((bf16[512,384]{1,0:T(8,128)(2,1)S(1)}, bf16[512,384]{1,0:T(8,128)(2,1)S(1)}, u32[]{:S(2)}, u32[]{:S(2)}) %collective-permute-start.10) | collective-permute-done | bytes 393248 | tf_op jit(solution)/shard_map/ppermute | solution.py:234
  41.0 1.1 %fusion = bf16[304,512]{1,0:T(8,128)(2,1)} fusion(bf16[512,384]{1,0:T(8,128)(2,1)S(1)} %collective-permute-done.10, f32[304,512]{1,0:T(8,128)S(1)} %fusion.18, f32[304,512]{1,0:T(8,128)S(1)} %collective-permute-done.8, f32[608,512]{1,0:T(8,128)S(1)} %add_add_fusion, bf16[304,768]{1,0:T(8,128)(2,1)S(1)} %get-tuple-element.29), kind=kOutput, calls=%fused_computation.3 | convolution fusion | flops 120160256 | bytes 2805760 | tf_op jit(solution)/shard_map/dot_general | solution.py:186
  (1 shorter events, 0.0 us)
Async XLA Ops:
  0.0 10.3 %collective-permute-start.1 = (bf16[304,6144]{1,0:T(8,128)(2,1)}, bf16[304,6144]{1,0:T(8,128)(2,1)}, u32[]{:S(2)}, u32[]{:S(2)}) collective-permute-start(bf16[304,6144]{1,0:T(8,128)(2,1)} %bitcast.13), channel_id=1, source_target_pairs={{0,1},{1,0},{2,3},{3,2},{4,5},{5,4},{6,7},{7,6},{8,9},{9,8},{10,11... | collective-permute-start | bytes 11206664 | tf_op jit(solution)/shard_map/ppermute | solution.py:202
  0.5 9.9 %copy-start = (bf16[6144,304]{0,1:T(8,128)(2,1)S(1)}, bf16[6144,304]{0,1:T(8,128)(2,1)}, u32[]{:S(2)}) copy-start(bf16[6144,304]{0,1:T(8,128)(2,1)} %param.7) | copy-start | bytes 11206660
  0.5 9.9 %copy-start.1 = (s32[64,2]{0,1:T(2,128)S(1)}, s32[64,2]{0,1:T(2,128)}, u32[]{:S(2)}) copy-start(s32[64,2]{0,1:T(2,128)} %param.5) | copy-start | bytes 1540
  4.9 3.1 %collective-permute-start.3 = (bf16[512,384]{1,0:T(8,128)(2,1)}, bf16[512,384]{1,0:T(8,128)(2,1)S(1)}, u32[]{:S(2)}, u32[]{:S(2)}) collective-permute-start(bf16[512,384]{1,0:T(8,128)(2,1)} %half_transform.1), channel_id=1, source_target_pairs={{0,1},{1,0},{2,3},{3,2},{4,5},{5,4},{6,7},{7,6},{8,9},{9,8},{10,11... | collective-permute-start | bytes 1179656 | tf_op jit(solution)/shard_map/ppermute | solution.py:214
  5.0 9.6 %collective-permute-start = (bf16[512,384]{1,0:T(8,128)(2,1)}, bf16[512,384]{1,0:T(8,128)(2,1)S(1)}, u32[]{:S(2)}, u32[]{:S(2)}) collective-permute-start(bf16[512,384]{1,0:T(8,128)(2,1)} %half_transform.1), channel_id=1, source_target_pairs={{0,4},{4,8},{8,12},{12,14},{14,10},{10,6},{6,2},{2,0},{5,1},{9,5},... | collective-permute-start | bytes 1179656 | tf_op jit(solution)/shard_map/ppermute | solution.py:224
  8.0 10.1 %collective-permute-start.4 = (bf16[512,384]{1,0:T(8,128)(2,1)S(1)}, bf16[512,384]{1,0:T(8,128)(2,1)S(1)}, u32[]{:S(2)}, u32[]{:S(2)}) collective-permute-start(bf16[512,384]{1,0:T(8,128)(2,1)S(1)} %collective-permute-done.3), channel_id=1, source_target_pairs={{0,4},{4,8},{8,12},{12,14},{14,10},{10,6},{6,2},{2,0},{5,1},{9,5},... | collective-permute-start | bytes 1179656 | tf_op jit(solution)/shard_map/ppermute | solution.py:224
  14.6 2.2 %copy-start.2 = (bf16[512,384]{1,0:T(8,128)(2,1)S(1)}, bf16[512,384]{1,0:T(8,128)(2,1)}, u32[]{:S(2)}) copy-start(bf16[512,384]{1,0:T(8,128)(2,1)} %half_transform.1) | copy-start | bytes 1179652
  14.6 7.8 %collective-permute-start.2 = (bf16[512,384]{1,0:T(8,128)(2,1)S(1)}, bf16[512,384]{1,0:T(8,128)(2,1)S(1)}, u32[]{:S(2)}, u32[]{:S(2)}) collective-permute-start(bf16[512,384]{1,0:T(8,128)(2,1)S(1)} %collective-permute-done), channel_id=1, source_target_pairs={{0,4},{4,8},{8,12},{12,14},{14,10},{10,6},{6,2},{2,0},{5,1},{9,5},... | collective-permute-start | bytes 1179656 | tf_op jit(solution)/shard_map/ppermute | solution.py:224
  18.1 8.5 %collective-permute-start.6 = (bf16[512,384]{1,0:T(8,128)(2,1)S(1)}, bf16[512,384]{1,0:T(8,128)(2,1)S(1)}, u32[]{:S(2)}, u32[]{:S(2)}) collective-permute-start(bf16[512,384]{1,0:T(8,128)(2,1)S(1)} %collective-permute-done.4), channel_id=1, source_target_pairs={{0,4},{4,8},{8,12},{12,14},{14,10},{10,6},{6,2},{2,0},{5,1},{9,5},... | collective-permute-start | bytes 1179656 | tf_op jit(solution)/shard_map/ppermute | solution.py:224
  22.4 8.4 %collective-permute-start.5 = (bf16[512,384]{1,0:T(8,128)(2,1)S(1)}, bf16[512,384]{1,0:T(8,128)(2,1)S(1)}, u32[]{:S(2)}, u32[]{:S(2)}) collective-permute-start(bf16[512,384]{1,0:T(8,128)(2,1)S(1)} %collective-permute-done.2), channel_id=1, source_target_pairs={{0,4},{4,8},{8,12},{12,14},{14,10},{10,6},{6,2},{2,0},{5,1},{9,5},... | collective-permute-start | bytes 1179656 | tf_op jit(solution)/shard_map/ppermute | solution.py:224
  26.6 8.4 %collective-permute-start.7 = (bf16[512,384]{1,0:T(8,128)(2,1)S(1)}, bf16[512,384]{1,0:T(8,128)(2,1)S(1)}, u32[]{:S(2)}, u32[]{:S(2)}) collective-permute-start(bf16[512,384]{1,0:T(8,128)(2,1)S(1)} %collective-permute-done.6), channel_id=1, source_target_pairs={{0,4},{4,8},{8,12},{12,14},{14,10},{10,6},{6,2},{2,0},{5,1},{9,5},... | collective-permute-start | bytes 1179656 | tf_op jit(solution)/shard_map/ppermute | solution.py:224
  30.8 8.4 %collective-permute-start.9 = (bf16[512,384]{1,0:T(8,128)(2,1)S(1)}, bf16[512,384]{1,0:T(8,128)(2,1)S(1)}, u32[]{:S(2)}, u32[]{:S(2)}) collective-permute-start(bf16[512,384]{1,0:T(8,128)(2,1)S(1)} %collective-permute-done.5), channel_id=1, source_target_pairs={{0,4},{4,8},{8,12},{12,14},{14,10},{10,6},{6,2},{2,0},{5,1},{9,5},... | collective-permute-start | bytes 1179656 | tf_op jit(solution)/shard_map/ppermute | solution.py:224
  35.6 4.0 %collective-permute-start.8 = (f32[304,512]{1,0:T(8,128)S(1)}, f32[304,512]{1,0:T(8,128)S(1)}, u32[]{:S(2)}, u32[]{:S(2)}) collective-permute-start(f32[304,512]{1,0:T(8,128)S(1)} %slice.45), channel_id=1, source_target_pairs={{0,1},{1,0},{2,3},{3,2},{4,5},{5,4},{6,7},{7,6},{8,9},{9,8},{10,11... | collective-permute-start | bytes 1867784 | tf_op jit(solution)/shard_map/ppermute | solution.py:232
  39.3 1.7 %collective-permute-start.10 = (bf16[512,384]{1,0:T(8,128)(2,1)S(1)}, bf16[512,384]{1,0:T(8,128)(2,1)S(1)}, u32[]{:S(2)}, u32[]{:S(2)}) collective-permute-start(bf16[512,384]{1,0:T(8,128)(2,1)S(1)} %collective-permute-done.9), channel_id=1, source_target_pairs={{0,1},{1,0},{2,3},{3,2},{4,5},{5,4},{6,7},{7,6},{8,9},{9,8},{10,11... | collective-permute-start | bytes 1179656 | tf_op jit(solution)/shard_map/ppermute | solution.py:234

commit v4 on v3

--- a/solution.py
+++ b/solution.py
@@ -12,8 +12,9 @@
 LANES = 128
 QB = 16
 PAIR = 2
-HALF_VMEM = 56 * 1024 * 1024
-WINDOW_VMEM = 24 * 1024 * 1024
+HALF_VMEM = 24 * 1024 * 1024
+STEP_VMEM = 24 * 1024 * 1024
+UNTIMED = pl.CostEstimate(flops=0, bytes_accessed=0, transcendentals=0)
 
 
 def occupied_rows(occ_ref, offset):
@@ -88,11 +89,12 @@
     occ_batch = occ.shape[0]
     width = AO_GROUP * QB
     rows, columns = occ_batch * ri_width, count * AO_GROUP
+    pairs, occ, tiles = (pltpu.with_memory_space_constraint(x, pltpu.HBM) for x in (pairs, occ, tiles))
     return pl.pallas_call(
         half_kernel,
         in_specs=[pl.BlockSpec(memory_space=pltpu.SMEM)] + [pl.BlockSpec(memory_space=pl.ANY)] * 3,
         out_specs=pl.BlockSpec(memory_space=pltpu.VMEM),
-        out_shape=jax.ShapeDtypeStruct((rows, columns), jnp.bfloat16),
+        out_shape=pltpu.VMEM((rows, columns), jnp.bfloat16),
         scratch_shapes=[
             pltpu.SMEM(pairs.shape, jnp.int32),
             pltpu.VMEM(occ.shape, jnp.bfloat16),
@@ -140,50 +142,116 @@
         write(j, here * keep + there * drop)
 
 
-def window_kernel(count, chips, me, pairs, own_ref, other_ref, both_ref, last_ref):
+def window_kernel(count, chips, me, pairs, vir_ref, own_ref, other_ref, last_ref):
     chip, core = me[0] // 2, lax.rem(me[0], 2)
     place = place_of(chip, chips)
-    behind = 2 * core - 1
-    rows, columns = own_ref.shape[0], count * AO_GROUP
+    columns = count * AO_GROUP
+
+    def store(out_ref, k, dev):
+        def write(j, value):
+            at = k * columns + j * LANES
+            out_ref[:, at : at + LANES] = value
+
+        take_windows(count, pairs, vir_ref, dev, write)
+
     for k in range(chips - 1):
-        source = chip_at(place + behind * ((k + 1) // 2), chips)
-        dev = 2 * source + (core if k == 0 or k % 2 == 1 else 1 - core)
-        for half, vir_ref in enumerate((own_ref, other_ref)):
-
-            def write(j, value, k=k, half=half):
-                at = k * columns + j * LANES
-                both_ref[half * rows : (half + 1) * rows, at : at + LANES] = value
-
-            take_windows(count, pairs, vir_ref, dev, write)
+        for out_ref, which in ((own_ref, core), (other_ref, 1 - core)):
+            source = chip_at(place + (2 * which - 1) * ((k + 1) // 2), chips)
+            store(out_ref, k, 2 * source + (which if k == 0 or k % 2 == 1 else 1 - which))
     source = chip_at(place + chips // 2, chips)
-    for k, dev in enumerate((2 * source + core, 2 * source + 1 - core)):
-
-        def write(j, value, k=k):
-            at = k * columns + j * LANES
-            last_ref[:, at : at + LANES] = value
-
-        take_windows(count, pairs, own_ref, dev, write)
-
-
-def windows(me, pairs, vir, other_vir, count, chips):
+    store(last_ref, 0, 2 * source + core)
+    store(last_ref, 1, 2 * source + 1 - core)
+
+
+def windows(me, pairs, vir, count, chips):
     rows, columns = vir.shape[0], count * AO_GROUP
     smem, vmem = pl.BlockSpec(memory_space=pltpu.SMEM), pl.BlockSpec(memory_space=pltpu.VMEM)
     return pl.pallas_call(
         functools.partial(window_kernel, count, chips),
-        in_specs=[smem, smem, vmem, vmem],
-        out_specs=[vmem, vmem],
+        in_specs=[smem, smem, vmem],
+        out_specs=[vmem, vmem, vmem],
         out_shape=[
-            jax.ShapeDtypeStruct((2 * rows, (chips - 1) * columns), vir.dtype),
+            jax.ShapeDtypeStruct((rows, (chips - 1) * columns), vir.dtype),
+            jax.ShapeDtypeStruct((rows, (chips - 1) * columns), vir.dtype),
             jax.ShapeDtypeStruct((rows, 2 * columns), vir.dtype),
         ],
-        compiler_params=pltpu.CompilerParams(vmem_limit_bytes=WINDOW_VMEM),
-        cost_estimate=pl.CostEstimate(flops=0, bytes_accessed=8 * vir.size, transcendentals=0),
+        compiler_params=pltpu.CompilerParams(vmem_limit_bytes=STEP_VMEM),
+        cost_estimate=UNTIMED,
         name="vir_windows",
-    )(me, pairs, vir, other_vir)
-
-
-def product(vir, block):
+    )(me, pairs, vir)
+
+
+def dot_columns(vir, block):
     return lax.dot_general(vir, block, (((1,), (1,)), ((), ())), preferred_element_type=jnp.float32)
+
+
+def add_kernel(k, own_w, other_w, block, other_block, *refs):
+    columns = block.shape[1]
+    at = slice(k * columns, (k + 1) * columns)
+    total = dot_columns(own_w[:, at], block[...]) + dot_columns(other_w[:, at], other_block[...])
+    refs[-1][...] = total + refs[0][...] if len(refs) == 2 else total
+
+
+def add_blocks(total, k, own_w, other_w, block, other_block):
+    shape = jax.ShapeDtypeStruct((own_w.shape[0], block.shape[0]), jnp.float32)
+    vmem = pl.BlockSpec(memory_space=pltpu.VMEM)
+    before = () if total is None else (total,)
+    return pl.pallas_call(
+        functools.partial(add_kernel, k),
+        in_specs=[vmem] * (4 + len(before)),
+        out_specs=vmem,
+        out_shape=shape,
+        input_output_aliases={4: 0} if before else {},
+        compiler_params=pltpu.CompilerParams(vmem_limit_bytes=STEP_VMEM),
+        cost_estimate=UNTIMED,
+        name="add_blocks",
+    )(own_w, other_w, block, other_block, *before)
+
+
+def last_kernel(last_w, last, own_sum, out_ref):
+    out_ref[...] = own_sum[...] + dot_columns(last_w[:, : last.shape[1]], last[...])
+
+
+def add_last(last_w, last, own_sum):
+    vmem = pl.BlockSpec(memory_space=pltpu.VMEM)
+    return pl.pallas_call(
+        last_kernel,
+        in_specs=[vmem] * 3,
+        out_specs=vmem,
+        out_shape=jax.ShapeDtypeStruct(own_sum.shape, own_sum.dtype),
+        input_output_aliases={2: 0},
+        compiler_params=pltpu.CompilerParams(vmem_limit_bytes=STEP_VMEM),
+        cost_estimate=UNTIMED,
+        name="add_last",
+    )(last_w, last, own_sum)
+
+
+def finish_kernel(cuts, last_w, block, total, out_hbm, out, sems):
+    columns = block.shape[1]
+    copies = []
+    for p, (begin, end) in enumerate(zip(cuts[:-1], cuts[1:])):
+        value = total[begin:end] + dot_columns(last_w[begin:end, columns:], block[...])
+        out[begin:end] = value.astype(out.dtype)
+        copies.append(pltpu.make_async_copy(out.at[begin:end], out_hbm.at[begin:end], sems.at[p]))
+        copies[-1].start()
+    for copy in copies:
+        copy.wait()
+
+
+def finish(last_w, block, total):
+    rows = total.shape[0]
+    cuts = [0, rows // 32 * 16, rows] if rows % 16 == 0 else [0, rows]
+    vmem = pl.BlockSpec(memory_space=pltpu.VMEM)
+    return pl.pallas_call(
+        functools.partial(finish_kernel, cuts),
+        in_specs=[vmem] * 3,
+        out_specs=pl.BlockSpec(memory_space=pl.ANY),
+        out_shape=jax.ShapeDtypeStruct(total.shape, jnp.bfloat16),
+        scratch_shapes=[pltpu.VMEM(total.shape, jnp.bfloat16), pltpu.SemaphoreType.DMA((len(cuts) - 1,))],
+        compiler_params=pltpu.CompilerParams(vmem_limit_bytes=STEP_VMEM),
+        cost_estimate=UNTIMED,
+        name="finish",
+    )(last_w, block, total)
 
 
 def on_device(chips, tiles, pairs, occ_coef, vir_coef):
@@ -191,7 +259,6 @@
     columns = count * AO_GROUP
     me = lax.axis_index("ao").astype(jnp.int32).reshape(1)
     pairs, occ, vir = pairs.T, occ_coef.T, vir_coef.T
-    rows = vir.shape[0]
 
     ring = [2 * p if p < chips // 2 else 2 * (chips - 1 - p) + 1 for p in range(chips)]
     links = [(ring[p], ring[(p + 1) % chips]) for p in range(chips)]
@@ -199,40 +266,38 @@
     across = [(d, d ^ 1) for d in range(2 * chips)]
 
     own = half_transform(me, pairs, occ, tiles)
-    both_w, last_w = windows(me, pairs, vir, lax.ppermute(vir, "ao", across), count, chips)
-    blocks = [own]
-    sums, summed = None, 0
-
-    def add_to(sums, k):
-        term = product(both_w[:, k * columns : (k + 1) * columns], blocks[k])
-        return term if sums is None else sums + term
-
+    blocks, other_blocks = [own], [lax.ppermute(own, "ao", across)]
+    first_other, vir = lax.optimization_barrier((other_blocks[0], vir))
+    own_w, other_w, last_w = windows(me, pairs, vir, count, chips)
+    total, summed = None, 0
     for message in range(1, chips):
         if message == 1:
             block = own
         elif message == 2:
-            block = lax.ppermute(own, "ao", across)
+            block = first_other
         else:
             block = blocks[message - 2]
         if message == 3:
-            block, both_w, last_w = lax.optimization_barrier((block, both_w, last_w))
-        elif message > 3:
-            while summed < message - 2:
-                sums = add_to(sums, summed)
-                summed += 1
-            block, sums = lax.optimization_barrier((block, sums))
+            block, own_w, other_w, last_w = lax.optimization_barrier((block, own_w, other_w, last_w))
+        if message > 3:
+            total = add_blocks(total, summed, own_w, other_w, blocks[summed], other_blocks[summed])
+            summed += 1
+            block, total = lax.optimization_barrier((block, total))
         block = lax.ppermute(block, "ao", onward)
         if message < chips - 1:
             blocks.append(block)
+            other_blocks.append(lax.ppermute(block, "ao", across))
         else:
             last = block
+    while summed < len(blocks) - 1:
+        total = add_blocks(total, summed, own_w, other_w, blocks[summed], other_blocks[summed])
+        summed += 1
+    last, total = lax.optimization_barrier((last, total))
+    other_last = lax.ppermute(last, "ao", across)
     while summed < len(blocks):
-        sums = add_to(sums, summed)
+        total = add_blocks(total, summed, own_w, other_w, blocks[summed], other_blocks[summed])
         summed += 1
-    received = lax.ppermute(sums[rows:], "ao", across)
-    total = sums[:rows] + received + product(last_w[:, :columns], last)
-    total = total + product(last_w[:, columns:], lax.ppermute(last, "ao", across))
-    return total.astype(jnp.bfloat16)
+    return finish(last_w, other_last, add_last(last_w, last, total))
 
 
 def solution(mesh):

time: 42.2 us -> 41.5 us (0.983)
  matrix products: 5.06 us -> 0 us
  waiting for transfers between devices: 11.7 us -> 16.1 us
  Pallas kernels: 8.62 us -> 11.6 us
  starting transfers between devices: 15.7 us -> 13.6 us
  other arithmetic: 0.78 us -> 0 us
    pallas_call x0 -> x9, Pallas kernels: none -> 5.12 us  [the longest x7 3.66 us: add_blocks(): pl.pallas_call(functools.partial(add_kernel, k), in_specs=[vmem] * (4 + l...]
    dot_general x9 -> x0, matrix products: 5.06 us -> none  [product(): lax.dot_general(vir, block, (((1,), (1,)), ((), ())), preferred_element_t...]
    ppermute x7, waiting for transfers between devices: 10.4 us -> 15.2 us  [on_device(): block = lax.ppermute(block, 'ao', onward)]
    ppermute x7, starting transfers between devices: 15 us -> 13.1 us  [on_device(): block = lax.ppermute(block, 'ao', onward)]
    pallas_call x1, Pallas kernels: 4.24 us -> 2.8 us  [windows(): pl.pallas_call(functools.partial(window_kernel, count, chips), in_specs=[...]
    add x3 -> x0, other arithmetic: 0.78 us -> none  [add_to(): return term if sums is None else sums + term]
    pallas_call x1, Pallas kernels: 4.39 us -> 3.64 us  [half_transform(): pl.pallas_call(half_kernel, in_specs=[pl.BlockSpec(memory_space=pltpu.SME...]
    ppermute x4 -> x8, waiting for transfers between devices: 1.36 us -> 0.83 us  [the longest x1 0.81 us: on_device(): other_last = lax.ppermute(last, 'ao', across)]
  transfers between devices with their start and end apart: 11 -> 15, of which waited for: 7 -> 8; matrix products, arithmetic and copies ran while one was open for 11% -> 0% of each run, Pallas kernels for 20% -> 17%
where the time goes in v4:
time: 41.5 us; the launch traced here: 41.3 us
  waiting for transfers between devices  16.1 us (39%)
  starting transfers between devices  13.6 us (33%)
  Pallas kernels  11.6 us (28%)
    ppermute x7, waiting for transfers between devices, on_device(): block = lax.ppermute(block, 'ao', onward)  15.2 us
    ppermute x7, starting transfers between devices, on_device(): block = lax.ppermute(block, 'ao', onward)  13.1 us
    pallas_call x7, Pallas kernels, add_blocks(): pl.pallas_call(functools.partial(add_kernel, k), in_specs=[vmem] * (4 + l...  3.66 us
    pallas_call x1, Pallas kernels, half_transform(): pl.pallas_call(half_kernel, in_specs=[pl.BlockSpec(memory_space=pltpu.SME...  3.64 us
    pallas_call x1, Pallas kernels, windows(): pl.pallas_call(functools.partial(window_kernel, count, chips), in_specs=[...  2.8 us
    pallas_call x1, Pallas kernels, finish(): pl.pallas_call(functools.partial(finish_kernel, cuts), in_specs=[vmem] *...  1.09 us
  transfers between devices with their start and end apart: 15, of which 8 were waited for; matrix products, arithmetic and copies ran while one was open for 0% of the time, Pallas kernels for 17%

profile of v4, /device:TPU:0, one launch (start us, length us, event | category | flops | bytes accessed | tf_op | source)
XLA Modules:
  0.0 41.3 jit_solution(4936516890845904798)
XLA Ops:
  0.0 0.0 copy-start
  0.0 0.0 copy-start.1
  0.0 3.6 %half_transform.1.block = bf16[512,384]{1,0:T(8,128)(2,1)S(1)} custom-call(s32[1]{0:T(128)} %bitcast.me, s32[2,64]{1,0:T(2,128)} %bitcast.5, bf16[8,6144]{1,0:T(8,128)(2,1)} %bitcast.7, bf16[4,128,64,128]{3,2,1,0:T(8,128)(2,1)} %tiles_ref.1), custom_call_target="tpu_custom_call" | custom-call | flops 603979776 | bytes 8388608 | tf_op jit(solution)/shard_map/half_transform/pallas_call | solution.py:93
  3.7 0.5 %collective-permute-start.1 = (bf16[512,384]{1,0:T(8,128)(2,1)S(1)}, bf16[512,384]{1,0:T(8,128)(2,1)S(1)}, u32[]{:S(2)}, u32[]{:S(2)}) collective-permute-start(bf16[512,384]{1,0:T(8,128)(2,1)S(1)} %half_transform.1.block), channel_id=1, source_target_pairs={{0,1},{1,0},{2,3},{3,2},{4,5},{5,4},{6,7},{7,6},{8,9},{9,8},{10,11... | collective-permute-start | bytes 1179656 | tf_op jit(solution)/shard_map/ppermute | solution.py:269
  4.2 2.6 %collective-permute-start = (bf16[512,384]{1,0:T(8,128)(2,1)S(1)}, bf16[512,384]{1,0:T(8,128)(2,1)S(1)}, u32[]{:S(2)}, u32[]{:S(2)}) collective-permute-start(bf16[512,384]{1,0:T(8,128)(2,1)S(1)} %half_transform.1.block), channel_id=1, source_target_pairs={{0,4},{4,8},{8,12},{12,14},{14,10},{10,6},{6,2},{2,0},{5,1},{9,5},... | collective-permute-start | bytes 1179656 | tf_op jit(solution)/shard_map/ppermute | solution.py:286
  6.8 0.0 collective-permute-done.1.other_block
  6.8 0.0 copy-done
  6.8 0.0 copy-done.1
  6.8 2.8 %vir_windows.1 = (bf16[304,2688]{1,0:T(8,128)(2,1)S(1)}, bf16[304,2688]{1,0:T(8,128)(2,1)S(1)}, bf16[304,768]{1,0:T(8,128)(2,1)S(1)}) custom-call(s32[1]{0:T(128)} %bitcast.me, s32[2,64]{1,0:T(2,128)S(1)} %bitcast.6, bf16[304,6144]{1,0:T(8,128)(2,1)S(1)} %bitcast.4), custom_call_target="tpu_custom_call" | custom-call | tf_op jit(solution)/shard_map/vir_windows/pallas_call | solution.py:169
  9.6 1.7 %collective-permute-start.4 = (bf16[512,384]{1,0:T(8,128)(2,1)S(1)}, bf16[512,384]{1,0:T(8,128)(2,1)S(1)}, u32[]{:S(2)}, u32[]{:S(2)}) collective-permute-start(bf16[512,384]{1,0:T(8,128)(2,1)S(1)} %collective-permute-done.1.other_block), channel_id=1, source_target_pairs={{0,4},{4,8},{8,12},{12,14},{14,10},{10,6},{6,2},{2,0},{5,1},{9,5},... | collective-permute-start | bytes 1179656 | tf_op jit(solution)/shard_map/ppermute | solution.py:286
  11.3 1.2 %collective-permute-done.block = bf16[512,384]{1,0:T(8,128)(2,1)S(1)} collective-permute-done((bf16[512,384]{1,0:T(8,128)(2,1)S(1)}, bf16[512,384]{1,0:T(8,128)(2,1)S(1)}, u32[]{:S(2)}, u32[]{:S(2)}) %collective-permute-start) | collective-permute-done | bytes 393248 | tf_op jit(solution)/shard_map/ppermute | solution.py:286
  12.5 2.1 %collective-permute-start.2 = (bf16[512,384]{1,0:T(8,128)(2,1)S(1)}, bf16[512,384]{1,0:T(8,128)(2,1)S(1)}, u32[]{:S(2)}, u32[]{:S(2)}) collective-permute-start(bf16[512,384]{1,0:T(8,128)(2,1)S(1)} %collective-permute-done.block), channel_id=1, source_target_pairs={{0,4},{4,8},{8,12},{12,14},{14,10},{10,6},{6,2},{2,0},{5,1},{9,5},... | collective-permute-start | bytes 1179656 | tf_op jit(solution)/shard_map/ppermute | solution.py:286
  14.6 0.0 collective-permute-start.3
  14.6 0.5 %add_blocks.7.refs_0_ = f32[304,512]{1,0:T(8,128)S(1)} custom-call(bf16[304,2688]{1,0:T(8,128)(2,1)S(1)} %get-tuple-element.30.own_w, bf16[304,2688]{1,0:T(8,128)(2,1)S(1)} %get-tuple-element.31.other_w, bf16[512,384]{1,0:T(8,128)(2,1)S(1)} %half_transform.1.block, bf16[512,384]{1,0:T(8,128)(2,1)S(1)} %collective-permute-done.1.other_block), custom_call_target="tpu_custom_call" | custom-call | tf_op jit(solution)/shard_map/add_blocks/pallas_call | solution.py:199
  15.1 2.4 %collective-permute-done.4.block = bf16[512,384]{1,0:T(8,128)(2,1)S(1)} collective-permute-done((bf16[512,384]{1,0:T(8,128)(2,1)S(1)}, bf16[512,384]{1,0:T(8,128)(2,1)S(1)}, u32[]{:S(2)}, u32[]{:S(2)}) %collective-permute-start.4) | collective-permute-done | bytes 393248 | tf_op jit(solution)/shard_map/ppermute | solution.py:286
  17.5 0.0 collective-permute-start.8
  17.5 1.7 %collective-permute-start.7 = (bf16[512,384]{1,0:T(8,128)(2,1)S(1)}, bf16[512,384]{1,0:T(8,128)(2,1)S(1)}, u32[]{:S(2)}, u32[]{:S(2)}) collective-permute-start(bf16[512,384]{1,0:T(8,128)(2,1)S(1)} %collective-permute-done.4.block), channel_id=1, source_target_pairs={{0,4},{4,8},{8,12},{12,14},{14,10},{10,6},{6,2},{2,0},{5,1},{9,5},... | collective-permute-start | bytes 1179656 | tf_op jit(solution)/shard_map/ppermute | solution.py:286
  19.1 2.6 %collective-permute-done.2.block = bf16[512,384]{1,0:T(8,128)(2,1)S(1)} collective-permute-done((bf16[512,384]{1,0:T(8,128)(2,1)S(1)}, bf16[512,384]{1,0:T(8,128)(2,1)S(1)}, u32[]{:S(2)}, u32[]{:S(2)}) %collective-permute-start.2) | collective-permute-done | bytes 393248 | tf_op jit(solution)/shard_map/ppermute | solution.py:286
  21.7 0.0 collective-permute-start.6
  21.7 0.0 collective-permute-done.3.other_block
  21.7 0.5 %add_blocks.8.refs_0_ = f32[304,512]{1,0:T(8,128)S(1)} custom-call(bf16[304,2688]{1,0:T(8,128)(2,1)S(1)} %get-tuple-element.30.own_w, bf16[304,2688]{1,0:T(8,128)(2,1)S(1)} %get-tuple-element.31.other_w, bf16[512,384]{1,0:T(8,128)(2,1)S(1)} %collective-permute-done.block, ...), custom_call_target="tpu_custom_call", output_to_operand_aliasing={{}: (4, {})} | custom-call | tf_op jit(solution)/shard_map/add_blocks/pallas_call | solution.py:199
  22.2 1.7 %collective-permute-start.5 = (bf16[512,384]{1,0:T(8,128)(2,1)S(1)}, bf16[512,384]{1,0:T(8,128)(2,1)S(1)}, u32[]{:S(2)}, u32[]{:S(2)}) collective-permute-start(bf16[512,384]{1,0:T(8,128)(2,1)S(1)} %collective-permute-done.2.block), channel_id=1, source_target_pairs={{0,4},{4,8},{8,12},{12,14},{14,10},{10,6},{6,2},{2,0},{5,1},{9,5},... | collective-permute-start | bytes 1179656 | tf_op jit(solution)/shard_map/ppermute | solution.py:286
  23.9 0.0 collective-permute-done.8.other_block
  23.9 0.5 %add_blocks.9.refs_0_ = f32[304,512]{1,0:T(8,128)S(1)} custom-call(bf16[304,2688]{1,0:T(8,128)(2,1)S(1)} %get-tuple-element.30.own_w, bf16[304,2688]{1,0:T(8,128)(2,1)S(1)} %get-tuple-element.31.other_w, bf16[512,384]{1,0:T(8,128)(2,1)S(1)} %collective-permute-done.4.block, ...), custom_call_target="tpu_custom_call", output_to_operand_aliasing={{}: (4, {})} | custom-call | tf_op jit(solution)/shard_map/add_blocks/pallas_call | solution.py:199
  24.4 1.4 %collective-permute-done.7.block = bf16[512,384]{1,0:T(8,128)(2,1)S(1)} collective-permute-done((bf16[512,384]{1,0:T(8,128)(2,1)S(1)}, bf16[512,384]{1,0:T(8,128)(2,1)S(1)}, u32[]{:S(2)}, u32[]{:S(2)}) %collective-permute-start.7) | collective-permute-done | bytes 393248 | tf_op jit(solution)/shard_map/ppermute | solution.py:286
  25.9 1.7 %collective-permute-start.13 = (bf16[512,384]{1,0:T(8,128)(2,1)S(1)}, bf16[512,384]{1,0:T(8,128)(2,1)S(1)}, u32[]{:S(2)}, u32[]{:S(2)}) collective-permute-start(bf16[512,384]{1,0:T(8,128)(2,1)S(1)} %collective-permute-done.7.block), channel_id=1, source_target_pairs={{0,4},{4,8},{8,12},{12,14},{14,10},{10,6},{6,2},{2,0},{5,1},{9,5},... | collective-permute-start | bytes 1179656 | tf_op jit(solution)/shard_map/ppermute | solution.py:286
  27.5 0.0 collective-permute-start.11
  27.5 0.0 collective-permute-done.6.other_block
  27.5 0.5 %add_blocks.10.refs_0_ = f32[304,512]{1,0:T(8,128)S(1)} custom-call(bf16[304,2688]{1,0:T(8,128)(2,1)S(1)} %get-tuple-element.30.own_w, bf16[304,2688]{1,0:T(8,128)(2,1)S(1)} %get-tuple-element.31.other_w, bf16[512,384]{1,0:T(8,128)(2,1)S(1)} %collective-permute-done.2.block, ...), custom_call_target="tpu_custom_call", output_to_operand_aliasing={{}: (4, {})} | custom-call | tf_op jit(solution)/shard_map/add_blocks/pallas_call | solution.py:199
  28.1 2.0 %collective-permute-done.5.block = bf16[512,384]{1,0:T(8,128)(2,1)S(1)} collective-permute-done((bf16[512,384]{1,0:T(8,128)(2,1)S(1)}, bf16[512,384]{1,0:T(8,128)(2,1)S(1)}, u32[]{:S(2)}, u32[]{:S(2)}) %collective-permute-start.5) | collective-permute-done | bytes 393248 | tf_op jit(solution)/shard_map/ppermute | solution.py:286
  30.1 0.0 collective-permute-start.10
  30.1 1.7 %collective-permute-start.9 = (bf16[512,384]{1,0:T(8,128)(2,1)S(1)}, bf16[512,384]{1,0:T(8,128)(2,1)S(1)}, u32[]{:S(2)}, u32[]{:S(2)}) collective-permute-start(bf16[512,384]{1,0:T(8,128)(2,1)S(1)} %collective-permute-done.5.block), channel_id=1, source_target_pairs={{0,4},{4,8},{8,12},{12,14},{14,10},{10,6},{6,2},{2,0},{5,1},{9,5},... | collective-permute-start | bytes 1179656 | tf_op jit(solution)/shard_map/ppermute | solution.py:286
  31.8 2.6 %collective-permute-done.13.block = bf16[512,384]{1,0:T(8,128)(2,1)S(1)} collective-permute-done((bf16[512,384]{1,0:T(8,128)(2,1)S(1)}, bf16[512,384]{1,0:T(8,128)(2,1)S(1)}, u32[]{:S(2)}, u32[]{:S(2)}) %collective-permute-start.13) | collective-permute-done | bytes 393248 | tf_op jit(solution)/shard_map/ppermute | solution.py:286
  34.3 0.0 collective-permute-start.14
  34.3 0.0 collective-permute-done.11.other_block
  34.3 0.5 %add_blocks.11.refs_0_ = f32[304,512]{1,0:T(8,128)S(1)} custom-call(bf16[304,2688]{1,0:T(8,128)(2,1)S(1)} %get-tuple-element.30.own_w, bf16[304,2688]{1,0:T(8,128)(2,1)S(1)} %get-tuple-element.31.other_w, bf16[512,384]{1,0:T(8,128)(2,1)S(1)} %collective-permute-done.7.block, ...), custom_call_target="tpu_custom_call", output_to_operand_aliasing={{}: (4, {})} | custom-call | tf_op jit(solution)/shard_map/add_blocks/pallas_call | solution.py:199
  34.9 0.0 collective-permute-done.10.other_block
  34.9 0.5 %add_blocks.12.refs_0_ = f32[304,512]{1,0:T(8,128)S(1)} custom-call(bf16[304,2688]{1,0:T(8,128)(2,1)S(1)} %get-tuple-element.30.own_w, bf16[304,2688]{1,0:T(8,128)(2,1)S(1)} %get-tuple-element.31.other_w, bf16[512,384]{1,0:T(8,128)(2,1)S(1)} %collective-permute-done.5.block, ...), custom_call_target="tpu_custom_call", output_to_operand_aliasing={{}: (4, {})} | custom-call | tf_op jit(solution)/shard_map/add_blocks/pallas_call | solution.py:199
  35.4 3.1 %collective-permute-done.9.last = bf16[512,384]{1,0:T(8,128)(2,1)S(1)} collective-permute-done((bf16[512,384]{1,0:T(8,128)(2,1)S(1)}, bf16[512,384]{1,0:T(8,128)(2,1)S(1)}, u32[]{:S(2)}, u32[]{:S(2)}) %collective-permute-start.9) | collective-permute-done | bytes 393248 | tf_op jit(solution)/shard_map/ppermute | solution.py:286
  38.5 0.0 collective-permute-start.12
  38.5 0.0 collective-permute-done.14.other_block
  38.5 0.5 %add_blocks.13.own_sum = f32[304,512]{1,0:T(8,128)S(1)} custom-call(bf16[304,2688]{1,0:T(8,128)(2,1)S(1)} %get-tuple-element.30.own_w, bf16[304,2688]{1,0:T(8,128)(2,1)S(1)} %get-tuple-element.31.other_w, bf16[512,384]{1,0:T(8,128)(2,1)S(1)} %collective-permute-done.13.block, ...), custom_call_target="tpu_custom_call", output_to_operand_aliasing={{}: (4, {})} | custom-call | tf_op jit(solution)/shard_map/add_blocks/pallas_call | solution.py:199
  39.1 0.4 add_last.1.total
  39.4 0.8 %collective-permute-done.12.block = bf16[512,384]{1,0:T(8,128)(2,1)S(1)} collective-permute-done((bf16[512,384]{1,0:T(8,128)(2,1)S(1)}, bf16[512,384]{1,0:T(8,128)(2,1)S(1)}, u32[]{:S(2)}, u32[]{:S(2)}) %collective-permute-start.12) | collective-permute-done | bytes 393248 | tf_op jit(solution)/shard_map/ppermute | solution.py:296
  40.3 1.1 %finish.1 = bf16[304,512]{1,0:T(8,128)(2,1)} custom-call(bf16[304,768]{1,0:T(8,128)(2,1)S(1)} %get-tuple-element.28.last_w, bf16[512,384]{1,0:T(8,128)(2,1)S(1)} %collective-permute-done.12.block, f32[304,512]{1,0:T(8,128)S(1)} %add_last.1.total), custom_call_target="tpu_custom_call" | custom-call | tf_op jit(solution)/shard_map/finish/pallas_call | solution.py:245
Async XLA Ops:
  0.0 6.8 %copy-start = (bf16[6144,304]{0,1:T(8,128)(2,1)S(1)}, bf16[6144,304]{0,1:T(8,128)(2,1)}, u32[]{:S(2)}) copy-start(bf16[6144,304]{0,1:T(8,128)(2,1)} %param.7) | copy-start | bytes 11206660
  0.0 6.8 %copy-start.1 = (s32[64,2]{0,1:T(2,128)S(1)}, s32[64,2]{0,1:T(2,128)}, u32[]{:S(2)}) copy-start(s32[64,2]{0,1:T(2,128)} %param.5) | copy-start | bytes 1540
  3.7 3.2 %collective-permute-start.1 = (bf16[512,384]{1,0:T(8,128)(2,1)S(1)}, bf16[512,384]{1,0:T(8,128)(2,1)S(1)}, u32[]{:S(2)}, u32[]{:S(2)}) collective-permute-start(bf16[512,384]{1,0:T(8,128)(2,1)S(1)} %half_transform.1.block), channel_id=1, source_target_pairs={{0,1},{1,0},{2,3},{3,2},{4,5},{5,4},{6,7},{7,6},{8,9},{9,8},{10,11... | collective-permute-start | bytes 1179656 | tf_op jit(solution)/shard_map/ppermute | solution.py:269
  4.2 8.3 %collective-permute-start = (bf16[512,384]{1,0:T(8,128)(2,1)S(1)}, bf16[512,384]{1,0:T(8,128)(2,1)S(1)}, u32[]{:S(2)}, u32[]{:S(2)}) collective-permute-start(bf16[512,384]{1,0:T(8,128)(2,1)S(1)} %half_transform.1.block), channel_id=1, source_target_pairs={{0,4},{4,8},{8,12},{12,14},{14,10},{10,6},{6,2},{2,0},{5,1},{9,5},... | collective-permute-start | bytes 1179656 | tf_op jit(solution)/shard_map/ppermute | solution.py:286
  9.6 7.8 %collective-permute-start.4 = (bf16[512,384]{1,0:T(8,128)(2,1)S(1)}, bf16[512,384]{1,0:T(8,128)(2,1)S(1)}, u32[]{:S(2)}, u32[]{:S(2)}) collective-permute-start(bf16[512,384]{1,0:T(8,128)(2,1)S(1)} %collective-permute-done.1.other_block), channel_id=1, source_target_pairs={{0,4},{4,8},{8,12},{12,14},{14,10},{10,6},{6,2},{2,0},{5,1},{9,5},... | collective-permute-start | bytes 1179656 | tf_op jit(solution)/shard_map/ppermute | solution.py:286
  12.5 9.2 %collective-permute-start.2 = (bf16[512,384]{1,0:T(8,128)(2,1)S(1)}, bf16[512,384]{1,0:T(8,128)(2,1)S(1)}, u32[]{:S(2)}, u32[]{:S(2)}) collective-permute-start(bf16[512,384]{1,0:T(8,128)(2,1)S(1)} %collective-permute-done.block), channel_id=1, source_target_pairs={{0,4},{4,8},{8,12},{12,14},{14,10},{10,6},{6,2},{2,0},{5,1},{9,5},... | collective-permute-start | bytes 1179656 | tf_op jit(solution)/shard_map/ppermute | solution.py:286
  14.6 7.1 %collective-permute-start.3 = (bf16[512,384]{1,0:T(8,128)(2,1)S(1)}, bf16[512,384]{1,0:T(8,128)(2,1)S(1)}, u32[]{:S(2)}, u32[]{:S(2)}) collective-permute-start(bf16[512,384]{1,0:T(8,128)(2,1)S(1)} %collective-permute-done.block), channel_id=1, source_target_pairs={{0,1},{1,0},{2,3},{3,2},{4,5},{5,4},{6,7},{7,6},{8,9},{9,8},{10,11... | collective-permute-start | bytes 1179656 | tf_op jit(solution)/shard_map/ppermute | solution.py:289
  17.5 6.5 %collective-permute-start.8 = (bf16[512,384]{1,0:T(8,128)(2,1)S(1)}, bf16[512,384]{1,0:T(8,128)(2,1)S(1)}, u32[]{:S(2)}, u32[]{:S(2)}) collective-permute-start(bf16[512,384]{1,0:T(8,128)(2,1)S(1)} %collective-permute-done.4.block), channel_id=1, source_target_pairs={{0,1},{1,0},{2,3},{3,2},{4,5},{5,4},{6,7},{7,6},{8,9},{9,8},{10,11... | collective-permute-start | bytes 1179656 | tf_op jit(solution)/shard_map/ppermute | solution.py:289
  17.5 8.4 %collective-permute-start.7 = (bf16[512,384]{1,0:T(8,128)(2,1)S(1)}, bf16[512,384]{1,0:T(8,128)(2,1)S(1)}, u32[]{:S(2)}, u32[]{:S(2)}) collective-permute-start(bf16[512,384]{1,0:T(8,128)(2,1)S(1)} %collective-permute-done.4.block), channel_id=1, source_target_pairs={{0,4},{4,8},{8,12},{12,14},{14,10},{10,6},{6,2},{2,0},{5,1},{9,5},... | collective-permute-start | bytes 1179656 | tf_op jit(solution)/shard_map/ppermute | solution.py:286
  21.7 5.9 %collective-permute-start.6 = (bf16[512,384]{1,0:T(8,128)(2,1)S(1)}, bf16[512,384]{1,0:T(8,128)(2,1)S(1)}, u32[]{:S(2)}, u32[]{:S(2)}) collective-permute-start(bf16[512,384]{1,0:T(8,128)(2,1)S(1)} %collective-permute-done.2.block), channel_id=1, source_target_pairs={{0,1},{1,0},{2,3},{3,2},{4,5},{5,4},{6,7},{7,6},{8,9},{9,8},{10,11... | collective-permute-start | bytes 1179656 | tf_op jit(solution)/shard_map/ppermute | solution.py:289
  22.2 7.9 %collective-permute-start.5 = (bf16[512,384]{1,0:T(8,128)(2,1)S(1)}, bf16[512,384]{1,0:T(8,128)(2,1)S(1)}, u32[]{:S(2)}, u32[]{:S(2)}) collective-permute-start(bf16[512,384]{1,0:T(8,128)(2,1)S(1)} %collective-permute-done.2.block), channel_id=1, source_target_pairs={{0,4},{4,8},{8,12},{12,14},{14,10},{10,6},{6,2},{2,0},{5,1},{9,5},... | collective-permute-start | bytes 1179656 | tf_op jit(solution)/shard_map/ppermute | solution.py:286
  25.9 8.4 %collective-permute-start.13 = (bf16[512,384]{1,0:T(8,128)(2,1)S(1)}, bf16[512,384]{1,0:T(8,128)(2,1)S(1)}, u32[]{:S(2)}, u32[]{:S(2)}) collective-permute-start(bf16[512,384]{1,0:T(8,128)(2,1)S(1)} %collective-permute-done.7.block), channel_id=1, source_target_pairs={{0,4},{4,8},{8,12},{12,14},{14,10},{10,6},{6,2},{2,0},{5,1},{9,5},... | collective-permute-start | bytes 1179656 | tf_op jit(solution)/shard_map/ppermute | solution.py:286
  27.5 6.8 %collective-permute-start.11 = (bf16[512,384]{1,0:T(8,128)(2,1)S(1)}, bf16[512,384]{1,0:T(8,128)(2,1)S(1)}, u32[]{:S(2)}, u32[]{:S(2)}) collective-permute-start(bf16[512,384]{1,0:T(8,128)(2,1)S(1)} %collective-permute-done.7.block), channel_id=1, source_target_pairs={{0,1},{1,0},{2,3},{3,2},{4,5},{5,4},{6,7},{7,6},{8,9},{9,8},{10,11... | collective-permute-start | bytes 1179656 | tf_op jit(solution)/shard_map/ppermute | solution.py:289
  30.1 4.8 %collective-permute-start.10 = (bf16[512,384]{1,0:T(8,128)(2,1)S(1)}, bf16[512,384]{1,0:T(8,128)(2,1)S(1)}, u32[]{:S(2)}, u32[]{:S(2)}) collective-permute-start(bf16[512,384]{1,0:T(8,128)(2,1)S(1)} %collective-permute-done.5.block), channel_id=1, source_target_pairs={{0,1},{1,0},{2,3},{3,2},{4,5},{5,4},{6,7},{7,6},{8,9},{9,8},{10,11... | collective-permute-start | bytes 1179656 | tf_op jit(solution)/shard_map/ppermute | solution.py:289
  30.1 8.4 %collective-permute-start.9 = (bf16[512,384]{1,0:T(8,128)(2,1)S(1)}, bf16[512,384]{1,0:T(8,128)(2,1)S(1)}, u32[]{:S(2)}, u32[]{:S(2)}) collective-permute-start(bf16[512,384]{1,0:T(8,128)(2,1)S(1)} %collective-permute-done.5.block), channel_id=1, source_target_pairs={{0,4},{4,8},{8,12},{12,14},{14,10},{10,6},{6,2},{2,0},{5,1},{9,5},... | collective-permute-start | bytes 1179656 | tf_op jit(solution)/shard_map/ppermute | solution.py:286
  34.3 4.2 %collective-permute-start.14 = (bf16[512,384]{1,0:T(8,128)(2,1)S(1)}, bf16[512,384]{1,0:T(8,128)(2,1)S(1)}, u32[]{:S(2)}, u32[]{:S(2)}) collective-permute-start(bf16[512,384]{1,0:T(8,128)(2,1)S(1)} %collective-permute-done.13.block), channel_id=1, source_target_pairs={{0,1},{1,0},{2,3},{3,2},{4,5},{5,4},{6,7},{7,6},{8,9},{9,8},{10,11... | collective-permute-start | bytes 1179656 | tf_op jit(solution)/shard_map/ppermute | solution.py:289
  38.5 1.7 %collective-permute-start.12 = (bf16[512,384]{1,0:T(8,128)(2,1)S(1)}, bf16[512,384]{1,0:T(8,128)(2,1)S(1)}, u32[]{:S(2)}, u32[]{:S(2)}) collective-permute-start(bf16[512,384]{1,0:T(8,128)(2,1)S(1)} %collective-permute-done.9.last), channel_id=1, source_target_pairs={{0,1},{1,0},{2,3},{3,2},{4,5},{5,4},{6,7},{7,6},{8,9},{9,8},{10,11... | collective-permute-start | bytes 1179656 | tf_op jit(solution)/shard_map/ppermute | solution.py:296

commit v5 on v4

--- a/solution.py
+++ b/solution.py
@@ -208,30 +208,36 @@
     )(own_w, other_w, block, other_block, *before)
 
 
-def last_kernel(last_w, last, own_sum, out_ref):
-    out_ref[...] = own_sum[...] + dot_columns(last_w[:, : last.shape[1]], last[...])
-
-
-def add_last(last_w, last, own_sum):
+def last_kernel(last_w, last_a, last_b, other_a, before, out_ref):
+    rows, columns = last_a.shape
+    own = last_w[:, :columns]
+    first = before[:, :rows] + dot_columns(own, last_a[...])
+    out_ref[:, :rows] = first + dot_columns(last_w[:, columns:], other_a[...])
+    out_ref[:, rows:] = before[:, rows:] + dot_columns(own, last_b[...])
+
+
+def add_last(last_w, last_a, last_b, other_a, before):
     vmem = pl.BlockSpec(memory_space=pltpu.VMEM)
     return pl.pallas_call(
         last_kernel,
-        in_specs=[vmem] * 3,
+        in_specs=[vmem] * 5,
         out_specs=vmem,
-        out_shape=jax.ShapeDtypeStruct(own_sum.shape, own_sum.dtype),
-        input_output_aliases={2: 0},
+        out_shape=jax.ShapeDtypeStruct(before.shape, before.dtype),
+        input_output_aliases={4: 0},
         compiler_params=pltpu.CompilerParams(vmem_limit_bytes=STEP_VMEM),
         cost_estimate=UNTIMED,
         name="add_last",
-    )(last_w, last, own_sum)
+    )(last_w, last_a, last_b, other_a, before)
 
 
 def finish_kernel(cuts, last_w, block, total, out_hbm, out, sems):
     columns = block.shape[1]
+    split = total.shape[1] - block.shape[0]
     copies = []
     for p, (begin, end) in enumerate(zip(cuts[:-1], cuts[1:])):
-        value = total[begin:end] + dot_columns(last_w[begin:end, columns:], block[...])
-        out[begin:end] = value.astype(out.dtype)
+        value = total[begin:end, split:] + dot_columns(last_w[begin:end, columns:], block[...])
+        out[begin:end, :split] = total[begin:end, :split].astype(out.dtype)
+        out[begin:end, split:] = value.astype(out.dtype)
         copies.append(pltpu.make_async_copy(out.at[begin:end], out_hbm.at[begin:end], sems.at[p]))
         copies[-1].start()
     for copy in copies:
@@ -283,21 +289,29 @@
             total = add_blocks(total, summed, own_w, other_w, blocks[summed], other_blocks[summed])
             summed += 1
             block, total = lax.optimization_barrier((block, total))
-        block = lax.ppermute(block, "ao", onward)
         if message < chips - 1:
+            block = lax.ppermute(block, "ao", onward)
             blocks.append(block)
-            other_blocks.append(lax.ppermute(block, "ao", across))
+            if message < chips - 2:
+                other_blocks.append(lax.ppermute(block, "ao", across))
+            else:
+                h = block.shape[0] // 2
+                other_blocks.append(jnp.concatenate([lax.ppermute(p, "ao", across) for p in (block[:h], block[h:])], 0))
         else:
-            last = block
+            half = block.shape[0] // 2
+            last_a = lax.ppermute(block[:half], "ao", onward)
+            last_b = lax.ppermute(block[half:], "ao", onward)
     while summed < len(blocks) - 1:
         total = add_blocks(total, summed, own_w, other_w, blocks[summed], other_blocks[summed])
         summed += 1
-    last, total = lax.optimization_barrier((last, total))
-    other_last = lax.ppermute(last, "ao", across)
+    last_a, total = lax.optimization_barrier((last_a, total))
+    other_a = lax.ppermute(last_a, "ao", across)
+    last_b, total = lax.optimization_barrier((last_b, total))
+    other_b = lax.ppermute(last_b, "ao", across)
     while summed < len(blocks):
         total = add_blocks(total, summed, own_w, other_w, blocks[summed], other_blocks[summed])
         summed += 1
-    return finish(last_w, other_last, add_last(last_w, last, total))
+    return finish(last_w, other_b, add_last(last_w, last_a, last_b, other_a, total))
 
 
 def solution(mesh):

time: 41.5 us -> 40.4 us (0.973)
  waiting for transfers between devices: 16.1 us -> 10.4 us
  starting transfers between devices: 13.6 us -> 18 us
    ppermute x7 -> x6, waiting for transfers between devices: 15.2 us -> 7.59 us  [on_device(): block = lax.ppermute(block, 'ao', onward)]
    ppermute x1 -> x6, starting transfers between devices: 0.01 us -> 4.27 us  [the longest x1 2.13 us: on_device(): last_a = lax.ppermute(block[:half], 'ao', onward)]
    ppermute x1 -> x6, waiting for transfers between devices: 0.81 us -> 2.78 us  [the longest x1 2.1 us: on_device(): last_b = lax.ppermute(block[half:], 'ao', onward)]
    ppermute x6 -> x5, starting transfers between devices: 0.02 us -> 0.52 us  [on_device(): other_blocks.append(lax.ppermute(block, 'ao', across))]
    ppermute x7 -> x6, starting transfers between devices: 13.1 us -> 12.6 us  [on_device(): block = lax.ppermute(block, 'ao', onward)]
  transfers between devices with their start and end apart: 15 -> 18, of which waited for: 8 -> 8; matrix products, arithmetic and copies ran while one was open for 0% -> 0% of each run, Pallas kernels for 17% -> 17%
where the time goes in v5:
time: 40.4 us; the launch traced here: 40.2 us
  starting transfers between devices  18 us (45%)
  Pallas kernels  11.6 us (29%)
  waiting for transfers between devices  10.4 us (26%)
    ppermute x6, starting transfers between devices, on_device(): block = lax.ppermute(block, 'ao', onward)  12.6 us
    ppermute x6, waiting for transfers between devices, on_device(): block = lax.ppermute(block, 'ao', onward)  7.59 us
    pallas_call x7, Pallas kernels, add_blocks(): pl.pallas_call(functools.partial(add_kernel, k), in_specs=[vmem] * (4 + l...  3.65 us
    pallas_call x1, Pallas kernels, half_transform(): pl.pallas_call(half_kernel, in_specs=[pl.BlockSpec(memory_space=pltpu.SME...  3.64 us
    pallas_call x1, Pallas kernels, windows(): pl.pallas_call(functools.partial(window_kernel, count, chips), in_specs=[...  2.8 us
    ppermute x1, starting transfers between devices, on_device(): last_a = lax.ppermute(block[:half], 'ao', onward)  2.13 us
    ppermute x1, waiting for transfers between devices, on_device(): last_b = lax.ppermute(block[half:], 'ao', onward)  2.1 us
    ppermute x1, starting transfers between devices, on_device(): last_b = lax.ppermute(block[half:], 'ao', onward)  1.58 us
  transfers between devices with their start and end apart: 18, of which 8 were waited for; matrix products, arithmetic and copies ran while one was open for 0% of the time, Pallas kernels for 17%

profile of v5, /device:TPU:0, one launch (start us, length us, event | category | flops | bytes accessed | tf_op | source)
XLA Modules:
  0.0 40.2 jit_solution(6862764912763727590)
XLA Ops:
  0.0 3.6 %half_transform.1.block = bf16[512,384]{1,0:T(8,128)(2,1)S(1)} custom-call(s32[1]{0:T(128)} %bitcast.me, s32[2,64]{1,0:T(2,128)} %bitcast.5, bf16[8,6144]{1,0:T(8,128)(2,1)} %bitcast.7, bf16[4,128,64,128]{3,2,1,0:T(8,128)(2,1)} %tiles_ref.1), custom_call_target="tpu_custom_call" | custom-call | flops 603979776 | bytes 8388608 | tf_op jit(solution)/shard_map/half_transform/pallas_call | solution.py:93
  3.7 0.5 %collective-permute-start.1 = (bf16[512,384]{1,0:T(8,128)(2,1)S(1)}, bf16[512,384]{1,0:T(8,128)(2,1)S(1)}, u32[]{:S(2)}, u32[]{:S(2)}) collective-permute-start(bf16[512,384]{1,0:T(8,128)(2,1)S(1)} %half_transform.1.block), channel_id=1, source_target_pairs={{0,1},{1,0},{2,3},{3,2},{4,5},{5,4},{6,7},{7,6},{8,9},{9,8},{10,11... | collective-permute-start | bytes 1179656 | tf_op jit(solution)/shard_map/ppermute | solution.py:275
  4.2 2.6 %collective-permute-start = (bf16[512,384]{1,0:T(8,128)(2,1)S(1)}, bf16[512,384]{1,0:T(8,128)(2,1)S(1)}, u32[]{:S(2)}, u32[]{:S(2)}) collective-permute-start(bf16[512,384]{1,0:T(8,128)(2,1)S(1)} %half_transform.1.block), channel_id=1, source_target_pairs={{0,4},{4,8},{8,12},{12,14},{14,10},{10,6},{6,2},{2,0},{5,1},{9,5},... | collective-permute-start | bytes 1179656 | tf_op jit(solution)/shard_map/ppermute | solution.py:293
  6.8 0.0 collective-permute-done.1.other_block
  6.8 1.7 %collective-permute-start.4 = (bf16[512,384]{1,0:T(8,128)(2,1)S(1)}, bf16[512,384]{1,0:T(8,128)(2,1)S(1)}, u32[]{:S(2)}, u32[]{:S(2)}) collective-permute-start(bf16[512,384]{1,0:T(8,128)(2,1)S(1)} %collective-permute-done.1.other_block), channel_id=1, source_target_pairs={{0,4},{4,8},{8,12},{12,14},{14,10},{10,6},{6,2},{2,0},{5,1},{9,5},... | collective-permute-start | bytes 1179656 | tf_op jit(solution)/shard_map/ppermute | solution.py:293
  8.5 0.0 copy-done.1
  8.5 2.8 %vir_windows.1 = (bf16[304,2688]{1,0:T(8,128)(2,1)S(1)}, bf16[304,2688]{1,0:T(8,128)(2,1)S(1)}, bf16[304,768]{1,0:T(8,128)(2,1)S(1)}) custom-call(s32[1]{0:T(128)} %bitcast.me, s32[2,64]{1,0:T(2,128)S(1)} %bitcast.6, bf16[304,6144]{1,0:T(8,128)(2,1)S(1)} %bitcast.4), custom_call_target="tpu_custom_call" | custom-call | tf_op jit(solution)/shard_map/vir_windows/pallas_call | solution.py:169
  11.3 1.2 %collective-permute-done.block = bf16[512,384]{1,0:T(8,128)(2,1)S(1)} collective-permute-done((bf16[512,384]{1,0:T(8,128)(2,1)S(1)}, bf16[512,384]{1,0:T(8,128)(2,1)S(1)}, u32[]{:S(2)}, u32[]{:S(2)}) %collective-permute-start) | collective-permute-done | bytes 393248 | tf_op jit(solution)/shard_map/ppermute | solution.py:293
  12.5 2.1 %collective-permute-start.2 = (bf16[512,384]{1,0:T(8,128)(2,1)S(1)}, bf16[512,384]{1,0:T(8,128)(2,1)S(1)}, u32[]{:S(2)}, u32[]{:S(2)}) collective-permute-start(bf16[512,384]{1,0:T(8,128)(2,1)S(1)} %collective-permute-done.block), channel_id=1, source_target_pairs={{0,4},{4,8},{8,12},{12,14},{14,10},{10,6},{6,2},{2,0},{5,1},{9,5},... | collective-permute-start | bytes 1179656 | tf_op jit(solution)/shard_map/ppermute | solution.py:293
  14.6 0.0 collective-permute-start.3
  14.6 0.5 %add_blocks.7.refs_0_ = f32[304,512]{1,0:T(8,128)S(1)} custom-call(bf16[304,2688]{1,0:T(8,128)(2,1)S(1)} %get-tuple-element.32.own_w, bf16[304,2688]{1,0:T(8,128)(2,1)S(1)} %get-tuple-element.33.other_w, bf16[512,384]{1,0:T(8,128)(2,1)S(1)} %half_transform.1.block, bf16[512,384]{1,0:T(8,128)(2,1)S(1)} %collective-permute-done.1.other_block), custom_call_target="tpu_custom_call" | custom-call | tf_op jit(solution)/shard_map/add_blocks/pallas_call | solution.py:199
  15.1 1.6 %collective-permute-done.4.block = bf16[512,384]{1,0:T(8,128)(2,1)S(1)} collective-permute-done((bf16[512,384]{1,0:T(8,128)(2,1)S(1)}, bf16[512,384]{1,0:T(8,128)(2,1)S(1)}, u32[]{:S(2)}, u32[]{:S(2)}) %collective-permute-start.4) | collective-permute-done | bytes 393248 | tf_op jit(solution)/shard_map/ppermute | solution.py:293
  16.7 0.0 collective-permute-start.8
  16.7 2.1 %collective-permute-start.7 = (bf16[512,384]{1,0:T(8,128)(2,1)S(1)}, bf16[512,384]{1,0:T(8,128)(2,1)S(1)}, u32[]{:S(2)}, u32[]{:S(2)}) collective-permute-start(bf16[512,384]{1,0:T(8,128)(2,1)S(1)} %collective-permute-done.4.block), channel_id=1, source_target_pairs={{0,4},{4,8},{8,12},{12,14},{14,10},{10,6},{6,2},{2,0},{5,1},{9,5},... | collective-permute-start | bytes 1179656 | tf_op jit(solution)/shard_map/ppermute | solution.py:293
  18.8 2.1 %collective-permute-done.2.block = bf16[512,384]{1,0:T(8,128)(2,1)S(1)} collective-permute-done((bf16[512,384]{1,0:T(8,128)(2,1)S(1)}, bf16[512,384]{1,0:T(8,128)(2,1)S(1)}, u32[]{:S(2)}, u32[]{:S(2)}) %collective-permute-start.2) | collective-permute-done | bytes 393248 | tf_op jit(solution)/shard_map/ppermute | solution.py:293
  20.9 0.0 collective-permute-start.6
  20.9 0.0 collective-permute-done.3.other_block
  20.9 0.5 %add_blocks.8.refs_0_ = f32[304,512]{1,0:T(8,128)S(1)} custom-call(bf16[304,2688]{1,0:T(8,128)(2,1)S(1)} %get-tuple-element.32.own_w, bf16[304,2688]{1,0:T(8,128)(2,1)S(1)} %get-tuple-element.33.other_w, bf16[512,384]{1,0:T(8,128)(2,1)S(1)} %collective-permute-done.block, ...), custom_call_target="tpu_custom_call", output_to_operand_aliasing={{}: (4, {})} | custom-call | tf_op jit(solution)/shard_map/add_blocks/pallas_call | solution.py:199
  21.5 2.1 %collective-permute-start.5 = (bf16[512,384]{1,0:T(8,128)(2,1)S(1)}, bf16[512,384]{1,0:T(8,128)(2,1)S(1)}, u32[]{:S(2)}, u32[]{:S(2)}) collective-permute-start(bf16[512,384]{1,0:T(8,128)(2,1)S(1)} %collective-permute-done.2.block), channel_id=1, source_target_pairs={{0,4},{4,8},{8,12},{12,14},{14,10},{10,6},{6,2},{2,0},{5,1},{9,5},... | collective-permute-start | bytes 1179656 | tf_op jit(solution)/shard_map/ppermute | solution.py:293
  23.6 0.0 collective-permute-done.8.other_block
  23.6 0.5 %add_blocks.9.refs_0_ = f32[304,512]{1,0:T(8,128)S(1)} custom-call(bf16[304,2688]{1,0:T(8,128)(2,1)S(1)} %get-tuple-element.32.own_w, bf16[304,2688]{1,0:T(8,128)(2,1)S(1)} %get-tuple-element.33.other_w, bf16[512,384]{1,0:T(8,128)(2,1)S(1)} %collective-permute-done.4.block, ...), custom_call_target="tpu_custom_call", output_to_operand_aliasing={{}: (4, {})} | custom-call | tf_op jit(solution)/shard_map/add_blocks/pallas_call | solution.py:199
  24.1 1.0 %collective-permute-done.7.block = bf16[512,384]{1,0:T(8,128)(2,1)S(1)} collective-permute-done((bf16[512,384]{1,0:T(8,128)(2,1)S(1)}, bf16[512,384]{1,0:T(8,128)(2,1)S(1)}, u32[]{:S(2)}, u32[]{:S(2)}) %collective-permute-start.7) | collective-permute-done | bytes 393248 | tf_op jit(solution)/shard_map/ppermute | solution.py:293
  25.1 2.1 %collective-permute-start.15 = (bf16[512,384]{1,0:T(8,128)(2,1)S(1)}, bf16[512,384]{1,0:T(8,128)(2,1)S(1)}, u32[]{:S(2)}, u32[]{:S(2)}) collective-permute-start(bf16[512,384]{1,0:T(8,128)(2,1)S(1)} %collective-permute-done.7.block), channel_id=1, source_target_pairs={{0,4},{4,8},{8,12},{12,14},{14,10},{10,6},{6,2},{2,0},{5,1},{9,5},... | collective-permute-start | bytes 1179656 | tf_op jit(solution)/shard_map/ppermute | solution.py:293
  27.2 0.0 collective-permute-done.6.other_block
  27.2 0.5 %add_blocks.10.refs_0_ = f32[304,512]{1,0:T(8,128)S(1)} custom-call(bf16[304,2688]{1,0:T(8,128)(2,1)S(1)} %get-tuple-element.32.own_w, bf16[304,2688]{1,0:T(8,128)(2,1)S(1)} %get-tuple-element.33.other_w, bf16[512,384]{1,0:T(8,128)(2,1)S(1)} %collective-permute-done.2.block, ...), custom_call_target="tpu_custom_call", output_to_operand_aliasing={{}: (4, {})} | custom-call | tf_op jit(solution)/shard_map/add_blocks/pallas_call | solution.py:199
  27.8 1.6 %collective-permute-done.5.block = bf16[512,384]{1,0:T(8,128)(2,1)S(1)} collective-permute-done((bf16[512,384]{1,0:T(8,128)(2,1)S(1)}, bf16[512,384]{1,0:T(8,128)(2,1)S(1)}, u32[]{:S(2)}, u32[]{:S(2)}) %collective-permute-start.5) | collective-permute-done | bytes 393248 | tf_op jit(solution)/shard_map/ppermute | solution.py:293
  29.4 0.0 collective-permute-start.12
  29.4 0.5 %collective-permute-start.11 = (bf16[512,384]{1,0:T(8,128)(2,1)S(1)}, bf16[512,384]{1,0:T(8,128)(2,1)S(1)}, u32[]{:S(2)}, u32[]{:S(2)}) collective-permute-start(bf16[512,384]{1,0:T(8,128)(2,1)S(1)} %collective-permute-done.5.block), channel_id=1, source_target_pairs={{0,1},{1,0},{2,3},{3,2},{4,5},{5,4},{6,7},{7,6},{8,9},{9,8},{10,11... | collective-permute-start | bytes 1179656 | tf_op jit(solution)/shard_map/ppermute | solution.py:296
  29.9 2.1 %collective-permute-start.10 = (bf16[256,384]{1,0:T(8,128)(2,1)S(1)}, bf16[256,384]{1,0:T(8,128)(2,1)S(1)}, u32[]{:S(2)}, u32[]{:S(2)}) collective-permute-start(bf16[256,384]{1,0:T(8,128)(2,1)S(1)} %get-tuple-element.49), channel_id=1, source_target_pairs={{0,4},{4,8},{8,12},{12,14},{14,10},{10,6},{6,2},{2,0},{5,1},{9,5},... | collective-permute-start | bytes 589832 | tf_op jit(solution)/shard_map/ppermute | solution.py:302
  32.0 1.6 %collective-permute-start.9 = (bf16[256,384]{1,0:T(8,128)(2,1)S(1)}, bf16[256,384]{1,0:T(8,128)(2,1)S(1)}, u32[]{:S(2)}, u32[]{:S(2)}) collective-permute-start(bf16[256,384]{1,0:T(8,128)(2,1)S(1)} %get-tuple-element.50), channel_id=1, source_target_pairs={{0,4},{4,8},{8,12},{12,14},{14,10},{10,6},{6,2},{2,0},{5,1},{9,5},... | collective-permute-start | bytes 589832 | tf_op jit(solution)/shard_map/ppermute | solution.py:303
  33.6 0.0 collective-permute-done.15.block
  33.7 0.1 collective-permute-start.16
  33.8 0.0 collective-permute-done.12.other_block
  33.8 0.5 %collective-permute-start.17 = (bf16[256,384]{1,0:T(8,128)(2,1)S(1)}, bf16[256,384]{1,0:T(8,128)(2,1)S(1)}, u32[]{:S(2)}, u32[]{:S(2)}) collective-permute-start(bf16[256,384]{1,0:T(8,128)(2,1)S(1)} %get-tuple-element.48), channel_id=1, source_target_pairs={{0,1},{1,0},{2,3},{3,2},{4,5},{5,4},{6,7},{7,6},{8,9},{9,8},{10,11... | collective-permute-start | bytes 589832 | tf_op jit(solution)/shard_map/ppermute | solution.py:299
  34.3 0.5 %add_blocks.11.refs_0_ = f32[304,512]{1,0:T(8,128)S(1)} custom-call(bf16[304,2688]{1,0:T(8,128)(2,1)S(1)} %get-tuple-element.32.own_w, bf16[304,2688]{1,0:T(8,128)(2,1)S(1)} %get-tuple-element.33.other_w, bf16[512,384]{1,0:T(8,128)(2,1)S(1)} %collective-permute-done.7.block, ...), custom_call_target="tpu_custom_call", output_to_operand_aliasing={{}: (4, {})} | custom-call | tf_op jit(solution)/shard_map/add_blocks/pallas_call | solution.py:199
  34.8 0.0 collective-permute-done.11.other_block
  34.8 0.5 %add_blocks.12.refs_0_ = f32[304,512]{1,0:T(8,128)S(1)} custom-call(bf16[304,2688]{1,0:T(8,128)(2,1)S(1)} %get-tuple-element.32.own_w, bf16[304,2688]{1,0:T(8,128)(2,1)S(1)} %get-tuple-element.33.other_w, bf16[512,384]{1,0:T(8,128)(2,1)S(1)} %collective-permute-done.5.block, ...), custom_call_target="tpu_custom_call", output_to_operand_aliasing={{}: (4, {})} | custom-call | tf_op jit(solution)/shard_map/add_blocks/pallas_call | solution.py:199
  35.3 0.4 collective-permute-done.10.last_a
  35.7 0.0 collective-permute-start.14
  35.7 2.1 %collective-permute-done.9.last_b = bf16[256,384]{1,0:T(8,128)(2,1)S(1)} collective-permute-done((bf16[256,384]{1,0:T(8,128)(2,1)S(1)}, bf16[256,384]{1,0:T(8,128)(2,1)S(1)}, u32[]{:S(2)}, u32[]{:S(2)}) %collective-permute-start.9) | collective-permute-done | bytes 196640 | tf_op jit(solution)/shard_map/ppermute | solution.py:303
  37.8 0.0 collective-permute-start.13
  37.8 0.0 collective-permute-done.16
  37.8 0.0 collective-permute-done.17
  37.9 0.5 %add_blocks.13.before = f32[304,512]{1,0:T(8,128)S(1)} custom-call(bf16[304,2688]{1,0:T(8,128)(2,1)S(1)} %get-tuple-element.32.own_w, bf16[304,2688]{1,0:T(8,128)(2,1)S(1)} %get-tuple-element.33.other_w, bf16[512,384]{1,0:T(8,128)(2,1)S(1)} %collective-permute-done.15.block, ...), custom_call_target="tpu_custom_call", output_to_operand_aliasing={{}: (4, {})} | custom-call | tf_op jit(solution)/shard_map/add_blocks/pallas_call | solution.py:199
  38.4 0.0 collective-permute-done.14.other_a
  38.4 0.5 %add_last.1.total = f32[304,512]{1,0:T(8,128)S(1)} custom-call(bf16[304,768]{1,0:T(8,128)(2,1)S(1)} %get-tuple-element.30.last_w, bf16[256,384]{1,0:T(8,128)(2,1)S(1)} %collective-permute-done.10.last_a, bf16[256,384]{1,0:T(8,128)(2,1)S(1)} %collective-permute-done.9.last_b, ...), custom_call_target="tpu_custom_call", output_to_operand_aliasing={{}: (4, {})} | custom-call | tf_op jit(solution)/shard_map/add_last/pallas_call | solution.py:221
  38.9 0.3 collective-permute-done.13.block
  39.2 1.0 %finish.1 = bf16[304,512]{1,0:T(8,128)(2,1)} custom-call(bf16[304,768]{1,0:T(8,128)(2,1)S(1)} %get-tuple-element.30.last_w, bf16[256,384]{1,0:T(8,128)(2,1)S(1)} %collective-permute-done.13.block, f32[304,512]{1,0:T(8,128)S(1)} %add_last.1.total), custom_call_target="tpu_custom_call" | custom-call | tf_op jit(solution)/shard_map/finish/pallas_call | solution.py:251
  (6 shorter events, 0.1 us)
Async XLA Ops:
  0.0 8.5 %copy-start = (bf16[6144,304]{0,1:T(8,128)(2,1)S(1)}, bf16[6144,304]{0,1:T(8,128)(2,1)}, u32[]{:S(2)}) copy-start(bf16[6144,304]{0,1:T(8,128)(2,1)} %param.7) | copy-start | bytes 11206660
  0.0 8.5 %copy-start.1 = (s32[64,2]{0,1:T(2,128)S(1)}, s32[64,2]{0,1:T(2,128)}, u32[]{:S(2)}) copy-start(s32[64,2]{0,1:T(2,128)} %param.5) | copy-start | bytes 1540
  3.7 3.2 %collective-permute-start.1 = (bf16[512,384]{1,0:T(8,128)(2,1)S(1)}, bf16[512,384]{1,0:T(8,128)(2,1)S(1)}, u32[]{:S(2)}, u32[]{:S(2)}) collective-permute-start(bf16[512,384]{1,0:T(8,128)(2,1)S(1)} %half_transform.1.block), channel_id=1, source_target_pairs={{0,1},{1,0},{2,3},{3,2},{4,5},{5,4},{6,7},{7,6},{8,9},{9,8},{10,11... | collective-permute-start | bytes 1179656 | tf_op jit(solution)/shard_map/ppermute | solution.py:275
  4.2 8.3 %collective-permute-start = (bf16[512,384]{1,0:T(8,128)(2,1)S(1)}, bf16[512,384]{1,0:T(8,128)(2,1)S(1)}, u32[]{:S(2)}, u32[]{:S(2)}) collective-permute-start(bf16[512,384]{1,0:T(8,128)(2,1)S(1)} %half_transform.1.block), channel_id=1, source_target_pairs={{0,4},{4,8},{8,12},{12,14},{14,10},{10,6},{6,2},{2,0},{5,1},{9,5},... | collective-permute-start | bytes 1179656 | tf_op jit(solution)/shard_map/ppermute | solution.py:293
  6.8 9.9 %collective-permute-start.4 = (bf16[512,384]{1,0:T(8,128)(2,1)S(1)}, bf16[512,384]{1,0:T(8,128)(2,1)S(1)}, u32[]{:S(2)}, u32[]{:S(2)}) collective-permute-start(bf16[512,384]{1,0:T(8,128)(2,1)S(1)} %collective-permute-done.1.other_block), channel_id=1, source_target_pairs={{0,4},{4,8},{8,12},{12,14},{14,10},{10,6},{6,2},{2,0},{5,1},{9,5},... | collective-permute-start | bytes 1179656 | tf_op jit(solution)/shard_map/ppermute | solution.py:293
  12.5 8.4 %collective-permute-start.2 = (bf16[512,384]{1,0:T(8,128)(2,1)S(1)}, bf16[512,384]{1,0:T(8,128)(2,1)S(1)}, u32[]{:S(2)}, u32[]{:S(2)}) collective-permute-start(bf16[512,384]{1,0:T(8,128)(2,1)S(1)} %collective-permute-done.block), channel_id=1, source_target_pairs={{0,4},{4,8},{8,12},{12,14},{14,10},{10,6},{6,2},{2,0},{5,1},{9,5},... | collective-permute-start | bytes 1179656 | tf_op jit(solution)/shard_map/ppermute | solution.py:293
  14.6 6.4 %collective-permute-start.3 = (bf16[512,384]{1,0:T(8,128)(2,1)S(1)}, bf16[512,384]{1,0:T(8,128)(2,1)S(1)}, u32[]{:S(2)}, u32[]{:S(2)}) collective-permute-start(bf16[512,384]{1,0:T(8,128)(2,1)S(1)} %collective-permute-done.block), channel_id=1, source_target_pairs={{0,1},{1,0},{2,3},{3,2},{4,5},{5,4},{6,7},{7,6},{8,9},{9,8},{10,11... | collective-permute-start | bytes 1179656 | tf_op jit(solution)/shard_map/ppermute | solution.py:296
  16.7 6.9 %collective-permute-start.8 = (bf16[512,384]{1,0:T(8,128)(2,1)S(1)}, bf16[512,384]{1,0:T(8,128)(2,1)S(1)}, u32[]{:S(2)}, u32[]{:S(2)}) collective-permute-start(bf16[512,384]{1,0:T(8,128)(2,1)S(1)} %collective-permute-done.4.block), channel_id=1, source_target_pairs={{0,1},{1,0},{2,3},{3,2},{4,5},{5,4},{6,7},{7,6},{8,9},{9,8},{10,11... | collective-permute-start | bytes 1179656 | tf_op jit(solution)/shard_map/ppermute | solution.py:296
  16.7 8.4 %collective-permute-start.7 = (bf16[512,384]{1,0:T(8,128)(2,1)S(1)}, bf16[512,384]{1,0:T(8,128)(2,1)S(1)}, u32[]{:S(2)}, u32[]{:S(2)}) collective-permute-start(bf16[512,384]{1,0:T(8,128)(2,1)S(1)} %collective-permute-done.4.block), channel_id=1, source_target_pairs={{0,4},{4,8},{8,12},{12,14},{14,10},{10,6},{6,2},{2,0},{5,1},{9,5},... | collective-permute-start | bytes 1179656 | tf_op jit(solution)/shard_map/ppermute | solution.py:293
  20.9 6.3 %collective-permute-start.6 = (bf16[512,384]{1,0:T(8,128)(2,1)S(1)}, bf16[512,384]{1,0:T(8,128)(2,1)S(1)}, u32[]{:S(2)}, u32[]{:S(2)}) collective-permute-start(bf16[512,384]{1,0:T(8,128)(2,1)S(1)} %collective-permute-done.2.block), channel_id=1, source_target_pairs={{0,1},{1,0},{2,3},{3,2},{4,5},{5,4},{6,7},{7,6},{8,9},{9,8},{10,11... | collective-permute-start | bytes 1179656 | tf_op jit(solution)/shard_map/ppermute | solution.py:296
  21.5 7.9 %collective-permute-start.5 = (bf16[512,384]{1,0:T(8,128)(2,1)S(1)}, bf16[512,384]{1,0:T(8,128)(2,1)S(1)}, u32[]{:S(2)}, u32[]{:S(2)}) collective-permute-start(bf16[512,384]{1,0:T(8,128)(2,1)S(1)} %collective-permute-done.2.block), channel_id=1, source_target_pairs={{0,4},{4,8},{8,12},{12,14},{14,10},{10,6},{6,2},{2,0},{5,1},{9,5},... | collective-permute-start | bytes 1179656 | tf_op jit(solution)/shard_map/ppermute | solution.py:293
  25.1 8.5 %collective-permute-start.15 = (bf16[512,384]{1,0:T(8,128)(2,1)S(1)}, bf16[512,384]{1,0:T(8,128)(2,1)S(1)}, u32[]{:S(2)}, u32[]{:S(2)}) collective-permute-start(bf16[512,384]{1,0:T(8,128)(2,1)S(1)} %collective-permute-done.7.block), channel_id=1, source_target_pairs={{0,4},{4,8},{8,12},{12,14},{14,10},{10,6},{6,2},{2,0},{5,1},{9,5},... | collective-permute-start | bytes 1179656 | tf_op jit(solution)/shard_map/ppermute | solution.py:293
  29.4 4.4 %collective-permute-start.12 = (bf16[512,384]{1,0:T(8,128)(2,1)S(1)}, bf16[512,384]{1,0:T(8,128)(2,1)S(1)}, u32[]{:S(2)}, u32[]{:S(2)}) collective-permute-start(bf16[512,384]{1,0:T(8,128)(2,1)S(1)} %collective-permute-done.7.block), channel_id=1, source_target_pairs={{0,1},{1,0},{2,3},{3,2},{4,5},{5,4},{6,7},{7,6},{8,9},{9,8},{10,11... | collective-permute-start | bytes 1179656 | tf_op jit(solution)/shard_map/ppermute | solution.py:296
  29.4 5.4 %collective-permute-start.11 = (bf16[512,384]{1,0:T(8,128)(2,1)S(1)}, bf16[512,384]{1,0:T(8,128)(2,1)S(1)}, u32[]{:S(2)}, u32[]{:S(2)}) collective-permute-start(bf16[512,384]{1,0:T(8,128)(2,1)S(1)} %collective-permute-done.5.block), channel_id=1, source_target_pairs={{0,1},{1,0},{2,3},{3,2},{4,5},{5,4},{6,7},{7,6},{8,9},{9,8},{10,11... | collective-permute-start | bytes 1179656 | tf_op jit(solution)/shard_map/ppermute | solution.py:296
  29.9 5.8 %collective-permute-start.10 = (bf16[256,384]{1,0:T(8,128)(2,1)S(1)}, bf16[256,384]{1,0:T(8,128)(2,1)S(1)}, u32[]{:S(2)}, u32[]{:S(2)}) collective-permute-start(bf16[256,384]{1,0:T(8,128)(2,1)S(1)} %get-tuple-element.49), channel_id=1, source_target_pairs={{0,4},{4,8},{8,12},{12,14},{14,10},{10,6},{6,2},{2,0},{5,1},{9,5},... | collective-permute-start | bytes 589832 | tf_op jit(solution)/shard_map/ppermute | solution.py:302
  32.0 5.7 %collective-permute-start.9 = (bf16[256,384]{1,0:T(8,128)(2,1)S(1)}, bf16[256,384]{1,0:T(8,128)(2,1)S(1)}, u32[]{:S(2)}, u32[]{:S(2)}) collective-permute-start(bf16[256,384]{1,0:T(8,128)(2,1)S(1)} %get-tuple-element.50), channel_id=1, source_target_pairs={{0,4},{4,8},{8,12},{12,14},{14,10},{10,6},{6,2},{2,0},{5,1},{9,5},... | collective-permute-start | bytes 589832 | tf_op jit(solution)/shard_map/ppermute | solution.py:303
  33.7 4.1 %collective-permute-start.16 = (bf16[256,384]{1,0:T(8,128)(2,1)S(1)}, bf16[256,384]{1,0:T(8,128)(2,1)S(1)}, u32[]{:S(2)}, u32[]{:S(2)}) collective-permute-start(bf16[256,384]{1,0:T(8,128)(2,1)S(1)} %get-tuple-element.47), channel_id=1, source_target_pairs={{0,1},{1,0},{2,3},{3,2},{4,5},{5,4},{6,7},{7,6},{8,9},{9,8},{10,11... | collective-permute-start | bytes 589832 | tf_op jit(solution)/shard_map/ppermute | solution.py:299
  33.8 4.0 %collective-permute-start.17 = (bf16[256,384]{1,0:T(8,128)(2,1)S(1)}, bf16[256,384]{1,0:T(8,128)(2,1)S(1)}, u32[]{:S(2)}, u32[]{:S(2)}) collective-permute-start(bf16[256,384]{1,0:T(8,128)(2,1)S(1)} %get-tuple-element.48), channel_id=1, source_target_pairs={{0,1},{1,0},{2,3},{3,2},{4,5},{5,4},{6,7},{7,6},{8,9},{9,8},{10,11... | collective-permute-start | bytes 589832 | tf_op jit(solution)/shard_map/ppermute | solution.py:299
  35.7 2.7 %collective-permute-start.14 = (bf16[256,384]{1,0:T(8,128)(2,1)S(1)}, bf16[256,384]{1,0:T(8,128)(2,1)S(1)}, u32[]{:S(2)}, u32[]{:S(2)}) collective-permute-start(bf16[256,384]{1,0:T(8,128)(2,1)S(1)} %collective-permute-done.10.last_a), channel_id=1, source_target_pairs={{0,1},{1,0},{2,3},{3,2},{4,5},{5,4},{6,7},{7,6},{8,9},{9,8},{10,11... | collective-permute-start | bytes 589832 | tf_op jit(solution)/shard_map/ppermute | solution.py:308
  37.8 1.4 %collective-permute-start.13 = (bf16[256,384]{1,0:T(8,128)(2,1)S(1)}, bf16[256,384]{1,0:T(8,128)(2,1)S(1)}, u32[]{:S(2)}, u32[]{:S(2)}) collective-permute-start(bf16[256,384]{1,0:T(8,128)(2,1)S(1)} %collective-permute-done.9.last_b), channel_id=1, source_target_pairs={{0,1},{1,0},{2,3},{3,2},{4,5},{5,4},{6,7},{7,6},{8,9},{9,8},{10,11... | collective-permute-start | bytes 589832 | tf_op jit(solution)/shard_map/ppermute | solution.py:310

commit v6 on v5

--- a/solution.py
+++ b/solution.py
@@ -32,15 +32,17 @@
     count, ri_width = tiles_ref.shape[0], tiles_ref.shape[2]
     occ_batch = occ_hbm.shape[0]
     width = AO_GROUP * QB
-    pairs_copy = pltpu.make_async_copy(pairs_hbm, pairs, sems.at[count])
-    occ_copy = pltpu.make_async_copy(occ_hbm, occ, sems.at[count + 1])
+    pairs_copy = pltpu.make_async_copy(pairs_hbm, pairs, sems.at[count + 1])
+    occ_copy = pltpu.make_async_copy(occ_hbm, occ, sems.at[count + 2])
     pairs_copy.start()
     occ_copy.start()
-    copies = [
-        pltpu.make_async_copy(tiles_ref.at[t, pl.ds(0, AO_GROUP)], held_tiles.at[t], sems.at[t]) for t in range(count)
-    ]
-    for copy in copies:
-        copy.start()
+    parts = [(t, 0, AO_GROUP) for t in range(count - 1)]
+    parts += [(count - 1, 0, AO_GROUP // 2), (count - 1, AO_GROUP // 2, AO_GROUP // 2)]
+    copies = []
+    for n, (t, r, size) in enumerate(parts):
+        source, target = tiles_ref.at[t, pl.ds(r, size)], held_tiles.at[t, pl.ds(r, size)]
+        copies.append(pltpu.make_async_copy(source, target, sems.at[n]))
+        copies[-1].start()
     row = lax.broadcasted_iota(jnp.int32, (LANES, width), 0)
     lane = lax.broadcasted_iota(jnp.int32, (LANES, width), 1)
     spread = jnp.where(jnp.right_shift(lane, QB.bit_length() - 1) == row, 1.0, 0.0).astype(jnp.bfloat16)
@@ -57,15 +59,22 @@
         for i in range(occ_batch):
             rows = jnp.broadcast_to(wide[t * occ_batch + i : t * occ_batch + i + 1], (QB, width))
             kron[t, i * QB : (i + 1) * QB, :] = jnp.where(diagonal, rows, 0.0).astype(jnp.bfloat16)
-    for t in range(count):
-        copies[t].wait()
+    rows = occ_batch * ri_width
+    for copy, (t, r, size) in zip(copies, parts):
+        copy.wait()
         for b in range(0, ri_width // QB, PAIR):
-            parts = [held_tiles[t, :, (b + k) * QB : (b + k + 1) * QB, :].reshape(width, LANES) for k in range(PAIR)]
-            half = jnp.dot(kron[t], jnp.concatenate(parts, 1), preferred_element_type=jnp.float32)
+            sides = [
+                held_tiles[t, r : r + size, (b + k) * QB : (b + k + 1) * QB, :].reshape(size * QB, LANES)
+                for k in range(PAIR)
+            ]
+            factor = kron[t, :, r * QB : (r + size) * QB]
+            half = jnp.dot(factor, jnp.concatenate(sides, 1), preferred_element_type=jnp.float32)
             for k in range(PAIR):
                 part = half[:, k * LANES : (k + 1) * LANES].reshape(occ_batch, QB, LANES)
-                held[t, :, (b + k) * QB : (b + k + 1) * QB, :] = part
-    rows = occ_batch * ri_width
+                at = slice((b + k) * QB, (b + k + 1) * QB)
+                if r > 0:
+                    part = part + held[t, :, at, :]
+                held[t, :, at, :] = part
     lane = lax.broadcasted_iota(jnp.int32, (rows, LANES), 1)
     pieces = []
     for s in range(count):
@@ -101,7 +110,7 @@
             pltpu.VMEM((count, AO_GROUP, ri_width, LANES), jnp.bfloat16),
             pltpu.VMEM((count, occ_batch * QB, width), jnp.bfloat16),
             pltpu.VMEM((count, occ_batch, ri_width, LANES), jnp.float32),
-            pltpu.SemaphoreType.DMA((count + 2,)),
+            pltpu.SemaphoreType.DMA((count + 3,)),
         ],
         compiler_params=pltpu.CompilerParams(vmem_limit_bytes=HALF_VMEM),
         cost_estimate=pl.CostEstimate(
@@ -208,56 +217,56 @@
     )(own_w, other_w, block, other_block, *before)
 
 
-def last_kernel(last_w, last_a, last_b, other_a, before, out_ref):
+def last_kernel(last_w, last_a, last_b, other_a, before, done_ref, rest_ref):
     rows, columns = last_a.shape
     own = last_w[:, :columns]
     first = before[:, :rows] + dot_columns(own, last_a[...])
-    out_ref[:, :rows] = first + dot_columns(last_w[:, columns:], other_a[...])
-    out_ref[:, rows:] = before[:, rows:] + dot_columns(own, last_b[...])
+    done_ref[...] = (first + dot_columns(last_w[:, columns:], other_a[...])).astype(done_ref.dtype)
+    rest_ref[...] = before[:, rows:] + dot_columns(own, last_b[...])
 
 
 def add_last(last_w, last_a, last_b, other_a, before):
     vmem = pl.BlockSpec(memory_space=pltpu.VMEM)
+    rows = before.shape[0]
     return pl.pallas_call(
         last_kernel,
         in_specs=[vmem] * 5,
-        out_specs=vmem,
-        out_shape=jax.ShapeDtypeStruct(before.shape, before.dtype),
-        input_output_aliases={4: 0},
+        out_specs=[vmem] * 2,
+        out_shape=[
+            jax.ShapeDtypeStruct((rows, last_a.shape[0]), jnp.bfloat16),
+            jax.ShapeDtypeStruct((rows, last_b.shape[0]), before.dtype),
+        ],
         compiler_params=pltpu.CompilerParams(vmem_limit_bytes=STEP_VMEM),
         cost_estimate=UNTIMED,
         name="add_last",
     )(last_w, last_a, last_b, other_a, before)
 
 
-def finish_kernel(cuts, last_w, block, total, out_hbm, out, sems):
+def finish_kernel(last_w, block, done, rest, out_hbm, out, sems):
     columns = block.shape[1]
-    split = total.shape[1] - block.shape[0]
-    copies = []
-    for p, (begin, end) in enumerate(zip(cuts[:-1], cuts[1:])):
-        value = total[begin:end, split:] + dot_columns(last_w[begin:end, columns:], block[...])
-        out[begin:end, :split] = total[begin:end, :split].astype(out.dtype)
-        out[begin:end, split:] = value.astype(out.dtype)
-        copies.append(pltpu.make_async_copy(out.at[begin:end], out_hbm.at[begin:end], sems.at[p]))
-        copies[-1].start()
-    for copy in copies:
-        copy.wait()
-
-
-def finish(last_w, block, total):
-    rows = total.shape[0]
-    cuts = [0, rows // 32 * 16, rows] if rows % 16 == 0 else [0, rows]
+    split = done.shape[1]
+    first = pltpu.make_async_copy(done, out_hbm.at[:, :split], sems.at[0])
+    first.start()
+    value = rest[...] + dot_columns(last_w[:, columns:], block[...])
+    out[...] = value.astype(out.dtype)
+    second = pltpu.make_async_copy(out, out_hbm.at[:, split:], sems.at[1])
+    second.start()
+    first.wait()
+    second.wait()
+
+
+def finish(last_w, block, done, rest):
     vmem = pl.BlockSpec(memory_space=pltpu.VMEM)
     return pl.pallas_call(
-        functools.partial(finish_kernel, cuts),
-        in_specs=[vmem] * 3,
+        finish_kernel,
+        in_specs=[vmem] * 4,
         out_specs=pl.BlockSpec(memory_space=pl.ANY),
-        out_shape=jax.ShapeDtypeStruct(total.shape, jnp.bfloat16),
-        scratch_shapes=[pltpu.VMEM(total.shape, jnp.bfloat16), pltpu.SemaphoreType.DMA((len(cuts) - 1,))],
+        out_shape=jax.ShapeDtypeStruct((rest.shape[0], done.shape[1] + rest.shape[1]), jnp.bfloat16),
+        scratch_shapes=[pltpu.VMEM(rest.shape, jnp.bfloat16), pltpu.SemaphoreType.DMA((2,))],
         compiler_params=pltpu.CompilerParams(vmem_limit_bytes=STEP_VMEM),
         cost_estimate=UNTIMED,
         name="finish",
-    )(last_w, block, total)
+    )(last_w, block, done, rest)
 
 
 def on_device(chips, tiles, pairs, occ_coef, vir_coef):
@@ -311,7 +320,7 @@
     while summed < len(blocks):
         total = add_blocks(total, summed, own_w, other_w, blocks[summed], other_blocks[summed])
         summed += 1
-    return finish(last_w, other_b, add_last(last_w, last_a, last_b, other_a, total))
+    return finish(last_w, other_b, *add_last(last_w, last_a, last_b, other_a, total))
 
 
 def solution(mesh):

time: 40.4 us -> 40.3 us (level)
  no operation moved by 1% of the time
where the time goes in v6:
time: 40.3 us; the launch traced here: 40.2 us
  starting transfers between devices  18 us (45%)
  Pallas kernels  11.4 us (28%)
  waiting for transfers between devices  10.5 us (26%)
    ppermute x6, starting transfers between devices, on_device(): block = lax.ppermute(block, 'ao', onward)  12.7 us
    ppermute x6, waiting for transfers between devices, on_device(): block = lax.ppermute(block, 'ao', onward)  7.58 us
    pallas_call x7, Pallas kernels, add_blocks(): pl.pallas_call(functools.partial(add_kernel, k), in_specs=[vmem] * (4 + l...  3.66 us
    pallas_call x1, Pallas kernels, half_transform(): pl.pallas_call(half_kernel, in_specs=[pl.BlockSpec(memory_space=pltpu.SME...  3.62 us
    pallas_call x1, Pallas kernels, windows(): pl.pallas_call(functools.partial(window_kernel, count, chips), in_specs=[...  2.8 us
    ppermute x1, starting transfers between devices, on_device(): last_a = lax.ppermute(block[:half], 'ao', onward)  2.13 us
    ppermute x1, waiting for transfers between devices, on_device(): last_b = lax.ppermute(block[half:], 'ao', onward)  2.1 us
    ppermute x1, starting transfers between devices, on_device(): last_b = lax.ppermute(block[half:], 'ao', onward)  1.57 us
  transfers between devices with their start and end apart: 18, of which 8 were waited for; matrix products, arithmetic and copies ran while one was open for 0% of the time, Pallas kernels for 17%

profile of v6, /device:TPU:0, one launch (start us, length us, event | category | flops | bytes accessed | tf_op | source)
XLA Modules:
  0.0 40.2 jit_solution(15301019459989598432)
XLA Ops:
  0.0 3.6 %half_transform.1.block = bf16[512,384]{1,0:T(8,128)(2,1)S(1)} custom-call(s32[1]{0:T(128)} %bitcast.me, s32[2,64]{1,0:T(2,128)} %bitcast.5, bf16[8,6144]{1,0:T(8,128)(2,1)} %bitcast.7, bf16[4,128,64,128]{3,2,1,0:T(8,128)(2,1)} %tiles_ref.1), custom_call_target="tpu_custom_call" | custom-call | flops 603979776 | bytes 8388608 | tf_op jit(solution)/shard_map/half_transform/pallas_call | solution.py:102
  3.6 0.5 %collective-permute-start.1 = (bf16[512,384]{1,0:T(8,128)(2,1)S(1)}, bf16[512,384]{1,0:T(8,128)(2,1)S(1)}, u32[]{:S(2)}, u32[]{:S(2)}) collective-permute-start(bf16[512,384]{1,0:T(8,128)(2,1)S(1)} %half_transform.1.block), channel_id=1, source_target_pairs={{0,1},{1,0},{2,3},{3,2},{4,5},{5,4},{6,7},{7,6},{8,9},{9,8},{10,11... | collective-permute-start | bytes 1179656 | tf_op jit(solution)/shard_map/ppermute | solution.py:284
  4.1 2.6 %collective-permute-start = (bf16[512,384]{1,0:T(8,128)(2,1)S(1)}, bf16[512,384]{1,0:T(8,128)(2,1)S(1)}, u32[]{:S(2)}, u32[]{:S(2)}) collective-permute-start(bf16[512,384]{1,0:T(8,128)(2,1)S(1)} %half_transform.1.block), channel_id=1, source_target_pairs={{0,4},{4,8},{8,12},{12,14},{14,10},{10,6},{6,2},{2,0},{5,1},{9,5},... | collective-permute-start | bytes 1179656 | tf_op jit(solution)/shard_map/ppermute | solution.py:302
  6.8 0.0 collective-permute-done.1.other_block
  6.8 1.7 %collective-permute-start.4 = (bf16[512,384]{1,0:T(8,128)(2,1)S(1)}, bf16[512,384]{1,0:T(8,128)(2,1)S(1)}, u32[]{:S(2)}, u32[]{:S(2)}) collective-permute-start(bf16[512,384]{1,0:T(8,128)(2,1)S(1)} %collective-permute-done.1.other_block), channel_id=1, source_target_pairs={{0,4},{4,8},{8,12},{12,14},{14,10},{10,6},{6,2},{2,0},{5,1},{9,5},... | collective-permute-start | bytes 1179656 | tf_op jit(solution)/shard_map/ppermute | solution.py:302
  8.4 0.0 copy-done
  8.4 2.8 %vir_windows.1 = (bf16[304,2688]{1,0:T(8,128)(2,1)S(1)}, bf16[304,2688]{1,0:T(8,128)(2,1)S(1)}, bf16[304,768]{1,0:T(8,128)(2,1)S(1)}) custom-call(s32[1]{0:T(128)} %bitcast.me, s32[2,64]{1,0:T(2,128)S(1)} %bitcast.6, bf16[304,6144]{1,0:T(8,128)(2,1)S(1)} %bitcast.4), custom_call_target="tpu_custom_call" | custom-call | tf_op jit(solution)/shard_map/vir_windows/pallas_call | solution.py:178
  11.3 1.2 %collective-permute-done.block = bf16[512,384]{1,0:T(8,128)(2,1)S(1)} collective-permute-done((bf16[512,384]{1,0:T(8,128)(2,1)S(1)}, bf16[512,384]{1,0:T(8,128)(2,1)S(1)}, u32[]{:S(2)}, u32[]{:S(2)}) %collective-permute-start) | collective-permute-done | bytes 393248 | tf_op jit(solution)/shard_map/ppermute | solution.py:302
  12.5 2.1 %collective-permute-start.2 = (bf16[512,384]{1,0:T(8,128)(2,1)S(1)}, bf16[512,384]{1,0:T(8,128)(2,1)S(1)}, u32[]{:S(2)}, u32[]{:S(2)}) collective-permute-start(bf16[512,384]{1,0:T(8,128)(2,1)S(1)} %collective-permute-done.block), channel_id=1, source_target_pairs={{0,4},{4,8},{8,12},{12,14},{14,10},{10,6},{6,2},{2,0},{5,1},{9,5},... | collective-permute-start | bytes 1179656 | tf_op jit(solution)/shard_map/ppermute | solution.py:302
  14.6 0.0 collective-permute-start.3
  14.6 0.5 %add_blocks.7.refs_0_ = f32[304,512]{1,0:T(8,128)S(1)} custom-call(bf16[304,2688]{1,0:T(8,128)(2,1)S(1)} %get-tuple-element.34.own_w, bf16[304,2688]{1,0:T(8,128)(2,1)S(1)} %get-tuple-element.35.other_w, bf16[512,384]{1,0:T(8,128)(2,1)S(1)} %half_transform.1.block, bf16[512,384]{1,0:T(8,128)(2,1)S(1)} %collective-permute-done.1.other_block), custom_call_target="tpu_custom_call" | custom-call | tf_op jit(solution)/shard_map/add_blocks/pallas_call | solution.py:208
  15.1 1.6 %collective-permute-done.4.block = bf16[512,384]{1,0:T(8,128)(2,1)S(1)} collective-permute-done((bf16[512,384]{1,0:T(8,128)(2,1)S(1)}, bf16[512,384]{1,0:T(8,128)(2,1)S(1)}, u32[]{:S(2)}, u32[]{:S(2)}) %collective-permute-start.4) | collective-permute-done | bytes 393248 | tf_op jit(solution)/shard_map/ppermute | solution.py:302
  16.7 0.0 collective-permute-start.8
  16.7 2.1 %collective-permute-start.7 = (bf16[512,384]{1,0:T(8,128)(2,1)S(1)}, bf16[512,384]{1,0:T(8,128)(2,1)S(1)}, u32[]{:S(2)}, u32[]{:S(2)}) collective-permute-start(bf16[512,384]{1,0:T(8,128)(2,1)S(1)} %collective-permute-done.4.block), channel_id=1, source_target_pairs={{0,4},{4,8},{8,12},{12,14},{14,10},{10,6},{6,2},{2,0},{5,1},{9,5},... | collective-permute-start | bytes 1179656 | tf_op jit(solution)/shard_map/ppermute | solution.py:302
  18.8 2.1 %collective-permute-done.2.block = bf16[512,384]{1,0:T(8,128)(2,1)S(1)} collective-permute-done((bf16[512,384]{1,0:T(8,128)(2,1)S(1)}, bf16[512,384]{1,0:T(8,128)(2,1)S(1)}, u32[]{:S(2)}, u32[]{:S(2)}) %collective-permute-start.2) | collective-permute-done | bytes 393248 | tf_op jit(solution)/shard_map/ppermute | solution.py:302
  20.9 0.0 collective-permute-start.6
  20.9 0.0 collective-permute-done.3.other_block
  20.9 0.5 %add_blocks.8.refs_0_ = f32[304,512]{1,0:T(8,128)S(1)} custom-call(bf16[304,2688]{1,0:T(8,128)(2,1)S(1)} %get-tuple-element.34.own_w, bf16[304,2688]{1,0:T(8,128)(2,1)S(1)} %get-tuple-element.35.other_w, bf16[512,384]{1,0:T(8,128)(2,1)S(1)} %collective-permute-done.block, ...), custom_call_target="tpu_custom_call", output_to_operand_aliasing={{}: (4, {})} | custom-call | tf_op jit(solution)/shard_map/add_blocks/pallas_call | solution.py:208
  21.4 2.1 %collective-permute-start.5 = (bf16[512,384]{1,0:T(8,128)(2,1)S(1)}, bf16[512,384]{1,0:T(8,128)(2,1)S(1)}, u32[]{:S(2)}, u32[]{:S(2)}) collective-permute-start(bf16[512,384]{1,0:T(8,128)(2,1)S(1)} %collective-permute-done.2.block), channel_id=1, source_target_pairs={{0,4},{4,8},{8,12},{12,14},{14,10},{10,6},{6,2},{2,0},{5,1},{9,5},... | collective-permute-start | bytes 1179656 | tf_op jit(solution)/shard_map/ppermute | solution.py:302
  23.6 0.0 collective-permute-done.8.other_block
  23.6 0.5 %add_blocks.9.refs_0_ = f32[304,512]{1,0:T(8,128)S(1)} custom-call(bf16[304,2688]{1,0:T(8,128)(2,1)S(1)} %get-tuple-element.34.own_w, bf16[304,2688]{1,0:T(8,128)(2,1)S(1)} %get-tuple-element.35.other_w, bf16[512,384]{1,0:T(8,128)(2,1)S(1)} %collective-permute-done.4.block, ...), custom_call_target="tpu_custom_call", output_to_operand_aliasing={{}: (4, {})} | custom-call | tf_op jit(solution)/shard_map/add_blocks/pallas_call | solution.py:208
  24.1 1.0 %collective-permute-done.7.block = bf16[512,384]{1,0:T(8,128)(2,1)S(1)} collective-permute-done((bf16[512,384]{1,0:T(8,128)(2,1)S(1)}, bf16[512,384]{1,0:T(8,128)(2,1)S(1)}, u32[]{:S(2)}, u32[]{:S(2)}) %collective-permute-start.7) | collective-permute-done | bytes 393248 | tf_op jit(solution)/shard_map/ppermute | solution.py:302
  25.1 2.1 %collective-permute-start.15 = (bf16[512,384]{1,0:T(8,128)(2,1)S(1)}, bf16[512,384]{1,0:T(8,128)(2,1)S(1)}, u32[]{:S(2)}, u32[]{:S(2)}) collective-permute-start(bf16[512,384]{1,0:T(8,128)(2,1)S(1)} %collective-permute-done.7.block), channel_id=1, source_target_pairs={{0,4},{4,8},{8,12},{12,14},{14,10},{10,6},{6,2},{2,0},{5,1},{9,5},... | collective-permute-start | bytes 1179656 | tf_op jit(solution)/shard_map/ppermute | solution.py:302
  27.2 0.0 collective-permute-done.6.other_block
  27.2 0.5 %add_blocks.10.refs_0_ = f32[304,512]{1,0:T(8,128)S(1)} custom-call(bf16[304,2688]{1,0:T(8,128)(2,1)S(1)} %get-tuple-element.34.own_w, bf16[304,2688]{1,0:T(8,128)(2,1)S(1)} %get-tuple-element.35.other_w, bf16[512,384]{1,0:T(8,128)(2,1)S(1)} %collective-permute-done.2.block, ...), custom_call_target="tpu_custom_call", output_to_operand_aliasing={{}: (4, {})} | custom-call | tf_op jit(solution)/shard_map/add_blocks/pallas_call | solution.py:208
  27.7 1.6 %collective-permute-done.5.block = bf16[512,384]{1,0:T(8,128)(2,1)S(1)} collective-permute-done((bf16[512,384]{1,0:T(8,128)(2,1)S(1)}, bf16[512,384]{1,0:T(8,128)(2,1)S(1)}, u32[]{:S(2)}, u32[]{:S(2)}) %collective-permute-start.5) | collective-permute-done | bytes 393248 | tf_op jit(solution)/shard_map/ppermute | solution.py:302
  29.3 0.0 collective-permute-start.12
  29.3 0.5 %collective-permute-start.11 = (bf16[512,384]{1,0:T(8,128)(2,1)S(1)}, bf16[512,384]{1,0:T(8,128)(2,1)S(1)}, u32[]{:S(2)}, u32[]{:S(2)}) collective-permute-start(bf16[512,384]{1,0:T(8,128)(2,1)S(1)} %collective-permute-done.5.block), channel_id=1, source_target_pairs={{0,1},{1,0},{2,3},{3,2},{4,5},{5,4},{6,7},{7,6},{8,9},{9,8},{10,11... | collective-permute-start | bytes 1179656 | tf_op jit(solution)/shard_map/ppermute | solution.py:305
  29.9 2.1 %collective-permute-start.10 = (bf16[256,384]{1,0:T(8,128)(2,1)S(1)}, bf16[256,384]{1,0:T(8,128)(2,1)S(1)}, u32[]{:S(2)}, u32[]{:S(2)}) collective-permute-start(bf16[256,384]{1,0:T(8,128)(2,1)S(1)} %get-tuple-element.53), channel_id=1, source_target_pairs={{0,4},{4,8},{8,12},{12,14},{14,10},{10,6},{6,2},{2,0},{5,1},{9,5},... | collective-permute-start | bytes 589832 | tf_op jit(solution)/shard_map/ppermute | solution.py:311
  32.0 1.6 %collective-permute-start.9 = (bf16[256,384]{1,0:T(8,128)(2,1)S(1)}, bf16[256,384]{1,0:T(8,128)(2,1)S(1)}, u32[]{:S(2)}, u32[]{:S(2)}) collective-permute-start(bf16[256,384]{1,0:T(8,128)(2,1)S(1)} %get-tuple-element.54), channel_id=1, source_target_pairs={{0,4},{4,8},{8,12},{12,14},{14,10},{10,6},{6,2},{2,0},{5,1},{9,5},... | collective-permute-start | bytes 589832 | tf_op jit(solution)/shard_map/ppermute | solution.py:312
  33.6 0.0 collective-permute-done.15.block
  33.6 0.1 collective-permute-start.16
  33.7 0.0 collective-permute-done.12.other_block
  33.7 0.5 %collective-permute-start.17 = (bf16[256,384]{1,0:T(8,128)(2,1)S(1)}, bf16[256,384]{1,0:T(8,128)(2,1)S(1)}, u32[]{:S(2)}, u32[]{:S(2)}) collective-permute-start(bf16[256,384]{1,0:T(8,128)(2,1)S(1)} %get-tuple-element.52), channel_id=1, source_target_pairs={{0,1},{1,0},{2,3},{3,2},{4,5},{5,4},{6,7},{7,6},{8,9},{9,8},{10,11... | collective-permute-start | bytes 589832 | tf_op jit(solution)/shard_map/ppermute | solution.py:308
  34.2 0.5 %add_blocks.11.refs_0_ = f32[304,512]{1,0:T(8,128)S(1)} custom-call(bf16[304,2688]{1,0:T(8,128)(2,1)S(1)} %get-tuple-element.34.own_w, bf16[304,2688]{1,0:T(8,128)(2,1)S(1)} %get-tuple-element.35.other_w, bf16[512,384]{1,0:T(8,128)(2,1)S(1)} %collective-permute-done.7.block, ...), custom_call_target="tpu_custom_call", output_to_operand_aliasing={{}: (4, {})} | custom-call | tf_op jit(solution)/shard_map/add_blocks/pallas_call | solution.py:208
  34.8 0.0 collective-permute-done.11.other_block
  34.8 0.5 %add_blocks.12.refs_0_ = f32[304,512]{1,0:T(8,128)S(1)} custom-call(bf16[304,2688]{1,0:T(8,128)(2,1)S(1)} %get-tuple-element.34.own_w, bf16[304,2688]{1,0:T(8,128)(2,1)S(1)} %get-tuple-element.35.other_w, bf16[512,384]{1,0:T(8,128)(2,1)S(1)} %collective-permute-done.5.block, ...), custom_call_target="tpu_custom_call", output_to_operand_aliasing={{}: (4, {})} | custom-call | tf_op jit(solution)/shard_map/add_blocks/pallas_call | solution.py:208
  35.3 0.4 collective-permute-done.10.last_a
  35.7 0.0 collective-permute-start.14
  35.7 2.1 %collective-permute-done.9.last_b = bf16[256,384]{1,0:T(8,128)(2,1)S(1)} collective-permute-done((bf16[256,384]{1,0:T(8,128)(2,1)S(1)}, bf16[256,384]{1,0:T(8,128)(2,1)S(1)}, u32[]{:S(2)}, u32[]{:S(2)}) %collective-permute-start.9) | collective-permute-done | bytes 196640 | tf_op jit(solution)/shard_map/ppermute | solution.py:312
  37.8 0.0 collective-permute-start.13
  37.8 0.0 collective-permute-done.16
  37.8 0.0 collective-permute-done.17
  37.8 0.5 %add_blocks.13.before = f32[304,512]{1,0:T(8,128)S(1)} custom-call(bf16[304,2688]{1,0:T(8,128)(2,1)S(1)} %get-tuple-element.34.own_w, bf16[304,2688]{1,0:T(8,128)(2,1)S(1)} %get-tuple-element.35.other_w, bf16[512,384]{1,0:T(8,128)(2,1)S(1)} %collective-permute-done.15.block, ...), custom_call_target="tpu_custom_call", output_to_operand_aliasing={{}: (4, {})} | custom-call | tf_op jit(solution)/shard_map/add_blocks/pallas_call | solution.py:208
  38.4 0.0 collective-permute-done.14.other_a
  38.4 0.4 %add_last.1 = (bf16[304,256]{1,0:T(8,128)(2,1)S(1)}, f32[304,256]{1,0:T(8,128)S(1)}) custom-call(bf16[304,768]{1,0:T(8,128)(2,1)S(1)} %get-tuple-element.32.last_w, bf16[256,384]{1,0:T(8,128)(2,1)S(1)} %collective-permute-done.10.last_a, bf16[256,384]{1,0:T(8,128)(2,1)S(1)} %collective-permute-done.9.last_b, ...), custom_call_target="tpu_custom_call" | custom-call | tf_op jit(solution)/shard_map/add_last/pallas_call | solution.py:231
  38.8 0.4 %collective-permute-done.13.block = bf16[256,384]{1,0:T(8,128)(2,1)S(1)} collective-permute-done((bf16[256,384]{1,0:T(8,128)(2,1)S(1)}, bf16[256,384]{1,0:T(8,128)(2,1)S(1)}, u32[]{:S(2)}, u32[]{:S(2)}) %collective-permute-start.13) | collective-permute-done | bytes 196640 | tf_op jit(solution)/shard_map/ppermute | solution.py:319
  39.2 1.0 %finish.1 = bf16[304,512]{1,0:T(8,128)(2,1)} custom-call(bf16[304,768]{1,0:T(8,128)(2,1)S(1)} %get-tuple-element.32.last_w, bf16[256,384]{1,0:T(8,128)(2,1)S(1)} %collective-permute-done.13.block, bf16[304,256]{1,0:T(8,128)(2,1)S(1)} %get-tuple-element.49.done, f32[304,256]{1,0:T(8,128)S(1)} %get-tuple-element.50.rest), custom_call_target="tpu_custom_call" | custom-call | tf_op jit(solution)/shard_map/finish/pallas_call | solution.py:260
  (6 shorter events, 0.1 us)
Async XLA Ops:
  0.0 8.4 %copy-start = (bf16[6144,304]{0,1:T(8,128)(2,1)S(1)}, bf16[6144,304]{0,1:T(8,128)(2,1)}, u32[]{:S(2)}) copy-start(bf16[6144,304]{0,1:T(8,128)(2,1)} %param.7) | copy-start | bytes 11206660
  0.0 8.4 %copy-start.1 = (s32[64,2]{0,1:T(2,128)S(1)}, s32[64,2]{0,1:T(2,128)}, u32[]{:S(2)}) copy-start(s32[64,2]{0,1:T(2,128)} %param.5) | copy-start | bytes 1540
  3.6 3.2 %collective-permute-start.1 = (bf16[512,384]{1,0:T(8,128)(2,1)S(1)}, bf16[512,384]{1,0:T(8,128)(2,1)S(1)}, u32[]{:S(2)}, u32[]{:S(2)}) collective-permute-start(bf16[512,384]{1,0:T(8,128)(2,1)S(1)} %half_transform.1.block), channel_id=1, source_target_pairs={{0,1},{1,0},{2,3},{3,2},{4,5},{5,4},{6,7},{7,6},{8,9},{9,8},{10,11... | collective-permute-start | bytes 1179656 | tf_op jit(solution)/shard_map/ppermute | solution.py:284
  4.1 8.3 %collective-permute-start = (bf16[512,384]{1,0:T(8,128)(2,1)S(1)}, bf16[512,384]{1,0:T(8,128)(2,1)S(1)}, u32[]{:S(2)}, u32[]{:S(2)}) collective-permute-start(bf16[512,384]{1,0:T(8,128)(2,1)S(1)} %half_transform.1.block), channel_id=1, source_target_pairs={{0,4},{4,8},{8,12},{12,14},{14,10},{10,6},{6,2},{2,0},{5,1},{9,5},... | collective-permute-start | bytes 1179656 | tf_op jit(solution)/shard_map/ppermute | solution.py:302
  6.8 9.9 %collective-permute-start.4 = (bf16[512,384]{1,0:T(8,128)(2,1)S(1)}, bf16[512,384]{1,0:T(8,128)(2,1)S(1)}, u32[]{:S(2)}, u32[]{:S(2)}) collective-permute-start(bf16[512,384]{1,0:T(8,128)(2,1)S(1)} %collective-permute-done.1.other_block), channel_id=1, source_target_pairs={{0,4},{4,8},{8,12},{12,14},{14,10},{10,6},{6,2},{2,0},{5,1},{9,5},... | collective-permute-start | bytes 1179656 | tf_op jit(solution)/shard_map/ppermute | solution.py:302
  12.5 8.4 %collective-permute-start.2 = (bf16[512,384]{1,0:T(8,128)(2,1)S(1)}, bf16[512,384]{1,0:T(8,128)(2,1)S(1)}, u32[]{:S(2)}, u32[]{:S(2)}) collective-permute-start(bf16[512,384]{1,0:T(8,128)(2,1)S(1)} %collective-permute-done.block), channel_id=1, source_target_pairs={{0,4},{4,8},{8,12},{12,14},{14,10},{10,6},{6,2},{2,0},{5,1},{9,5},... | collective-permute-start | bytes 1179656 | tf_op jit(solution)/shard_map/ppermute | solution.py:302
  14.6 6.4 %collective-permute-start.3 = (bf16[512,384]{1,0:T(8,128)(2,1)S(1)}, bf16[512,384]{1,0:T(8,128)(2,1)S(1)}, u32[]{:S(2)}, u32[]{:S(2)}) collective-permute-start(bf16[512,384]{1,0:T(8,128)(2,1)S(1)} %collective-permute-done.block), channel_id=1, source_target_pairs={{0,1},{1,0},{2,3},{3,2},{4,5},{5,4},{6,7},{7,6},{8,9},{9,8},{10,11... | collective-permute-start | bytes 1179656 | tf_op jit(solution)/shard_map/ppermute | solution.py:305
  16.7 6.9 %collective-permute-start.8 = (bf16[512,384]{1,0:T(8,128)(2,1)S(1)}, bf16[512,384]{1,0:T(8,128)(2,1)S(1)}, u32[]{:S(2)}, u32[]{:S(2)}) collective-permute-start(bf16[512,384]{1,0:T(8,128)(2,1)S(1)} %collective-permute-done.4.block), channel_id=1, source_target_pairs={{0,1},{1,0},{2,3},{3,2},{4,5},{5,4},{6,7},{7,6},{8,9},{9,8},{10,11... | collective-permute-start | bytes 1179656 | tf_op jit(solution)/shard_map/ppermute | solution.py:305
  16.7 8.4 %collective-permute-start.7 = (bf16[512,384]{1,0:T(8,128)(2,1)S(1)}, bf16[512,384]{1,0:T(8,128)(2,1)S(1)}, u32[]{:S(2)}, u32[]{:S(2)}) collective-permute-start(bf16[512,384]{1,0:T(8,128)(2,1)S(1)} %collective-permute-done.4.block), channel_id=1, source_target_pairs={{0,4},{4,8},{8,12},{12,14},{14,10},{10,6},{6,2},{2,0},{5,1},{9,5},... | collective-permute-start | bytes 1179656 | tf_op jit(solution)/shard_map/ppermute | solution.py:302
  20.9 6.3 %collective-permute-start.6 = (bf16[512,384]{1,0:T(8,128)(2,1)S(1)}, bf16[512,384]{1,0:T(8,128)(2,1)S(1)}, u32[]{:S(2)}, u32[]{:S(2)}) collective-permute-start(bf16[512,384]{1,0:T(8,128)(2,1)S(1)} %collective-permute-done.2.block), channel_id=1, source_target_pairs={{0,1},{1,0},{2,3},{3,2},{4,5},{5,4},{6,7},{7,6},{8,9},{9,8},{10,11... | collective-permute-start | bytes 1179656 | tf_op jit(solution)/shard_map/ppermute | solution.py:305
  21.4 7.9 %collective-permute-start.5 = (bf16[512,384]{1,0:T(8,128)(2,1)S(1)}, bf16[512,384]{1,0:T(8,128)(2,1)S(1)}, u32[]{:S(2)}, u32[]{:S(2)}) collective-permute-start(bf16[512,384]{1,0:T(8,128)(2,1)S(1)} %collective-permute-done.2.block), channel_id=1, source_target_pairs={{0,4},{4,8},{8,12},{12,14},{14,10},{10,6},{6,2},{2,0},{5,1},{9,5},... | collective-permute-start | bytes 1179656 | tf_op jit(solution)/shard_map/ppermute | solution.py:302
  25.1 8.5 %collective-permute-start.15 = (bf16[512,384]{1,0:T(8,128)(2,1)S(1)}, bf16[512,384]{1,0:T(8,128)(2,1)S(1)}, u32[]{:S(2)}, u32[]{:S(2)}) collective-permute-start(bf16[512,384]{1,0:T(8,128)(2,1)S(1)} %collective-permute-done.7.block), channel_id=1, source_target_pairs={{0,4},{4,8},{8,12},{12,14},{14,10},{10,6},{6,2},{2,0},{5,1},{9,5},... | collective-permute-start | bytes 1179656 | tf_op jit(solution)/shard_map/ppermute | solution.py:302
  29.3 4.4 %collective-permute-start.12 = (bf16[512,384]{1,0:T(8,128)(2,1)S(1)}, bf16[512,384]{1,0:T(8,128)(2,1)S(1)}, u32[]{:S(2)}, u32[]{:S(2)}) collective-permute-start(bf16[512,384]{1,0:T(8,128)(2,1)S(1)} %collective-permute-done.7.block), channel_id=1, source_target_pairs={{0,1},{1,0},{2,3},{3,2},{4,5},{5,4},{6,7},{7,6},{8,9},{9,8},{10,11... | collective-permute-start | bytes 1179656 | tf_op jit(solution)/shard_map/ppermute | solution.py:305
  29.3 5.4 %collective-permute-start.11 = (bf16[512,384]{1,0:T(8,128)(2,1)S(1)}, bf16[512,384]{1,0:T(8,128)(2,1)S(1)}, u32[]{:S(2)}, u32[]{:S(2)}) collective-permute-start(bf16[512,384]{1,0:T(8,128)(2,1)S(1)} %collective-permute-done.5.block), channel_id=1, source_target_pairs={{0,1},{1,0},{2,3},{3,2},{4,5},{5,4},{6,7},{7,6},{8,9},{9,8},{10,11... | collective-permute-start | bytes 1179656 | tf_op jit(solution)/shard_map/ppermute | solution.py:305
  29.9 5.8 %collective-permute-start.10 = (bf16[256,384]{1,0:T(8,128)(2,1)S(1)}, bf16[256,384]{1,0:T(8,128)(2,1)S(1)}, u32[]{:S(2)}, u32[]{:S(2)}) collective-permute-start(bf16[256,384]{1,0:T(8,128)(2,1)S(1)} %get-tuple-element.53), channel_id=1, source_target_pairs={{0,4},{4,8},{8,12},{12,14},{14,10},{10,6},{6,2},{2,0},{5,1},{9,5},... | collective-permute-start | bytes 589832 | tf_op jit(solution)/shard_map/ppermute | solution.py:311
  32.0 5.7 %collective-permute-start.9 = (bf16[256,384]{1,0:T(8,128)(2,1)S(1)}, bf16[256,384]{1,0:T(8,128)(2,1)S(1)}, u32[]{:S(2)}, u32[]{:S(2)}) collective-permute-start(bf16[256,384]{1,0:T(8,128)(2,1)S(1)} %get-tuple-element.54), channel_id=1, source_target_pairs={{0,4},{4,8},{8,12},{12,14},{14,10},{10,6},{6,2},{2,0},{5,1},{9,5},... | collective-permute-start | bytes 589832 | tf_op jit(solution)/shard_map/ppermute | solution.py:312
  33.6 4.1 %collective-permute-start.16 = (bf16[256,384]{1,0:T(8,128)(2,1)S(1)}, bf16[256,384]{1,0:T(8,128)(2,1)S(1)}, u32[]{:S(2)}, u32[]{:S(2)}) collective-permute-start(bf16[256,384]{1,0:T(8,128)(2,1)S(1)} %get-tuple-element.51), channel_id=1, source_target_pairs={{0,1},{1,0},{2,3},{3,2},{4,5},{5,4},{6,7},{7,6},{8,9},{9,8},{10,11... | collective-permute-start | bytes 589832 | tf_op jit(solution)/shard_map/ppermute | solution.py:308
  33.7 4.0 %collective-permute-start.17 = (bf16[256,384]{1,0:T(8,128)(2,1)S(1)}, bf16[256,384]{1,0:T(8,128)(2,1)S(1)}, u32[]{:S(2)}, u32[]{:S(2)}) collective-permute-start(bf16[256,384]{1,0:T(8,128)(2,1)S(1)} %get-tuple-element.52), channel_id=1, source_target_pairs={{0,1},{1,0},{2,3},{3,2},{4,5},{5,4},{6,7},{7,6},{8,9},{9,8},{10,11... | collective-permute-start | bytes 589832 | tf_op jit(solution)/shard_map/ppermute | solution.py:308
  35.7 2.7 %collective-permute-start.14 = (bf16[256,384]{1,0:T(8,128)(2,1)S(1)}, bf16[256,384]{1,0:T(8,128)(2,1)S(1)}, u32[]{:S(2)}, u32[]{:S(2)}) collective-permute-start(bf16[256,384]{1,0:T(8,128)(2,1)S(1)} %collective-permute-done.10.last_a), channel_id=1, source_target_pairs={{0,1},{1,0},{2,3},{3,2},{4,5},{5,4},{6,7},{7,6},{8,9},{9,8},{10,11... | collective-permute-start | bytes 589832 | tf_op jit(solution)/shard_map/ppermute | solution.py:317
  37.8 1.4 %collective-permute-start.13 = (bf16[256,384]{1,0:T(8,128)(2,1)S(1)}, bf16[256,384]{1,0:T(8,128)(2,1)S(1)}, u32[]{:S(2)}, u32[]{:S(2)}) collective-permute-start(bf16[256,384]{1,0:T(8,128)(2,1)S(1)} %collective-permute-done.9.last_b), channel_id=1, source_target_pairs={{0,1},{1,0},{2,3},{3,2},{4,5},{5,4},{6,7},{7,6},{8,9},{9,8},{10,11... | collective-permute-start | bytes 589832 | tf_op jit(solution)/shard_map/ppermute | solution.py:319

commit v7 on v6

--- a/solution.py
+++ b/solution.py
@@ -297,7 +297,10 @@
         if message > 3:
             total = add_blocks(total, summed, own_w, other_w, blocks[summed], other_blocks[summed])
             summed += 1
-            block, total = lax.optimization_barrier((block, total))
+            if message == chips - 1:
+                block, total, other_blocks[summed] = lax.optimization_barrier((block, total, other_blocks[summed]))
+            else:
+                block, total = lax.optimization_barrier((block, total))
         if message < chips - 1:
             block = lax.ppermute(block, "ao", onward)
             blocks.append(block)

time: 40.3 us -> 40.3 us (level)
  starting transfers between devices: 18 us -> 17.5 us
  waiting for transfers between devices: 10.5 us -> 11 us
    ppermute x6, waiting for transfers between devices: 7.58 us -> 8.11 us  [on_device(): block = lax.ppermute(block, 'ao', onward)]
    ppermute x5, starting transfers between devices: 0.52 us -> 0.01 us  [on_device(): other_blocks.append(lax.ppermute(block, 'ao', across))]
where the time goes in v7:
time: 40.3 us; the launch traced here: 40.2 us
  starting transfers between devices  17.5 us (43%)
  Pallas kernels  11.5 us (29%)
  waiting for transfers between devices  11 us (27%)
    ppermute x6, starting transfers between devices, on_device(): block = lax.ppermute(block, 'ao', onward)  12.7 us
    ppermute x6, waiting for transfers between devices, on_device(): block = lax.ppermute(block, 'ao', onward)  8.11 us
    pallas_call x7, Pallas kernels, add_blocks(): pl.pallas_call(functools.partial(add_kernel, k), in_specs=[vmem] * (4 + l...  3.66 us
    pallas_call x1, Pallas kernels, half_transform(): pl.pallas_call(half_kernel, in_specs=[pl.BlockSpec(memory_space=pltpu.SME...  3.62 us
    pallas_call x1, Pallas kernels, windows(): pl.pallas_call(functools.partial(window_kernel, count, chips), in_specs=[...  2.8 us
    ppermute x1, starting transfers between devices, on_device(): last_a = lax.ppermute(block[:half], 'ao', onward)  2.13 us
    ppermute x1, waiting for transfers between devices, on_device(): last_b = lax.ppermute(block[half:], 'ao', onward)  2.1 us
    ppermute x1, starting transfers between devices, on_device(): last_b = lax.ppermute(block[half:], 'ao', onward)  1.58 us
  transfers between devices with their start and end apart: 18, of which 8 were waited for; matrix products, arithmetic and copies ran while one was open for 0% of the time, Pallas kernels for 17%

profile of v7, /device:TPU:0, one launch (start us, length us, event | category | flops | bytes accessed | tf_op | source)
XLA Modules:
  0.0 40.2 jit_solution(14512034947984317835)
XLA Ops:
  0.0 3.6 %half_transform.1.block = bf16[512,384]{1,0:T(8,128)(2,1)S(1)} custom-call(s32[1]{0:T(128)} %bitcast.me, s32[2,64]{1,0:T(2,128)} %bitcast.5, bf16[8,6144]{1,0:T(8,128)(2,1)} %bitcast.7, bf16[4,128,64,128]{3,2,1,0:T(8,128)(2,1)} %tiles_ref.1), custom_call_target="tpu_custom_call" | custom-call | flops 603979776 | bytes 8388608 | tf_op jit(solution)/shard_map/half_transform/pallas_call | solution.py:102
  3.6 0.5 %collective-permute-start.1 = (bf16[512,384]{1,0:T(8,128)(2,1)S(1)}, bf16[512,384]{1,0:T(8,128)(2,1)S(1)}, u32[]{:S(2)}, u32[]{:S(2)}) collective-permute-start(bf16[512,384]{1,0:T(8,128)(2,1)S(1)} %half_transform.1.block), channel_id=1, source_target_pairs={{0,1},{1,0},{2,3},{3,2},{4,5},{5,4},{6,7},{7,6},{8,9},{9,8},{10,11... | collective-permute-start | bytes 1179656 | tf_op jit(solution)/shard_map/ppermute | solution.py:284
  4.1 2.6 %collective-permute-start = (bf16[512,384]{1,0:T(8,128)(2,1)S(1)}, bf16[512,384]{1,0:T(8,128)(2,1)S(1)}, u32[]{:S(2)}, u32[]{:S(2)}) collective-permute-start(bf16[512,384]{1,0:T(8,128)(2,1)S(1)} %half_transform.1.block), channel_id=1, source_target_pairs={{0,4},{4,8},{8,12},{12,14},{14,10},{10,6},{6,2},{2,0},{5,1},{9,5},... | collective-permute-start | bytes 1179656 | tf_op jit(solution)/shard_map/ppermute | solution.py:305
  6.8 0.0 collective-permute-done.1.other_block
  6.8 1.7 %collective-permute-start.4 = (bf16[512,384]{1,0:T(8,128)(2,1)S(1)}, bf16[512,384]{1,0:T(8,128)(2,1)S(1)}, u32[]{:S(2)}, u32[]{:S(2)}) collective-permute-start(bf16[512,384]{1,0:T(8,128)(2,1)S(1)} %collective-permute-done.1.other_block), channel_id=1, source_target_pairs={{0,4},{4,8},{8,12},{12,14},{14,10},{10,6},{6,2},{2,0},{5,1},{9,5},... | collective-permute-start | bytes 1179656 | tf_op jit(solution)/shard_map/ppermute | solution.py:305
  8.4 0.0 copy-done
  8.4 2.8 %vir_windows.1 = (bf16[304,2688]{1,0:T(8,128)(2,1)S(1)}, bf16[304,2688]{1,0:T(8,128)(2,1)S(1)}, bf16[304,768]{1,0:T(8,128)(2,1)S(1)}) custom-call(s32[1]{0:T(128)} %bitcast.me, s32[2,64]{1,0:T(2,128)S(1)} %bitcast.6, bf16[304,6144]{1,0:T(8,128)(2,1)S(1)} %bitcast.4), custom_call_target="tpu_custom_call" | custom-call | tf_op jit(solution)/shard_map/vir_windows/pallas_call | solution.py:178
  11.3 1.2 %collective-permute-done.block = bf16[512,384]{1,0:T(8,128)(2,1)S(1)} collective-permute-done((bf16[512,384]{1,0:T(8,128)(2,1)S(1)}, bf16[512,384]{1,0:T(8,128)(2,1)S(1)}, u32[]{:S(2)}, u32[]{:S(2)}) %collective-permute-start) | collective-permute-done | bytes 393248 | tf_op jit(solution)/shard_map/ppermute | solution.py:305
  12.5 0.0 collective-permute-start.3
  12.5 2.1 %collective-permute-start.2 = (bf16[512,384]{1,0:T(8,128)(2,1)S(1)}, bf16[512,384]{1,0:T(8,128)(2,1)S(1)}, u32[]{:S(2)}, u32[]{:S(2)}) collective-permute-start(bf16[512,384]{1,0:T(8,128)(2,1)S(1)} %collective-permute-done.block), channel_id=1, source_target_pairs={{0,4},{4,8},{8,12},{12,14},{14,10},{10,6},{6,2},{2,0},{5,1},{9,5},... | collective-permute-start | bytes 1179656 | tf_op jit(solution)/shard_map/ppermute | solution.py:305
  14.6 0.5 %add_blocks.7.refs_0_ = f32[304,512]{1,0:T(8,128)S(1)} custom-call(bf16[304,2688]{1,0:T(8,128)(2,1)S(1)} %get-tuple-element.35.own_w, bf16[304,2688]{1,0:T(8,128)(2,1)S(1)} %get-tuple-element.36.other_w, bf16[512,384]{1,0:T(8,128)(2,1)S(1)} %half_transform.1.block, bf16[512,384]{1,0:T(8,128)(2,1)S(1)} %collective-permute-done.1.other_block), custom_call_target="tpu_custom_call" | custom-call | tf_op jit(solution)/shard_map/add_blocks/pallas_call | solution.py:208
  15.1 1.6 %collective-permute-done.4.block = bf16[512,384]{1,0:T(8,128)(2,1)S(1)} collective-permute-done((bf16[512,384]{1,0:T(8,128)(2,1)S(1)}, bf16[512,384]{1,0:T(8,128)(2,1)S(1)}, u32[]{:S(2)}, u32[]{:S(2)}) %collective-permute-start.4) | collective-permute-done | bytes 393248 | tf_op jit(solution)/shard_map/ppermute | solution.py:305
  16.7 2.1 %collective-permute-start.7 = (bf16[512,384]{1,0:T(8,128)(2,1)S(1)}, bf16[512,384]{1,0:T(8,128)(2,1)S(1)}, u32[]{:S(2)}, u32[]{:S(2)}) collective-permute-start(bf16[512,384]{1,0:T(8,128)(2,1)S(1)} %collective-permute-done.4.block), channel_id=1, source_target_pairs={{0,4},{4,8},{8,12},{12,14},{14,10},{10,6},{6,2},{2,0},{5,1},{9,5},... | collective-permute-start | bytes 1179656 | tf_op jit(solution)/shard_map/ppermute | solution.py:305
  18.8 0.0 collective-permute-start.8
  18.8 0.0 collective-permute-done.3.other_block
  18.8 0.5 %add_blocks.8.refs_0_ = f32[304,512]{1,0:T(8,128)S(1)} custom-call(bf16[304,2688]{1,0:T(8,128)(2,1)S(1)} %get-tuple-element.35.own_w, bf16[304,2688]{1,0:T(8,128)(2,1)S(1)} %get-tuple-element.36.other_w, bf16[512,384]{1,0:T(8,128)(2,1)S(1)} %collective-permute-done.block, ...), custom_call_target="tpu_custom_call", output_to_operand_aliasing={{}: (4, {})} | custom-call | tf_op jit(solution)/shard_map/add_blocks/pallas_call | solution.py:208
  19.3 1.6 %collective-permute-done.2.block = bf16[512,384]{1,0:T(8,128)(2,1)S(1)} collective-permute-done((bf16[512,384]{1,0:T(8,128)(2,1)S(1)}, bf16[512,384]{1,0:T(8,128)(2,1)S(1)}, u32[]{:S(2)}, u32[]{:S(2)}) %collective-permute-start.2) | collective-permute-done | bytes 393248 | tf_op jit(solution)/shard_map/ppermute | solution.py:305
  20.9 2.1 %collective-permute-start.5 = (bf16[512,384]{1,0:T(8,128)(2,1)S(1)}, bf16[512,384]{1,0:T(8,128)(2,1)S(1)}, u32[]{:S(2)}, u32[]{:S(2)}) collective-permute-start(bf16[512,384]{1,0:T(8,128)(2,1)S(1)} %collective-permute-done.2.block), channel_id=1, source_target_pairs={{0,4},{4,8},{8,12},{12,14},{14,10},{10,6},{6,2},{2,0},{5,1},{9,5},... | collective-permute-start | bytes 1179656 | tf_op jit(solution)/shard_map/ppermute | solution.py:305
  23.0 0.0 collective-permute-start.6
  23.0 2.1 %collective-permute-done.7.block = bf16[512,384]{1,0:T(8,128)(2,1)S(1)} collective-permute-done((bf16[512,384]{1,0:T(8,128)(2,1)S(1)}, bf16[512,384]{1,0:T(8,128)(2,1)S(1)}, u32[]{:S(2)}, u32[]{:S(2)}) %collective-permute-start.7) | collective-permute-done | bytes 393248 | tf_op jit(solution)/shard_map/ppermute | solution.py:305
  25.1 0.0 collective-permute-start.9
  25.1 0.0 collective-permute-done.8.other_block
  25.1 0.5 %add_blocks.9.refs_0_ = f32[304,512]{1,0:T(8,128)S(1)} custom-call(bf16[304,2688]{1,0:T(8,128)(2,1)S(1)} %get-tuple-element.35.own_w, bf16[304,2688]{1,0:T(8,128)(2,1)S(1)} %get-tuple-element.36.other_w, bf16[512,384]{1,0:T(8,128)(2,1)S(1)} %collective-permute-done.4.block, ...), custom_call_target="tpu_custom_call", output_to_operand_aliasing={{}: (4, {})} | custom-call | tf_op jit(solution)/shard_map/add_blocks/pallas_call | solution.py:208
  25.7 2.1 %collective-permute-start.15 = (bf16[512,384]{1,0:T(8,128)(2,1)S(1)}, bf16[512,384]{1,0:T(8,128)(2,1)S(1)}, u32[]{:S(2)}, u32[]{:S(2)}) collective-permute-start(bf16[512,384]{1,0:T(8,128)(2,1)S(1)} %collective-permute-done.7.block), channel_id=1, source_target_pairs={{0,4},{4,8},{8,12},{12,14},{14,10},{10,6},{6,2},{2,0},{5,1},{9,5},... | collective-permute-start | bytes 1179656 | tf_op jit(solution)/shard_map/ppermute | solution.py:305
  27.8 1.5 %collective-permute-done.5.block = bf16[512,384]{1,0:T(8,128)(2,1)S(1)} collective-permute-done((bf16[512,384]{1,0:T(8,128)(2,1)S(1)}, bf16[512,384]{1,0:T(8,128)(2,1)S(1)}, u32[]{:S(2)}, u32[]{:S(2)}) %collective-permute-start.5) | collective-permute-done | bytes 393248 | tf_op jit(solution)/shard_map/ppermute | solution.py:305
  29.3 0.0 collective-permute-start.12
  29.3 0.0 collective-permute-done.6.other_block
  29.3 0.5 %add_blocks.10.refs_0_ = f32[304,512]{1,0:T(8,128)S(1)} custom-call(bf16[304,2688]{1,0:T(8,128)(2,1)S(1)} %get-tuple-element.35.own_w, bf16[304,2688]{1,0:T(8,128)(2,1)S(1)} %get-tuple-element.36.other_w, bf16[512,384]{1,0:T(8,128)(2,1)S(1)} %collective-permute-done.2.block, ...), custom_call_target="tpu_custom_call", output_to_operand_aliasing={{}: (4, {})} | custom-call | tf_op jit(solution)/shard_map/add_blocks/pallas_call | solution.py:208
  29.9 0.0 collective-permute-done.9.other_block
  29.9 2.1 %collective-permute-start.11 = (bf16[256,384]{1,0:T(8,128)(2,1)S(1)}, bf16[256,384]{1,0:T(8,128)(2,1)S(1)}, u32[]{:S(2)}, u32[]{:S(2)}) collective-permute-start(bf16[256,384]{1,0:T(8,128)(2,1)S(1)} %get-tuple-element.55), channel_id=1, source_target_pairs={{0,4},{4,8},{8,12},{12,14},{14,10},{10,6},{6,2},{2,0},{5,1},{9,5},... | collective-permute-start | bytes 589832 | tf_op jit(solution)/shard_map/ppermute | solution.py:314
  32.1 1.6 %collective-permute-start.10 = (bf16[256,384]{1,0:T(8,128)(2,1)S(1)}, bf16[256,384]{1,0:T(8,128)(2,1)S(1)}, u32[]{:S(2)}, u32[]{:S(2)}) collective-permute-start(bf16[256,384]{1,0:T(8,128)(2,1)S(1)} %get-tuple-element.56), channel_id=1, source_target_pairs={{0,4},{4,8},{8,12},{12,14},{14,10},{10,6},{6,2},{2,0},{5,1},{9,5},... | collective-permute-start | bytes 589832 | tf_op jit(solution)/shard_map/ppermute | solution.py:315
  33.6 0.0 collective-permute-done.15.block
  33.7 0.1 collective-permute-start.16
  33.8 0.5 %collective-permute-start.17 = (bf16[256,384]{1,0:T(8,128)(2,1)S(1)}, bf16[256,384]{1,0:T(8,128)(2,1)S(1)}, u32[]{:S(2)}, u32[]{:S(2)}) collective-permute-start(bf16[256,384]{1,0:T(8,128)(2,1)S(1)} %get-tuple-element.54), channel_id=1, source_target_pairs={{0,1},{1,0},{2,3},{3,2},{4,5},{5,4},{6,7},{7,6},{8,9},{9,8},{10,11... | collective-permute-start | bytes 589832 | tf_op jit(solution)/shard_map/ppermute | solution.py:311
  34.3 0.5 %add_blocks.11.refs_0_ = f32[304,512]{1,0:T(8,128)S(1)} custom-call(bf16[304,2688]{1,0:T(8,128)(2,1)S(1)} %get-tuple-element.35.own_w, bf16[304,2688]{1,0:T(8,128)(2,1)S(1)} %get-tuple-element.36.other_w, bf16[512,384]{1,0:T(8,128)(2,1)S(1)} %collective-permute-done.7.block, ...), custom_call_target="tpu_custom_call", output_to_operand_aliasing={{}: (4, {})} | custom-call | tf_op jit(solution)/shard_map/add_blocks/pallas_call | solution.py:208
  34.8 0.0 collective-permute-done.12.other_block
  34.8 0.5 %add_blocks.12.refs_0_ = f32[304,512]{1,0:T(8,128)S(1)} custom-call(bf16[304,2688]{1,0:T(8,128)(2,1)S(1)} %get-tuple-element.35.own_w, bf16[304,2688]{1,0:T(8,128)(2,1)S(1)} %get-tuple-element.36.other_w, bf16[512,384]{1,0:T(8,128)(2,1)S(1)} %collective-permute-done.5.block, ...), custom_call_target="tpu_custom_call", output_to_operand_aliasing={{}: (4, {})} | custom-call | tf_op jit(solution)/shard_map/add_blocks/pallas_call | solution.py:208
  35.3 0.3 collective-permute-done.11.last_a
  35.7 0.0 collective-permute-start.14
  35.7 2.1 %collective-permute-done.10.last_b = bf16[256,384]{1,0:T(8,128)(2,1)S(1)} collective-permute-done((bf16[256,384]{1,0:T(8,128)(2,1)S(1)}, bf16[256,384]{1,0:T(8,128)(2,1)S(1)}, u32[]{:S(2)}, u32[]{:S(2)}) %collective-permute-start.10) | collective-permute-done | bytes 196640 | tf_op jit(solution)/shard_map/ppermute | solution.py:315
  37.8 0.0 collective-permute-start.13
  37.8 0.0 collective-permute-done.16
  37.8 0.0 collective-permute-done.17
  37.8 0.5 %add_blocks.13.before = f32[304,512]{1,0:T(8,128)S(1)} custom-call(bf16[304,2688]{1,0:T(8,128)(2,1)S(1)} %get-tuple-element.35.own_w, bf16[304,2688]{1,0:T(8,128)(2,1)S(1)} %get-tuple-element.36.other_w, bf16[512,384]{1,0:T(8,128)(2,1)S(1)} %collective-permute-done.15.block, ...), custom_call_target="tpu_custom_call", output_to_operand_aliasing={{}: (4, {})} | custom-call | tf_op jit(solution)/shard_map/add_blocks/pallas_call | solution.py:208
  38.4 0.0 collective-permute-done.14.other_a
  38.4 0.4 %add_last.1 = (bf16[304,256]{1,0:T(8,128)(2,1)S(1)}, f32[304,256]{1,0:T(8,128)S(1)}) custom-call(bf16[304,768]{1,0:T(8,128)(2,1)S(1)} %get-tuple-element.33.last_w, bf16[256,384]{1,0:T(8,128)(2,1)S(1)} %collective-permute-done.11.last_a, bf16[256,384]{1,0:T(8,128)(2,1)S(1)} %collective-permute-done.10.last_b, ...), custom_call_target="tpu_custom_call" | custom-call | tf_op jit(solution)/shard_map/add_last/pallas_call | solution.py:231
  38.8 0.4 %collective-permute-done.13.block = bf16[256,384]{1,0:T(8,128)(2,1)S(1)} collective-permute-done((bf16[256,384]{1,0:T(8,128)(2,1)S(1)}, bf16[256,384]{1,0:T(8,128)(2,1)S(1)}, u32[]{:S(2)}, u32[]{:S(2)}) %collective-permute-start.13) | collective-permute-done | bytes 196640 | tf_op jit(solution)/shard_map/ppermute | solution.py:322
  39.2 1.0 %finish.1 = bf16[304,512]{1,0:T(8,128)(2,1)} custom-call(bf16[304,768]{1,0:T(8,128)(2,1)S(1)} %get-tuple-element.33.last_w, bf16[256,384]{1,0:T(8,128)(2,1)S(1)} %collective-permute-done.13.block, bf16[304,256]{1,0:T(8,128)(2,1)S(1)} %get-tuple-element.51.done, f32[304,256]{1,0:T(8,128)S(1)} %get-tuple-element.52.rest), custom_call_target="tpu_custom_call" | custom-call | tf_op jit(solution)/shard_map/finish/pallas_call | solution.py:260
  (6 shorter events, 0.1 us)
Async XLA Ops:
  0.0 8.4 %copy-start = (bf16[6144,304]{0,1:T(8,128)(2,1)S(1)}, bf16[6144,304]{0,1:T(8,128)(2,1)}, u32[]{:S(2)}) copy-start(bf16[6144,304]{0,1:T(8,128)(2,1)} %param.7) | copy-start | bytes 11206660
  0.0 8.4 %copy-start.1 = (s32[64,2]{0,1:T(2,128)S(1)}, s32[64,2]{0,1:T(2,128)}, u32[]{:S(2)}) copy-start(s32[64,2]{0,1:T(2,128)} %param.5) | copy-start | bytes 1540
  3.6 3.2 %collective-permute-start.1 = (bf16[512,384]{1,0:T(8,128)(2,1)S(1)}, bf16[512,384]{1,0:T(8,128)(2,1)S(1)}, u32[]{:S(2)}, u32[]{:S(2)}) collective-permute-start(bf16[512,384]{1,0:T(8,128)(2,1)S(1)} %half_transform.1.block), channel_id=1, source_target_pairs={{0,1},{1,0},{2,3},{3,2},{4,5},{5,4},{6,7},{7,6},{8,9},{9,8},{10,11... | collective-permute-start | bytes 1179656 | tf_op jit(solution)/shard_map/ppermute | solution.py:284
  4.1 8.3 %collective-permute-start = (bf16[512,384]{1,0:T(8,128)(2,1)S(1)}, bf16[512,384]{1,0:T(8,128)(2,1)S(1)}, u32[]{:S(2)}, u32[]{:S(2)}) collective-permute-start(bf16[512,384]{1,0:T(8,128)(2,1)S(1)} %half_transform.1.block), channel_id=1, source_target_pairs={{0,4},{4,8},{8,12},{12,14},{14,10},{10,6},{6,2},{2,0},{5,1},{9,5},... | collective-permute-start | bytes 1179656 | tf_op jit(solution)/shard_map/ppermute | solution.py:305
  6.8 9.9 %collective-permute-start.4 = (bf16[512,384]{1,0:T(8,128)(2,1)S(1)}, bf16[512,384]{1,0:T(8,128)(2,1)S(1)}, u32[]{:S(2)}, u32[]{:S(2)}) collective-permute-start(bf16[512,384]{1,0:T(8,128)(2,1)S(1)} %collective-permute-done.1.other_block), channel_id=1, source_target_pairs={{0,4},{4,8},{8,12},{12,14},{14,10},{10,6},{6,2},{2,0},{5,1},{9,5},... | collective-permute-start | bytes 1179656 | tf_op jit(solution)/shard_map/ppermute | solution.py:305
  12.5 6.3 %collective-permute-start.3 = (bf16[512,384]{1,0:T(8,128)(2,1)S(1)}, bf16[512,384]{1,0:T(8,128)(2,1)S(1)}, u32[]{:S(2)}, u32[]{:S(2)}) collective-permute-start(bf16[512,384]{1,0:T(8,128)(2,1)S(1)} %collective-permute-done.block), channel_id=1, source_target_pairs={{0,1},{1,0},{2,3},{3,2},{4,5},{5,4},{6,7},{7,6},{8,9},{9,8},{10,11... | collective-permute-start | bytes 1179656 | tf_op jit(solution)/shard_map/ppermute | solution.py:308
  12.5 8.4 %collective-permute-start.2 = (bf16[512,384]{1,0:T(8,128)(2,1)S(1)}, bf16[512,384]{1,0:T(8,128)(2,1)S(1)}, u32[]{:S(2)}, u32[]{:S(2)}) collective-permute-start(bf16[512,384]{1,0:T(8,128)(2,1)S(1)} %collective-permute-done.block), channel_id=1, source_target_pairs={{0,4},{4,8},{8,12},{12,14},{14,10},{10,6},{6,2},{2,0},{5,1},{9,5},... | collective-permute-start | bytes 1179656 | tf_op jit(solution)/shard_map/ppermute | solution.py:305
  16.7 8.4 %collective-permute-start.7 = (bf16[512,384]{1,0:T(8,128)(2,1)S(1)}, bf16[512,384]{1,0:T(8,128)(2,1)S(1)}, u32[]{:S(2)}, u32[]{:S(2)}) collective-permute-start(bf16[512,384]{1,0:T(8,128)(2,1)S(1)} %collective-permute-done.4.block), channel_id=1, source_target_pairs={{0,4},{4,8},{8,12},{12,14},{14,10},{10,6},{6,2},{2,0},{5,1},{9,5},... | collective-permute-start | bytes 1179656 | tf_op jit(solution)/shard_map/ppermute | solution.py:305
  18.8 6.4 %collective-permute-start.8 = (bf16[512,384]{1,0:T(8,128)(2,1)S(1)}, bf16[512,384]{1,0:T(8,128)(2,1)S(1)}, u32[]{:S(2)}, u32[]{:S(2)}) collective-permute-start(bf16[512,384]{1,0:T(8,128)(2,1)S(1)} %collective-permute-done.4.block), channel_id=1, source_target_pairs={{0,1},{1,0},{2,3},{3,2},{4,5},{5,4},{6,7},{7,6},{8,9},{9,8},{10,11... | collective-permute-start | bytes 1179656 | tf_op jit(solution)/shard_map/ppermute | solution.py:308
  20.9 8.4 %collective-permute-start.5 = (bf16[512,384]{1,0:T(8,128)(2,1)S(1)}, bf16[512,384]{1,0:T(8,128)(2,1)S(1)}, u32[]{:S(2)}, u32[]{:S(2)}) collective-permute-start(bf16[512,384]{1,0:T(8,128)(2,1)S(1)} %collective-permute-done.2.block), channel_id=1, source_target_pairs={{0,4},{4,8},{8,12},{12,14},{14,10},{10,6},{6,2},{2,0},{5,1},{9,5},... | collective-permute-start | bytes 1179656 | tf_op jit(solution)/shard_map/ppermute | solution.py:305
  23.0 6.4 %collective-permute-start.6 = (bf16[512,384]{1,0:T(8,128)(2,1)S(1)}, bf16[512,384]{1,0:T(8,128)(2,1)S(1)}, u32[]{:S(2)}, u32[]{:S(2)}) collective-permute-start(bf16[512,384]{1,0:T(8,128)(2,1)S(1)} %collective-permute-done.2.block), channel_id=1, source_target_pairs={{0,1},{1,0},{2,3},{3,2},{4,5},{5,4},{6,7},{7,6},{8,9},{9,8},{10,11... | collective-permute-start | bytes 1179656 | tf_op jit(solution)/shard_map/ppermute | solution.py:308
  25.1 4.8 %collective-permute-start.9 = (bf16[512,384]{1,0:T(8,128)(2,1)S(1)}, bf16[512,384]{1,0:T(8,128)(2,1)S(1)}, u32[]{:S(2)}, u32[]{:S(2)}) collective-permute-start(bf16[512,384]{1,0:T(8,128)(2,1)S(1)} %collective-permute-done.7.block), channel_id=1, source_target_pairs={{0,1},{1,0},{2,3},{3,2},{4,5},{5,4},{6,7},{7,6},{8,9},{9,8},{10,11... | collective-permute-start | bytes 1179656 | tf_op jit(solution)/shard_map/ppermute | solution.py:308
  25.7 8.0 %collective-permute-start.15 = (bf16[512,384]{1,0:T(8,128)(2,1)S(1)}, bf16[512,384]{1,0:T(8,128)(2,1)S(1)}, u32[]{:S(2)}, u32[]{:S(2)}) collective-permute-start(bf16[512,384]{1,0:T(8,128)(2,1)S(1)} %collective-permute-done.7.block), channel_id=1, source_target_pairs={{0,4},{4,8},{8,12},{12,14},{14,10},{10,6},{6,2},{2,0},{5,1},{9,5},... | collective-permute-start | bytes 1179656 | tf_op jit(solution)/shard_map/ppermute | solution.py:305
  29.3 5.5 %collective-permute-start.12 = (bf16[512,384]{1,0:T(8,128)(2,1)S(1)}, bf16[512,384]{1,0:T(8,128)(2,1)S(1)}, u32[]{:S(2)}, u32[]{:S(2)}) collective-permute-start(bf16[512,384]{1,0:T(8,128)(2,1)S(1)} %collective-permute-done.5.block), channel_id=1, source_target_pairs={{0,1},{1,0},{2,3},{3,2},{4,5},{5,4},{6,7},{7,6},{8,9},{9,8},{10,11... | collective-permute-start | bytes 1179656 | tf_op jit(solution)/shard_map/ppermute | solution.py:308
  29.9 5.7 %collective-permute-start.11 = (bf16[256,384]{1,0:T(8,128)(2,1)S(1)}, bf16[256,384]{1,0:T(8,128)(2,1)S(1)}, u32[]{:S(2)}, u32[]{:S(2)}) collective-permute-start(bf16[256,384]{1,0:T(8,128)(2,1)S(1)} %get-tuple-element.55), channel_id=1, source_target_pairs={{0,4},{4,8},{8,12},{12,14},{14,10},{10,6},{6,2},{2,0},{5,1},{9,5},... | collective-permute-start | bytes 589832 | tf_op jit(solution)/shard_map/ppermute | solution.py:314
  32.1 5.7 %collective-permute-start.10 = (bf16[256,384]{1,0:T(8,128)(2,1)S(1)}, bf16[256,384]{1,0:T(8,128)(2,1)S(1)}, u32[]{:S(2)}, u32[]{:S(2)}) collective-permute-start(bf16[256,384]{1,0:T(8,128)(2,1)S(1)} %get-tuple-element.56), channel_id=1, source_target_pairs={{0,4},{4,8},{8,12},{12,14},{14,10},{10,6},{6,2},{2,0},{5,1},{9,5},... | collective-permute-start | bytes 589832 | tf_op jit(solution)/shard_map/ppermute | solution.py:315
  33.7 4.1 %collective-permute-start.16 = (bf16[256,384]{1,0:T(8,128)(2,1)S(1)}, bf16[256,384]{1,0:T(8,128)(2,1)S(1)}, u32[]{:S(2)}, u32[]{:S(2)}) collective-permute-start(bf16[256,384]{1,0:T(8,128)(2,1)S(1)} %get-tuple-element.53), channel_id=1, source_target_pairs={{0,1},{1,0},{2,3},{3,2},{4,5},{5,4},{6,7},{7,6},{8,9},{9,8},{10,11... | collective-permute-start | bytes 589832 | tf_op jit(solution)/shard_map/ppermute | solution.py:311
  33.8 4.0 %collective-permute-start.17 = (bf16[256,384]{1,0:T(8,128)(2,1)S(1)}, bf16[256,384]{1,0:T(8,128)(2,1)S(1)}, u32[]{:S(2)}, u32[]{:S(2)}) collective-permute-start(bf16[256,384]{1,0:T(8,128)(2,1)S(1)} %get-tuple-element.54), channel_id=1, source_target_pairs={{0,1},{1,0},{2,3},{3,2},{4,5},{5,4},{6,7},{7,6},{8,9},{9,8},{10,11... | collective-permute-start | bytes 589832 | tf_op jit(solution)/shard_map/ppermute | solution.py:311
  35.7 2.7 %collective-permute-start.14 = (bf16[256,384]{1,0:T(8,128)(2,1)S(1)}, bf16[256,384]{1,0:T(8,128)(2,1)S(1)}, u32[]{:S(2)}, u32[]{:S(2)}) collective-permute-start(bf16[256,384]{1,0:T(8,128)(2,1)S(1)} %collective-permute-done.11.last_a), channel_id=1, source_target_pairs={{0,1},{1,0},{2,3},{3,2},{4,5},{5,4},{6,7},{7,6},{8,9},{9,8},{10,11... | collective-permute-start | bytes 589832 | tf_op jit(solution)/shard_map/ppermute | solution.py:320
  37.8 1.4 %collective-permute-start.13 = (bf16[256,384]{1,0:T(8,128)(2,1)S(1)}, bf16[256,384]{1,0:T(8,128)(2,1)S(1)}, u32[]{:S(2)}, u32[]{:S(2)}) collective-permute-start(bf16[256,384]{1,0:T(8,128)(2,1)S(1)} %collective-permute-done.10.last_b), channel_id=1, source_target_pairs={{0,1},{1,0},{2,3},{3,2},{4,5},{5,4},{6,7},{7,6},{8,9},{9,8},{10,11... | collective-permute-start | bytes 589832 | tf_op jit(solution)/shard_map/ppermute | solution.py:322

commit v8 on v7

--- a/solution.py
+++ b/solution.py
@@ -282,7 +282,7 @@
 
     own = half_transform(me, pairs, occ, tiles)
     blocks, other_blocks = [own], [lax.ppermute(own, "ao", across)]
-    first_other, vir = lax.optimization_barrier((other_blocks[0], vir))
+    first_other = other_blocks[0]
     own_w, other_w, last_w = windows(me, pairs, vir, count, chips)
     total, summed = None, 0
     for message in range(1, chips):

time: 40.3 us -> 40.3 us (level)
  no operation moved by 1% of the time
where the time goes in v8:
time: 40.3 us; the launch traced here: 40.2 us
  starting transfers between devices  17.5 us (43%)
  Pallas kernels  11.5 us (29%)
  waiting for transfers between devices  11 us (27%)
    ppermute x6, starting transfers between devices, on_device(): block = lax.ppermute(block, 'ao', onward)  12.7 us
    ppermute x6, waiting for transfers between devices, on_device(): block = lax.ppermute(block, 'ao', onward)  8.11 us
    pallas_call x7, Pallas kernels, add_blocks(): pl.pallas_call(functools.partial(add_kernel, k), in_specs=[vmem] * (4 + l...  3.66 us
    pallas_call x1, Pallas kernels, half_transform(): pl.pallas_call(half_kernel, in_specs=[pl.BlockSpec(memory_space=pltpu.SME...  3.62 us
    pallas_call x1, Pallas kernels, windows(): pl.pallas_call(functools.partial(window_kernel, count, chips), in_specs=[...  2.8 us
    ppermute x1, starting transfers between devices, on_device(): last_a = lax.ppermute(block[:half], 'ao', onward)  2.13 us
    ppermute x1, waiting for transfers between devices, on_device(): last_b = lax.ppermute(block[half:], 'ao', onward)  2.1 us
    ppermute x1, starting transfers between devices, on_device(): last_b = lax.ppermute(block[half:], 'ao', onward)  1.58 us
  transfers between devices with their start and end apart: 18, of which 8 were waited for; matrix products, arithmetic and copies ran while one was open for 0% of the time, Pallas kernels for 17%

profile of v8, /device:TPU:0, one launch (start us, length us, event | category | flops | bytes accessed | tf_op | source)
XLA Modules:
  0.0 40.2 jit_solution(14512034947984317835)
XLA Ops:
  0.0 3.6 %half_transform.1.block = bf16[512,384]{1,0:T(8,128)(2,1)S(1)} custom-call(s32[1]{0:T(128)} %bitcast.me, s32[2,64]{1,0:T(2,128)} %bitcast.5, bf16[8,6144]{1,0:T(8,128)(2,1)} %bitcast.7, bf16[4,128,64,128]{3,2,1,0:T(8,128)(2,1)} %tiles_ref.1), custom_call_target="tpu_custom_call" | custom-call | flops 603979776 | bytes 8388608 | tf_op jit(solution)/shard_map/half_transform/pallas_call | solution.py:102
  3.6 0.5 %collective-permute-start.3 = (bf16[512,384]{1,0:T(8,128)(2,1)S(1)}, bf16[512,384]{1,0:T(8,128)(2,1)S(1)}, u32[]{:S(2)}, u32[]{:S(2)}) collective-permute-start(bf16[512,384]{1,0:T(8,128)(2,1)S(1)} %half_transform.1.block), channel_id=1, source_target_pairs={{0,1},{1,0},{2,3},{3,2},{4,5},{5,4},{6,7},{7,6},{8,9},{9,8},{10,11... | collective-permute-start | bytes 1179656 | tf_op jit(solution)/shard_map/ppermute | solution.py:284
  4.1 2.6 %collective-permute-start = (bf16[512,384]{1,0:T(8,128)(2,1)S(1)}, bf16[512,384]{1,0:T(8,128)(2,1)S(1)}, u32[]{:S(2)}, u32[]{:S(2)}) collective-permute-start(bf16[512,384]{1,0:T(8,128)(2,1)S(1)} %half_transform.1.block), channel_id=1, source_target_pairs={{0,4},{4,8},{8,12},{12,14},{14,10},{10,6},{6,2},{2,0},{5,1},{9,5},... | collective-permute-start | bytes 1179656 | tf_op jit(solution)/shard_map/ppermute | solution.py:305
  6.8 0.0 collective-permute-done.3.other_block
  6.8 1.7 %collective-permute-start.4 = (bf16[512,384]{1,0:T(8,128)(2,1)S(1)}, bf16[512,384]{1,0:T(8,128)(2,1)S(1)}, u32[]{:S(2)}, u32[]{:S(2)}) collective-permute-start(bf16[512,384]{1,0:T(8,128)(2,1)S(1)} %collective-permute-done.3.other_block), channel_id=1, source_target_pairs={{0,4},{4,8},{8,12},{12,14},{14,10},{10,6},{6,2},{2,0},{5,1},{9,5},... | collective-permute-start | bytes 1179656 | tf_op jit(solution)/shard_map/ppermute | solution.py:305
  8.4 0.0 copy-done
  8.4 2.8 %vir_windows.1 = (bf16[304,2688]{1,0:T(8,128)(2,1)S(1)}, bf16[304,2688]{1,0:T(8,128)(2,1)S(1)}, bf16[304,768]{1,0:T(8,128)(2,1)S(1)}) custom-call(s32[1]{0:T(128)} %bitcast.me, s32[2,64]{1,0:T(2,128)S(1)} %bitcast.6, bf16[304,6144]{1,0:T(8,128)(2,1)S(1)} %bitcast.4), custom_call_target="tpu_custom_call" | custom-call | tf_op jit(solution)/shard_map/vir_windows/pallas_call | solution.py:178
  11.3 1.2 %collective-permute-done.block = bf16[512,384]{1,0:T(8,128)(2,1)S(1)} collective-permute-done((bf16[512,384]{1,0:T(8,128)(2,1)S(1)}, bf16[512,384]{1,0:T(8,128)(2,1)S(1)}, u32[]{:S(2)}, u32[]{:S(2)}) %collective-permute-start) | collective-permute-done | bytes 393248 | tf_op jit(solution)/shard_map/ppermute | solution.py:305
  12.5 0.0 collective-permute-start.2
  12.5 2.1 %collective-permute-start.1 = (bf16[512,384]{1,0:T(8,128)(2,1)S(1)}, bf16[512,384]{1,0:T(8,128)(2,1)S(1)}, u32[]{:S(2)}, u32[]{:S(2)}) collective-permute-start(bf16[512,384]{1,0:T(8,128)(2,1)S(1)} %collective-permute-done.block), channel_id=1, source_target_pairs={{0,4},{4,8},{8,12},{12,14},{14,10},{10,6},{6,2},{2,0},{5,1},{9,5},... | collective-permute-start | bytes 1179656 | tf_op jit(solution)/shard_map/ppermute | solution.py:305
  14.6 0.5 %add_blocks.7.refs_0_ = f32[304,512]{1,0:T(8,128)S(1)} custom-call(bf16[304,2688]{1,0:T(8,128)(2,1)S(1)} %get-tuple-element.32.own_w, bf16[304,2688]{1,0:T(8,128)(2,1)S(1)} %get-tuple-element.33.other_w, bf16[512,384]{1,0:T(8,128)(2,1)S(1)} %half_transform.1.block, bf16[512,384]{1,0:T(8,128)(2,1)S(1)} %collective-permute-done.3.other_block), custom_call_target="tpu_custom_call" | custom-call | tf_op jit(solution)/shard_map/add_blocks/pallas_call | solution.py:208
  15.1 1.6 %collective-permute-done.4.block = bf16[512,384]{1,0:T(8,128)(2,1)S(1)} collective-permute-done((bf16[512,384]{1,0:T(8,128)(2,1)S(1)}, bf16[512,384]{1,0:T(8,128)(2,1)S(1)}, u32[]{:S(2)}, u32[]{:S(2)}) %collective-permute-start.4) | collective-permute-done | bytes 393248 | tf_op jit(solution)/shard_map/ppermute | solution.py:305
  16.7 2.1 %collective-permute-start.7 = (bf16[512,384]{1,0:T(8,128)(2,1)S(1)}, bf16[512,384]{1,0:T(8,128)(2,1)S(1)}, u32[]{:S(2)}, u32[]{:S(2)}) collective-permute-start(bf16[512,384]{1,0:T(8,128)(2,1)S(1)} %collective-permute-done.4.block), channel_id=1, source_target_pairs={{0,4},{4,8},{8,12},{12,14},{14,10},{10,6},{6,2},{2,0},{5,1},{9,5},... | collective-permute-start | bytes 1179656 | tf_op jit(solution)/shard_map/ppermute | solution.py:305
  18.8 0.0 collective-permute-start.8
  18.8 0.0 collective-permute-done.2.other_block
  18.8 0.5 %add_blocks.8.refs_0_ = f32[304,512]{1,0:T(8,128)S(1)} custom-call(bf16[304,2688]{1,0:T(8,128)(2,1)S(1)} %get-tuple-element.32.own_w, bf16[304,2688]{1,0:T(8,128)(2,1)S(1)} %get-tuple-element.33.other_w, bf16[512,384]{1,0:T(8,128)(2,1)S(1)} %collective-permute-done.block, ...), custom_call_target="tpu_custom_call", output_to_operand_aliasing={{}: (4, {})} | custom-call | tf_op jit(solution)/shard_map/add_blocks/pallas_call | solution.py:208
  19.3 1.6 %collective-permute-done.1.block = bf16[512,384]{1,0:T(8,128)(2,1)S(1)} collective-permute-done((bf16[512,384]{1,0:T(8,128)(2,1)S(1)}, bf16[512,384]{1,0:T(8,128)(2,1)S(1)}, u32[]{:S(2)}, u32[]{:S(2)}) %collective-permute-start.1) | collective-permute-done | bytes 393248 | tf_op jit(solution)/shard_map/ppermute | solution.py:305
  20.9 2.1 %collective-permute-start.5 = (bf16[512,384]{1,0:T(8,128)(2,1)S(1)}, bf16[512,384]{1,0:T(8,128)(2,1)S(1)}, u32[]{:S(2)}, u32[]{:S(2)}) collective-permute-start(bf16[512,384]{1,0:T(8,128)(2,1)S(1)} %collective-permute-done.1.block), channel_id=1, source_target_pairs={{0,4},{4,8},{8,12},{12,14},{14,10},{10,6},{6,2},{2,0},{5,1},{9,5},... | collective-permute-start | bytes 1179656 | tf_op jit(solution)/shard_map/ppermute | solution.py:305
  23.0 0.0 collective-permute-start.6
  23.0 2.1 %collective-permute-done.7.block = bf16[512,384]{1,0:T(8,128)(2,1)S(1)} collective-permute-done((bf16[512,384]{1,0:T(8,128)(2,1)S(1)}, bf16[512,384]{1,0:T(8,128)(2,1)S(1)}, u32[]{:S(2)}, u32[]{:S(2)}) %collective-permute-start.7) | collective-permute-done | bytes 393248 | tf_op jit(solution)/shard_map/ppermute | solution.py:305
  25.1 0.0 collective-permute-start.9
  25.1 0.0 collective-permute-done.8.other_block
  25.1 0.5 %add_blocks.9.refs_0_ = f32[304,512]{1,0:T(8,128)S(1)} custom-call(bf16[304,2688]{1,0:T(8,128)(2,1)S(1)} %get-tuple-element.32.own_w, bf16[304,2688]{1,0:T(8,128)(2,1)S(1)} %get-tuple-element.33.other_w, bf16[512,384]{1,0:T(8,128)(2,1)S(1)} %collective-permute-done.4.block, ...), custom_call_target="tpu_custom_call", output_to_operand_aliasing={{}: (4, {})} | custom-call | tf_op jit(solution)/shard_map/add_blocks/pallas_call | solution.py:208
  25.7 2.1 %collective-permute-start.15 = (bf16[512,384]{1,0:T(8,128)(2,1)S(1)}, bf16[512,384]{1,0:T(8,128)(2,1)S(1)}, u32[]{:S(2)}, u32[]{:S(2)}) collective-permute-start(bf16[512,384]{1,0:T(8,128)(2,1)S(1)} %collective-permute-done.7.block), channel_id=1, source_target_pairs={{0,4},{4,8},{8,12},{12,14},{14,10},{10,6},{6,2},{2,0},{5,1},{9,5},... | collective-permute-start | bytes 1179656 | tf_op jit(solution)/shard_map/ppermute | solution.py:305
  27.8 1.5 %collective-permute-done.5.block = bf16[512,384]{1,0:T(8,128)(2,1)S(1)} collective-permute-done((bf16[512,384]{1,0:T(8,128)(2,1)S(1)}, bf16[512,384]{1,0:T(8,128)(2,1)S(1)}, u32[]{:S(2)}, u32[]{:S(2)}) %collective-permute-start.5) | collective-permute-done | bytes 393248 | tf_op jit(solution)/shard_map/ppermute | solution.py:305
  29.3 0.0 collective-permute-start.12
  29.3 0.0 collective-permute-done.6.other_block
  29.3 0.5 %add_blocks.10.refs_0_ = f32[304,512]{1,0:T(8,128)S(1)} custom-call(bf16[304,2688]{1,0:T(8,128)(2,1)S(1)} %get-tuple-element.32.own_w, bf16[304,2688]{1,0:T(8,128)(2,1)S(1)} %get-tuple-element.33.other_w, bf16[512,384]{1,0:T(8,128)(2,1)S(1)} %collective-permute-done.1.block, ...), custom_call_target="tpu_custom_call", output_to_operand_aliasing={{}: (4, {})} | custom-call | tf_op jit(solution)/shard_map/add_blocks/pallas_call | solution.py:208
  29.9 0.0 collective-permute-done.9.other_block
  29.9 2.1 %collective-permute-start.11 = (bf16[256,384]{1,0:T(8,128)(2,1)S(1)}, bf16[256,384]{1,0:T(8,128)(2,1)S(1)}, u32[]{:S(2)}, u32[]{:S(2)}) collective-permute-start(bf16[256,384]{1,0:T(8,128)(2,1)S(1)} %get-tuple-element.51), channel_id=1, source_target_pairs={{0,4},{4,8},{8,12},{12,14},{14,10},{10,6},{6,2},{2,0},{5,1},{9,5},... | collective-permute-start | bytes 589832 | tf_op jit(solution)/shard_map/ppermute | solution.py:314
  32.1 1.6 %collective-permute-start.10 = (bf16[256,384]{1,0:T(8,128)(2,1)S(1)}, bf16[256,384]{1,0:T(8,128)(2,1)S(1)}, u32[]{:S(2)}, u32[]{:S(2)}) collective-permute-start(bf16[256,384]{1,0:T(8,128)(2,1)S(1)} %get-tuple-element.52), channel_id=1, source_target_pairs={{0,4},{4,8},{8,12},{12,14},{14,10},{10,6},{6,2},{2,0},{5,1},{9,5},... | collective-permute-start | bytes 589832 | tf_op jit(solution)/shard_map/ppermute | solution.py:315
  33.6 0.0 collective-permute-done.15.block
  33.7 0.1 collective-permute-start.16
  33.8 0.5 %collective-permute-start.17 = (bf16[256,384]{1,0:T(8,128)(2,1)S(1)}, bf16[256,384]{1,0:T(8,128)(2,1)S(1)}, u32[]{:S(2)}, u32[]{:S(2)}) collective-permute-start(bf16[256,384]{1,0:T(8,128)(2,1)S(1)} %get-tuple-element.50), channel_id=1, source_target_pairs={{0,1},{1,0},{2,3},{3,2},{4,5},{5,4},{6,7},{7,6},{8,9},{9,8},{10,11... | collective-permute-start | bytes 589832 | tf_op jit(solution)/shard_map/ppermute | solution.py:311
  34.3 0.5 %add_blocks.11.refs_0_ = f32[304,512]{1,0:T(8,128)S(1)} custom-call(bf16[304,2688]{1,0:T(8,128)(2,1)S(1)} %get-tuple-element.32.own_w, bf16[304,2688]{1,0:T(8,128)(2,1)S(1)} %get-tuple-element.33.other_w, bf16[512,384]{1,0:T(8,128)(2,1)S(1)} %collective-permute-done.7.block, ...), custom_call_target="tpu_custom_call", output_to_operand_aliasing={{}: (4, {})} | custom-call | tf_op jit(solution)/shard_map/add_blocks/pallas_call | solution.py:208
  34.8 0.0 collective-permute-done.12.other_block
  34.8 0.5 %add_blocks.12.refs_0_ = f32[304,512]{1,0:T(8,128)S(1)} custom-call(bf16[304,2688]{1,0:T(8,128)(2,1)S(1)} %get-tuple-element.32.own_w, bf16[304,2688]{1,0:T(8,128)(2,1)S(1)} %get-tuple-element.33.other_w, bf16[512,384]{1,0:T(8,128)(2,1)S(1)} %collective-permute-done.5.block, ...), custom_call_target="tpu_custom_call", output_to_operand_aliasing={{}: (4, {})} | custom-call | tf_op jit(solution)/shard_map/add_blocks/pallas_call | solution.py:208
  35.3 0.3 collective-permute-done.11.last_a
  35.7 0.0 collective-permute-start.14
  35.7 2.1 %collective-permute-done.10.last_b = bf16[256,384]{1,0:T(8,128)(2,1)S(1)} collective-permute-done((bf16[256,384]{1,0:T(8,128)(2,1)S(1)}, bf16[256,384]{1,0:T(8,128)(2,1)S(1)}, u32[]{:S(2)}, u32[]{:S(2)}) %collective-permute-start.10) | collective-permute-done | bytes 196640 | tf_op jit(solution)/shard_map/ppermute | solution.py:315
  37.8 0.0 collective-permute-start.13
  37.8 0.0 collective-permute-done.16
  37.8 0.0 collective-permute-done.17
  37.8 0.5 %add_blocks.13.before = f32[304,512]{1,0:T(8,128)S(1)} custom-call(bf16[304,2688]{1,0:T(8,128)(2,1)S(1)} %get-tuple-element.32.own_w, bf16[304,2688]{1,0:T(8,128)(2,1)S(1)} %get-tuple-element.33.other_w, bf16[512,384]{1,0:T(8,128)(2,1)S(1)} %collective-permute-done.15.block, ...), custom_call_target="tpu_custom_call", output_to_operand_aliasing={{}: (4, {})} | custom-call | tf_op jit(solution)/shard_map/add_blocks/pallas_call | solution.py:208
  38.4 0.0 collective-permute-done.14.other_a
  38.4 0.4 %add_last.1 = (bf16[304,256]{1,0:T(8,128)(2,1)S(1)}, f32[304,256]{1,0:T(8,128)S(1)}) custom-call(bf16[304,768]{1,0:T(8,128)(2,1)S(1)} %get-tuple-element.30.last_w, bf16[256,384]{1,0:T(8,128)(2,1)S(1)} %collective-permute-done.11.last_a, bf16[256,384]{1,0:T(8,128)(2,1)S(1)} %collective-permute-done.10.last_b, ...), custom_call_target="tpu_custom_call" | custom-call | tf_op jit(solution)/shard_map/add_last/pallas_call | solution.py:231
  38.8 0.4 %collective-permute-done.13.block = bf16[256,384]{1,0:T(8,128)(2,1)S(1)} collective-permute-done((bf16[256,384]{1,0:T(8,128)(2,1)S(1)}, bf16[256,384]{1,0:T(8,128)(2,1)S(1)}, u32[]{:S(2)}, u32[]{:S(2)}) %collective-permute-start.13) | collective-permute-done | bytes 196640 | tf_op jit(solution)/shard_map/ppermute | solution.py:322
  39.2 1.0 %finish.1 = bf16[304,512]{1,0:T(8,128)(2,1)} custom-call(bf16[304,768]{1,0:T(8,128)(2,1)S(1)} %get-tuple-element.30.last_w, bf16[256,384]{1,0:T(8,128)(2,1)S(1)} %collective-permute-done.13.block, bf16[304,256]{1,0:T(8,128)(2,1)S(1)} %get-tuple-element.47.done, f32[304,256]{1,0:T(8,128)S(1)} %get-tuple-element.48.rest), custom_call_target="tpu_custom_call" | custom-call | tf_op jit(solution)/shard_map/finish/pallas_call | solution.py:260
  (6 shorter events, 0.1 us)
Async XLA Ops:
  0.0 8.4 %copy-start = (bf16[6144,304]{0,1:T(8,128)(2,1)S(1)}, bf16[6144,304]{0,1:T(8,128)(2,1)}, u32[]{:S(2)}) copy-start(bf16[6144,304]{0,1:T(8,128)(2,1)} %param.7) | copy-start | bytes 11206660
  0.0 8.4 %copy-start.1 = (s32[64,2]{0,1:T(2,128)S(1)}, s32[64,2]{0,1:T(2,128)}, u32[]{:S(2)}) copy-start(s32[64,2]{0,1:T(2,128)} %param.5) | copy-start | bytes 1540
  3.6 3.2 %collective-permute-start.3 = (bf16[512,384]{1,0:T(8,128)(2,1)S(1)}, bf16[512,384]{1,0:T(8,128)(2,1)S(1)}, u32[]{:S(2)}, u32[]{:S(2)}) collective-permute-start(bf16[512,384]{1,0:T(8,128)(2,1)S(1)} %half_transform.1.block), channel_id=1, source_target_pairs={{0,1},{1,0},{2,3},{3,2},{4,5},{5,4},{6,7},{7,6},{8,9},{9,8},{10,11... | collective-permute-start | bytes 1179656 | tf_op jit(solution)/shard_map/ppermute | solution.py:284
  4.1 8.3 %collective-permute-start = (bf16[512,384]{1,0:T(8,128)(2,1)S(1)}, bf16[512,384]{1,0:T(8,128)(2,1)S(1)}, u32[]{:S(2)}, u32[]{:S(2)}) collective-permute-start(bf16[512,384]{1,0:T(8,128)(2,1)S(1)} %half_transform.1.block), channel_id=1, source_target_pairs={{0,4},{4,8},{8,12},{12,14},{14,10},{10,6},{6,2},{2,0},{5,1},{9,5},... | collective-permute-start | bytes 1179656 | tf_op jit(solution)/shard_map/ppermute | solution.py:305
  6.8 9.9 %collective-permute-start.4 = (bf16[512,384]{1,0:T(8,128)(2,1)S(1)}, bf16[512,384]{1,0:T(8,128)(2,1)S(1)}, u32[]{:S(2)}, u32[]{:S(2)}) collective-permute-start(bf16[512,384]{1,0:T(8,128)(2,1)S(1)} %collective-permute-done.3.other_block), channel_id=1, source_target_pairs={{0,4},{4,8},{8,12},{12,14},{14,10},{10,6},{6,2},{2,0},{5,1},{9,5},... | collective-permute-start | bytes 1179656 | tf_op jit(solution)/shard_map/ppermute | solution.py:305
  12.5 6.3 %collective-permute-start.2 = (bf16[512,384]{1,0:T(8,128)(2,1)S(1)}, bf16[512,384]{1,0:T(8,128)(2,1)S(1)}, u32[]{:S(2)}, u32[]{:S(2)}) collective-permute-start(bf16[512,384]{1,0:T(8,128)(2,1)S(1)} %collective-permute-done.block), channel_id=1, source_target_pairs={{0,1},{1,0},{2,3},{3,2},{4,5},{5,4},{6,7},{7,6},{8,9},{9,8},{10,11... | collective-permute-start | bytes 1179656 | tf_op jit(solution)/shard_map/ppermute | solution.py:308
  12.5 8.4 %collective-permute-start.1 = (bf16[512,384]{1,0:T(8,128)(2,1)S(1)}, bf16[512,384]{1,0:T(8,128)(2,1)S(1)}, u32[]{:S(2)}, u32[]{:S(2)}) collective-permute-start(bf16[512,384]{1,0:T(8,128)(2,1)S(1)} %collective-permute-done.block), channel_id=1, source_target_pairs={{0,4},{4,8},{8,12},{12,14},{14,10},{10,6},{6,2},{2,0},{5,1},{9,5},... | collective-permute-start | bytes 1179656 | tf_op jit(solution)/shard_map/ppermute | solution.py:305
  16.7 8.4 %collective-permute-start.7 = (bf16[512,384]{1,0:T(8,128)(2,1)S(1)}, bf16[512,384]{1,0:T(8,128)(2,1)S(1)}, u32[]{:S(2)}, u32[]{:S(2)}) collective-permute-start(bf16[512,384]{1,0:T(8,128)(2,1)S(1)} %collective-permute-done.4.block), channel_id=1, source_target_pairs={{0,4},{4,8},{8,12},{12,14},{14,10},{10,6},{6,2},{2,0},{5,1},{9,5},... | collective-permute-start | bytes 1179656 | tf_op jit(solution)/shard_map/ppermute | solution.py:305
  18.8 6.4 %collective-permute-start.8 = (bf16[512,384]{1,0:T(8,128)(2,1)S(1)}, bf16[512,384]{1,0:T(8,128)(2,1)S(1)}, u32[]{:S(2)}, u32[]{:S(2)}) collective-permute-start(bf16[512,384]{1,0:T(8,128)(2,1)S(1)} %collective-permute-done.4.block), channel_id=1, source_target_pairs={{0,1},{1,0},{2,3},{3,2},{4,5},{5,4},{6,7},{7,6},{8,9},{9,8},{10,11... | collective-permute-start | bytes 1179656 | tf_op jit(solution)/shard_map/ppermute | solution.py:308
  20.9 8.4 %collective-permute-start.5 = (bf16[512,384]{1,0:T(8,128)(2,1)S(1)}, bf16[512,384]{1,0:T(8,128)(2,1)S(1)}, u32[]{:S(2)}, u32[]{:S(2)}) collective-permute-start(bf16[512,384]{1,0:T(8,128)(2,1)S(1)} %collective-permute-done.1.block), channel_id=1, source_target_pairs={{0,4},{4,8},{8,12},{12,14},{14,10},{10,6},{6,2},{2,0},{5,1},{9,5},... | collective-permute-start | bytes 1179656 | tf_op jit(solution)/shard_map/ppermute | solution.py:305
  23.0 6.4 %collective-permute-start.6 = (bf16[512,384]{1,0:T(8,128)(2,1)S(1)}, bf16[512,384]{1,0:T(8,128)(2,1)S(1)}, u32[]{:S(2)}, u32[]{:S(2)}) collective-permute-start(bf16[512,384]{1,0:T(8,128)(2,1)S(1)} %collective-permute-done.1.block), channel_id=1, source_target_pairs={{0,1},{1,0},{2,3},{3,2},{4,5},{5,4},{6,7},{7,6},{8,9},{9,8},{10,11... | collective-permute-start | bytes 1179656 | tf_op jit(solution)/shard_map/ppermute | solution.py:308
  25.1 4.8 %collective-permute-start.9 = (bf16[512,384]{1,0:T(8,128)(2,1)S(1)}, bf16[512,384]{1,0:T(8,128)(2,1)S(1)}, u32[]{:S(2)}, u32[]{:S(2)}) collective-permute-start(bf16[512,384]{1,0:T(8,128)(2,1)S(1)} %collective-permute-done.7.block), channel_id=1, source_target_pairs={{0,1},{1,0},{2,3},{3,2},{4,5},{5,4},{6,7},{7,6},{8,9},{9,8},{10,11... | collective-permute-start | bytes 1179656 | tf_op jit(solution)/shard_map/ppermute | solution.py:308
  25.7 8.0 %collective-permute-start.15 = (bf16[512,384]{1,0:T(8,128)(2,1)S(1)}, bf16[512,384]{1,0:T(8,128)(2,1)S(1)}, u32[]{:S(2)}, u32[]{:S(2)}) collective-permute-start(bf16[512,384]{1,0:T(8,128)(2,1)S(1)} %collective-permute-done.7.block), channel_id=1, source_target_pairs={{0,4},{4,8},{8,12},{12,14},{14,10},{10,6},{6,2},{2,0},{5,1},{9,5},... | collective-permute-start | bytes 1179656 | tf_op jit(solution)/shard_map/ppermute | solution.py:305
  29.3 5.5 %collective-permute-start.12 = (bf16[512,384]{1,0:T(8,128)(2,1)S(1)}, bf16[512,384]{1,0:T(8,128)(2,1)S(1)}, u32[]{:S(2)}, u32[]{:S(2)}) collective-permute-start(bf16[512,384]{1,0:T(8,128)(2,1)S(1)} %collective-permute-done.5.block), channel_id=1, source_target_pairs={{0,1},{1,0},{2,3},{3,2},{4,5},{5,4},{6,7},{7,6},{8,9},{9,8},{10,11... | collective-permute-start | bytes 1179656 | tf_op jit(solution)/shard_map/ppermute | solution.py:308
  29.9 5.7 %collective-permute-start.11 = (bf16[256,384]{1,0:T(8,128)(2,1)S(1)}, bf16[256,384]{1,0:T(8,128)(2,1)S(1)}, u32[]{:S(2)}, u32[]{:S(2)}) collective-permute-start(bf16[256,384]{1,0:T(8,128)(2,1)S(1)} %get-tuple-element.51), channel_id=1, source_target_pairs={{0,4},{4,8},{8,12},{12,14},{14,10},{10,6},{6,2},{2,0},{5,1},{9,5},... | collective-permute-start | bytes 589832 | tf_op jit(solution)/shard_map/ppermute | solution.py:314
  32.1 5.7 %collective-permute-start.10 = (bf16[256,384]{1,0:T(8,128)(2,1)S(1)}, bf16[256,384]{1,0:T(8,128)(2,1)S(1)}, u32[]{:S(2)}, u32[]{:S(2)}) collective-permute-start(bf16[256,384]{1,0:T(8,128)(2,1)S(1)} %get-tuple-element.52), channel_id=1, source_target_pairs={{0,4},{4,8},{8,12},{12,14},{14,10},{10,6},{6,2},{2,0},{5,1},{9,5},... | collective-permute-start | bytes 589832 | tf_op jit(solution)/shard_map/ppermute | solution.py:315
  33.7 4.1 %collective-permute-start.16 = (bf16[256,384]{1,0:T(8,128)(2,1)S(1)}, bf16[256,384]{1,0:T(8,128)(2,1)S(1)}, u32[]{:S(2)}, u32[]{:S(2)}) collective-permute-start(bf16[256,384]{1,0:T(8,128)(2,1)S(1)} %get-tuple-element.49), channel_id=1, source_target_pairs={{0,1},{1,0},{2,3},{3,2},{4,5},{5,4},{6,7},{7,6},{8,9},{9,8},{10,11... | collective-permute-start | bytes 589832 | tf_op jit(solution)/shard_map/ppermute | solution.py:311
  33.8 4.0 %collective-permute-start.17 = (bf16[256,384]{1,0:T(8,128)(2,1)S(1)}, bf16[256,384]{1,0:T(8,128)(2,1)S(1)}, u32[]{:S(2)}, u32[]{:S(2)}) collective-permute-start(bf16[256,384]{1,0:T(8,128)(2,1)S(1)} %get-tuple-element.50), channel_id=1, source_target_pairs={{0,1},{1,0},{2,3},{3,2},{4,5},{5,4},{6,7},{7,6},{8,9},{9,8},{10,11... | collective-permute-start | bytes 589832 | tf_op jit(solution)/shard_map/ppermute | solution.py:311
  35.7 2.7 %collective-permute-start.14 = (bf16[256,384]{1,0:T(8,128)(2,1)S(1)}, bf16[256,384]{1,0:T(8,128)(2,1)S(1)}, u32[]{:S(2)}, u32[]{:S(2)}) collective-permute-start(bf16[256,384]{1,0:T(8,128)(2,1)S(1)} %collective-permute-done.11.last_a), channel_id=1, source_target_pairs={{0,1},{1,0},{2,3},{3,2},{4,5},{5,4},{6,7},{7,6},{8,9},{9,8},{10,11... | collective-permute-start | bytes 589832 | tf_op jit(solution)/shard_map/ppermute | solution.py:320
  37.8 1.4 %collective-permute-start.13 = (bf16[256,384]{1,0:T(8,128)(2,1)S(1)}, bf16[256,384]{1,0:T(8,128)(2,1)S(1)}, u32[]{:S(2)}, u32[]{:S(2)}) collective-permute-start(bf16[256,384]{1,0:T(8,128)(2,1)S(1)} %collective-permute-done.10.last_b), channel_id=1, source_target_pairs={{0,1},{1,0},{2,3},{3,2},{4,5},{5,4},{6,7},{7,6},{8,9},{9,8},{10,11... | collective-permute-start | bytes 589832 | tf_op jit(solution)/shard_map/ppermute | solution.py:322

commit v9 on v8

--- a/solution.py
+++ b/solution.py
@@ -185,7 +185,7 @@
             jax.ShapeDtypeStruct((rows, 2 * columns), vir.dtype),
         ],
         compiler_params=pltpu.CompilerParams(vmem_limit_bytes=STEP_VMEM),
-        cost_estimate=UNTIMED,
+        cost_estimate=pl.CostEstimate(flops=0, bytes_accessed=4 * vir.size, transcendentals=0),
         name="vir_windows",
     )(me, pairs, vir)
 

time: 40.3 us -> 40.3 us (level)
  no operation moved by 1% of the time
where the time goes in v9:
time: 40.3 us; the launch traced here: 40.2 us
  starting transfers between devices  17.5 us (43%)
  Pallas kernels  11.5 us (29%)
  waiting for transfers between devices  11 us (27%)
    ppermute x6, starting transfers between devices, on_device(): block = lax.ppermute(block, 'ao', onward)  12.7 us
    ppermute x6, waiting for transfers between devices, on_device(): block = lax.ppermute(block, 'ao', onward)  8.11 us
    pallas_call x7, Pallas kernels, add_blocks(): pl.pallas_call(functools.partial(add_kernel, k), in_specs=[vmem] * (4 + l...  3.66 us
    pallas_call x1, Pallas kernels, half_transform(): pl.pallas_call(half_kernel, in_specs=[pl.BlockSpec(memory_space=pltpu.SME...  3.62 us
    pallas_call x1, Pallas kernels, windows(): pl.pallas_call(functools.partial(window_kernel, count, chips), in_specs=[...  2.8 us
    ppermute x1, starting transfers between devices, on_device(): last_a = lax.ppermute(block[:half], 'ao', onward)  2.13 us
    ppermute x1, waiting for transfers between devices, on_device(): last_b = lax.ppermute(block[half:], 'ao', onward)  2.1 us
    ppermute x1, starting transfers between devices, on_device(): last_b = lax.ppermute(block[half:], 'ao', onward)  1.58 us
  transfers between devices with their start and end apart: 18, of which 8 were waited for; matrix products, arithmetic and copies ran while one was open for 0% of the time, Pallas kernels for 17%

profile of v9, /device:TPU:0, one launch (start us, length us, event | category | flops | bytes accessed | tf_op | source)
XLA Modules:
  0.0 40.2 jit_solution(14512034947984317835)
XLA Ops:
  0.0 3.6 %half_transform.1.block = bf16[512,384]{1,0:T(8,128)(2,1)S(1)} custom-call(s32[1]{0:T(128)} %bitcast.me, s32[2,64]{1,0:T(2,128)} %bitcast.5, bf16[8,6144]{1,0:T(8,128)(2,1)} %bitcast.7, bf16[4,128,64,128]{3,2,1,0:T(8,128)(2,1)} %tiles_ref.1), custom_call_target="tpu_custom_call" | custom-call | flops 603979776 | bytes 8388608 | tf_op jit(solution)/shard_map/half_transform/pallas_call | solution.py:102
  3.6 0.5 %collective-permute-start.3 = (bf16[512,384]{1,0:T(8,128)(2,1)S(1)}, bf16[512,384]{1,0:T(8,128)(2,1)S(1)}, u32[]{:S(2)}, u32[]{:S(2)}) collective-permute-start(bf16[512,384]{1,0:T(8,128)(2,1)S(1)} %half_transform.1.block), channel_id=1, source_target_pairs={{0,1},{1,0},{2,3},{3,2},{4,5},{5,4},{6,7},{7,6},{8,9},{9,8},{10,11... | collective-permute-start | bytes 1179656 | tf_op jit(solution)/shard_map/ppermute | solution.py:284
  4.1 2.6 %collective-permute-start = (bf16[512,384]{1,0:T(8,128)(2,1)S(1)}, bf16[512,384]{1,0:T(8,128)(2,1)S(1)}, u32[]{:S(2)}, u32[]{:S(2)}) collective-permute-start(bf16[512,384]{1,0:T(8,128)(2,1)S(1)} %half_transform.1.block), channel_id=1, source_target_pairs={{0,4},{4,8},{8,12},{12,14},{14,10},{10,6},{6,2},{2,0},{5,1},{9,5},... | collective-permute-start | bytes 1179656 | tf_op jit(solution)/shard_map/ppermute | solution.py:305
  6.8 0.0 collective-permute-done.3.other_block
  6.8 1.7 %collective-permute-start.4 = (bf16[512,384]{1,0:T(8,128)(2,1)S(1)}, bf16[512,384]{1,0:T(8,128)(2,1)S(1)}, u32[]{:S(2)}, u32[]{:S(2)}) collective-permute-start(bf16[512,384]{1,0:T(8,128)(2,1)S(1)} %collective-permute-done.3.other_block), channel_id=1, source_target_pairs={{0,4},{4,8},{8,12},{12,14},{14,10},{10,6},{6,2},{2,0},{5,1},{9,5},... | collective-permute-start | bytes 1179656 | tf_op jit(solution)/shard_map/ppermute | solution.py:305
  8.4 0.0 copy-done
  8.4 2.8 %vir_windows.1 = (bf16[304,2688]{1,0:T(8,128)(2,1)S(1)}, bf16[304,2688]{1,0:T(8,128)(2,1)S(1)}, bf16[304,768]{1,0:T(8,128)(2,1)S(1)}) custom-call(s32[1]{0:T(128)} %bitcast.me, s32[2,64]{1,0:T(2,128)S(1)} %bitcast.6, bf16[304,6144]{1,0:T(8,128)(2,1)S(1)} %bitcast.4), custom_call_target="tpu_custom_call" | custom-call | bytes 7471104 | tf_op jit(solution)/shard_map/vir_windows/pallas_call | solution.py:178
  11.3 1.2 %collective-permute-done.block = bf16[512,384]{1,0:T(8,128)(2,1)S(1)} collective-permute-done((bf16[512,384]{1,0:T(8,128)(2,1)S(1)}, bf16[512,384]{1,0:T(8,128)(2,1)S(1)}, u32[]{:S(2)}, u32[]{:S(2)}) %collective-permute-start) | collective-permute-done | bytes 393248 | tf_op jit(solution)/shard_map/ppermute | solution.py:305
  12.5 0.0 collective-permute-start.2
  12.5 2.1 %collective-permute-start.1 = (bf16[512,384]{1,0:T(8,128)(2,1)S(1)}, bf16[512,384]{1,0:T(8,128)(2,1)S(1)}, u32[]{:S(2)}, u32[]{:S(2)}) collective-permute-start(bf16[512,384]{1,0:T(8,128)(2,1)S(1)} %collective-permute-done.block), channel_id=1, source_target_pairs={{0,4},{4,8},{8,12},{12,14},{14,10},{10,6},{6,2},{2,0},{5,1},{9,5},... | collective-permute-start | bytes 1179656 | tf_op jit(solution)/shard_map/ppermute | solution.py:305
  14.6 0.5 %add_blocks.7.refs_0_ = f32[304,512]{1,0:T(8,128)S(1)} custom-call(bf16[304,2688]{1,0:T(8,128)(2,1)S(1)} %get-tuple-element.32.own_w, bf16[304,2688]{1,0:T(8,128)(2,1)S(1)} %get-tuple-element.33.other_w, bf16[512,384]{1,0:T(8,128)(2,1)S(1)} %half_transform.1.block, bf16[512,384]{1,0:T(8,128)(2,1)S(1)} %collective-permute-done.3.other_block), custom_call_target="tpu_custom_call" | custom-call | tf_op jit(solution)/shard_map/add_blocks/pallas_call | solution.py:208
  15.1 1.6 %collective-permute-done.4.block = bf16[512,384]{1,0:T(8,128)(2,1)S(1)} collective-permute-done((bf16[512,384]{1,0:T(8,128)(2,1)S(1)}, bf16[512,384]{1,0:T(8,128)(2,1)S(1)}, u32[]{:S(2)}, u32[]{:S(2)}) %collective-permute-start.4) | collective-permute-done | bytes 393248 | tf_op jit(solution)/shard_map/ppermute | solution.py:305
  16.7 2.1 %collective-permute-start.7 = (bf16[512,384]{1,0:T(8,128)(2,1)S(1)}, bf16[512,384]{1,0:T(8,128)(2,1)S(1)}, u32[]{:S(2)}, u32[]{:S(2)}) collective-permute-start(bf16[512,384]{1,0:T(8,128)(2,1)S(1)} %collective-permute-done.4.block), channel_id=1, source_target_pairs={{0,4},{4,8},{8,12},{12,14},{14,10},{10,6},{6,2},{2,0},{5,1},{9,5},... | collective-permute-start | bytes 1179656 | tf_op jit(solution)/shard_map/ppermute | solution.py:305
  18.8 0.0 collective-permute-start.8
  18.8 0.0 collective-permute-done.2.other_block
  18.8 0.5 %add_blocks.8.refs_0_ = f32[304,512]{1,0:T(8,128)S(1)} custom-call(bf16[304,2688]{1,0:T(8,128)(2,1)S(1)} %get-tuple-element.32.own_w, bf16[304,2688]{1,0:T(8,128)(2,1)S(1)} %get-tuple-element.33.other_w, bf16[512,384]{1,0:T(8,128)(2,1)S(1)} %collective-permute-done.block, ...), custom_call_target="tpu_custom_call", output_to_operand_aliasing={{}: (4, {})} | custom-call | tf_op jit(solution)/shard_map/add_blocks/pallas_call | solution.py:208
  19.3 1.6 %collective-permute-done.1.block = bf16[512,384]{1,0:T(8,128)(2,1)S(1)} collective-permute-done((bf16[512,384]{1,0:T(8,128)(2,1)S(1)}, bf16[512,384]{1,0:T(8,128)(2,1)S(1)}, u32[]{:S(2)}, u32[]{:S(2)}) %collective-permute-start.1) | collective-permute-done | bytes 393248 | tf_op jit(solution)/shard_map/ppermute | solution.py:305
  20.9 2.1 %collective-permute-start.5 = (bf16[512,384]{1,0:T(8,128)(2,1)S(1)}, bf16[512,384]{1,0:T(8,128)(2,1)S(1)}, u32[]{:S(2)}, u32[]{:S(2)}) collective-permute-start(bf16[512,384]{1,0:T(8,128)(2,1)S(1)} %collective-permute-done.1.block), channel_id=1, source_target_pairs={{0,4},{4,8},{8,12},{12,14},{14,10},{10,6},{6,2},{2,0},{5,1},{9,5},... | collective-permute-start | bytes 1179656 | tf_op jit(solution)/shard_map/ppermute | solution.py:305
  23.0 0.0 collective-permute-start.6
  23.0 2.1 %collective-permute-done.7.block = bf16[512,384]{1,0:T(8,128)(2,1)S(1)} collective-permute-done((bf16[512,384]{1,0:T(8,128)(2,1)S(1)}, bf16[512,384]{1,0:T(8,128)(2,1)S(1)}, u32[]{:S(2)}, u32[]{:S(2)}) %collective-permute-start.7) | collective-permute-done | bytes 393248 | tf_op jit(solution)/shard_map/ppermute | solution.py:305
  25.1 0.0 collective-permute-start.9
  25.1 0.0 collective-permute-done.8.other_block
  25.1 0.5 %add_blocks.9.refs_0_ = f32[304,512]{1,0:T(8,128)S(1)} custom-call(bf16[304,2688]{1,0:T(8,128)(2,1)S(1)} %get-tuple-element.32.own_w, bf16[304,2688]{1,0:T(8,128)(2,1)S(1)} %get-tuple-element.33.other_w, bf16[512,384]{1,0:T(8,128)(2,1)S(1)} %collective-permute-done.4.block, ...), custom_call_target="tpu_custom_call", output_to_operand_aliasing={{}: (4, {})} | custom-call | tf_op jit(solution)/shard_map/add_blocks/pallas_call | solution.py:208
  25.7 2.1 %collective-permute-start.15 = (bf16[512,384]{1,0:T(8,128)(2,1)S(1)}, bf16[512,384]{1,0:T(8,128)(2,1)S(1)}, u32[]{:S(2)}, u32[]{:S(2)}) collective-permute-start(bf16[512,384]{1,0:T(8,128)(2,1)S(1)} %collective-permute-done.7.block), channel_id=1, source_target_pairs={{0,4},{4,8},{8,12},{12,14},{14,10},{10,6},{6,2},{2,0},{5,1},{9,5},... | collective-permute-start | bytes 1179656 | tf_op jit(solution)/shard_map/ppermute | solution.py:305
  27.8 1.5 %collective-permute-done.5.block = bf16[512,384]{1,0:T(8,128)(2,1)S(1)} collective-permute-done((bf16[512,384]{1,0:T(8,128)(2,1)S(1)}, bf16[512,384]{1,0:T(8,128)(2,1)S(1)}, u32[]{:S(2)}, u32[]{:S(2)}) %collective-permute-start.5) | collective-permute-done | bytes 393248 | tf_op jit(solution)/shard_map/ppermute | solution.py:305
  29.3 0.0 collective-permute-start.12
  29.3 0.0 collective-permute-done.6.other_block
  29.3 0.5 %add_blocks.10.refs_0_ = f32[304,512]{1,0:T(8,128)S(1)} custom-call(bf16[304,2688]{1,0:T(8,128)(2,1)S(1)} %get-tuple-element.32.own_w, bf16[304,2688]{1,0:T(8,128)(2,1)S(1)} %get-tuple-element.33.other_w, bf16[512,384]{1,0:T(8,128)(2,1)S(1)} %collective-permute-done.1.block, ...), custom_call_target="tpu_custom_call", output_to_operand_aliasing={{}: (4, {})} | custom-call | tf_op jit(solution)/shard_map/add_blocks/pallas_call | solution.py:208
  29.9 0.0 collective-permute-done.9.other_block
  29.9 2.1 %collective-permute-start.11 = (bf16[256,384]{1,0:T(8,128)(2,1)S(1)}, bf16[256,384]{1,0:T(8,128)(2,1)S(1)}, u32[]{:S(2)}, u32[]{:S(2)}) collective-permute-start(bf16[256,384]{1,0:T(8,128)(2,1)S(1)} %get-tuple-element.51), channel_id=1, source_target_pairs={{0,4},{4,8},{8,12},{12,14},{14,10},{10,6},{6,2},{2,0},{5,1},{9,5},... | collective-permute-start | bytes 589832 | tf_op jit(solution)/shard_map/ppermute | solution.py:314
  32.1 1.6 %collective-permute-start.10 = (bf16[256,384]{1,0:T(8,128)(2,1)S(1)}, bf16[256,384]{1,0:T(8,128)(2,1)S(1)}, u32[]{:S(2)}, u32[]{:S(2)}) collective-permute-start(bf16[256,384]{1,0:T(8,128)(2,1)S(1)} %get-tuple-element.52), channel_id=1, source_target_pairs={{0,4},{4,8},{8,12},{12,14},{14,10},{10,6},{6,2},{2,0},{5,1},{9,5},... | collective-permute-start | bytes 589832 | tf_op jit(solution)/shard_map/ppermute | solution.py:315
  33.6 0.0 collective-permute-done.15.block
  33.7 0.1 collective-permute-start.16
  33.8 0.5 %collective-permute-start.17 = (bf16[256,384]{1,0:T(8,128)(2,1)S(1)}, bf16[256,384]{1,0:T(8,128)(2,1)S(1)}, u32[]{:S(2)}, u32[]{:S(2)}) collective-permute-start(bf16[256,384]{1,0:T(8,128)(2,1)S(1)} %get-tuple-element.50), channel_id=1, source_target_pairs={{0,1},{1,0},{2,3},{3,2},{4,5},{5,4},{6,7},{7,6},{8,9},{9,8},{10,11... | collective-permute-start | bytes 589832 | tf_op jit(solution)/shard_map/ppermute | solution.py:311
  34.3 0.5 %add_blocks.11.refs_0_ = f32[304,512]{1,0:T(8,128)S(1)} custom-call(bf16[304,2688]{1,0:T(8,128)(2,1)S(1)} %get-tuple-element.32.own_w, bf16[304,2688]{1,0:T(8,128)(2,1)S(1)} %get-tuple-element.33.other_w, bf16[512,384]{1,0:T(8,128)(2,1)S(1)} %collective-permute-done.7.block, ...), custom_call_target="tpu_custom_call", output_to_operand_aliasing={{}: (4, {})} | custom-call | tf_op jit(solution)/shard_map/add_blocks/pallas_call | solution.py:208
  34.8 0.0 collective-permute-done.12.other_block
  34.8 0.5 %add_blocks.12.refs_0_ = f32[304,512]{1,0:T(8,128)S(1)} custom-call(bf16[304,2688]{1,0:T(8,128)(2,1)S(1)} %get-tuple-element.32.own_w, bf16[304,2688]{1,0:T(8,128)(2,1)S(1)} %get-tuple-element.33.other_w, bf16[512,384]{1,0:T(8,128)(2,1)S(1)} %collective-permute-done.5.block, ...), custom_call_target="tpu_custom_call", output_to_operand_aliasing={{}: (4, {})} | custom-call | tf_op jit(solution)/shard_map/add_blocks/pallas_call | solution.py:208
  35.3 0.3 collective-permute-done.11.last_a
  35.7 0.0 collective-permute-start.14
  35.7 2.1 %collective-permute-done.10.last_b = bf16[256,384]{1,0:T(8,128)(2,1)S(1)} collective-permute-done((bf16[256,384]{1,0:T(8,128)(2,1)S(1)}, bf16[256,384]{1,0:T(8,128)(2,1)S(1)}, u32[]{:S(2)}, u32[]{:S(2)}) %collective-permute-start.10) | collective-permute-done | bytes 196640 | tf_op jit(solution)/shard_map/ppermute | solution.py:315
  37.8 0.0 collective-permute-start.13
  37.8 0.0 collective-permute-done.16
  37.8 0.0 collective-permute-done.17
  37.8 0.5 %add_blocks.13.before = f32[304,512]{1,0:T(8,128)S(1)} custom-call(bf16[304,2688]{1,0:T(8,128)(2,1)S(1)} %get-tuple-element.32.own_w, bf16[304,2688]{1,0:T(8,128)(2,1)S(1)} %get-tuple-element.33.other_w, bf16[512,384]{1,0:T(8,128)(2,1)S(1)} %collective-permute-done.15.block, ...), custom_call_target="tpu_custom_call", output_to_operand_aliasing={{}: (4, {})} | custom-call | tf_op jit(solution)/shard_map/add_blocks/pallas_call | solution.py:208
  38.4 0.0 collective-permute-done.14.other_a
  38.4 0.4 %add_last.1 = (bf16[304,256]{1,0:T(8,128)(2,1)S(1)}, f32[304,256]{1,0:T(8,128)S(1)}) custom-call(bf16[304,768]{1,0:T(8,128)(2,1)S(1)} %get-tuple-element.30.last_w, bf16[256,384]{1,0:T(8,128)(2,1)S(1)} %collective-permute-done.11.last_a, bf16[256,384]{1,0:T(8,128)(2,1)S(1)} %collective-permute-done.10.last_b, ...), custom_call_target="tpu_custom_call" | custom-call | tf_op jit(solution)/shard_map/add_last/pallas_call | solution.py:231
  38.8 0.4 %collective-permute-done.13.block = bf16[256,384]{1,0:T(8,128)(2,1)S(1)} collective-permute-done((bf16[256,384]{1,0:T(8,128)(2,1)S(1)}, bf16[256,384]{1,0:T(8,128)(2,1)S(1)}, u32[]{:S(2)}, u32[]{:S(2)}) %collective-permute-start.13) | collective-permute-done | bytes 196640 | tf_op jit(solution)/shard_map/ppermute | solution.py:322
  39.2 1.0 %finish.1 = bf16[304,512]{1,0:T(8,128)(2,1)} custom-call(bf16[304,768]{1,0:T(8,128)(2,1)S(1)} %get-tuple-element.30.last_w, bf16[256,384]{1,0:T(8,128)(2,1)S(1)} %collective-permute-done.13.block, bf16[304,256]{1,0:T(8,128)(2,1)S(1)} %get-tuple-element.47.done, f32[304,256]{1,0:T(8,128)S(1)} %get-tuple-element.48.rest), custom_call_target="tpu_custom_call" | custom-call | tf_op jit(solution)/shard_map/finish/pallas_call | solution.py:260
  (6 shorter events, 0.1 us)
Async XLA Ops:
  0.0 8.4 %copy-start = (bf16[6144,304]{0,1:T(8,128)(2,1)S(1)}, bf16[6144,304]{0,1:T(8,128)(2,1)}, u32[]{:S(2)}) copy-start(bf16[6144,304]{0,1:T(8,128)(2,1)} %param.7) | copy-start | bytes 11206660
  0.0 8.4 %copy-start.1 = (s32[64,2]{0,1:T(2,128)S(1)}, s32[64,2]{0,1:T(2,128)}, u32[]{:S(2)}) copy-start(s32[64,2]{0,1:T(2,128)} %param.5) | copy-start | bytes 1540
  3.6 3.2 %collective-permute-start.3 = (bf16[512,384]{1,0:T(8,128)(2,1)S(1)}, bf16[512,384]{1,0:T(8,128)(2,1)S(1)}, u32[]{:S(2)}, u32[]{:S(2)}) collective-permute-start(bf16[512,384]{1,0:T(8,128)(2,1)S(1)} %half_transform.1.block), channel_id=1, source_target_pairs={{0,1},{1,0},{2,3},{3,2},{4,5},{5,4},{6,7},{7,6},{8,9},{9,8},{10,11... | collective-permute-start | bytes 1179656 | tf_op jit(solution)/shard_map/ppermute | solution.py:284
  4.1 8.3 %collective-permute-start = (bf16[512,384]{1,0:T(8,128)(2,1)S(1)}, bf16[512,384]{1,0:T(8,128)(2,1)S(1)}, u32[]{:S(2)}, u32[]{:S(2)}) collective-permute-start(bf16[512,384]{1,0:T(8,128)(2,1)S(1)} %half_transform.1.block), channel_id=1, source_target_pairs={{0,4},{4,8},{8,12},{12,14},{14,10},{10,6},{6,2},{2,0},{5,1},{9,5},... | collective-permute-start | bytes 1179656 | tf_op jit(solution)/shard_map/ppermute | solution.py:305
  6.8 9.9 %collective-permute-start.4 = (bf16[512,384]{1,0:T(8,128)(2,1)S(1)}, bf16[512,384]{1,0:T(8,128)(2,1)S(1)}, u32[]{:S(2)}, u32[]{:S(2)}) collective-permute-start(bf16[512,384]{1,0:T(8,128)(2,1)S(1)} %collective-permute-done.3.other_block), channel_id=1, source_target_pairs={{0,4},{4,8},{8,12},{12,14},{14,10},{10,6},{6,2},{2,0},{5,1},{9,5},... | collective-permute-start | bytes 1179656 | tf_op jit(solution)/shard_map/ppermute | solution.py:305
  12.5 6.3 %collective-permute-start.2 = (bf16[512,384]{1,0:T(8,128)(2,1)S(1)}, bf16[512,384]{1,0:T(8,128)(2,1)S(1)}, u32[]{:S(2)}, u32[]{:S(2)}) collective-permute-start(bf16[512,384]{1,0:T(8,128)(2,1)S(1)} %collective-permute-done.block), channel_id=1, source_target_pairs={{0,1},{1,0},{2,3},{3,2},{4,5},{5,4},{6,7},{7,6},{8,9},{9,8},{10,11... | collective-permute-start | bytes 1179656 | tf_op jit(solution)/shard_map/ppermute | solution.py:308
  12.5 8.4 %collective-permute-start.1 = (bf16[512,384]{1,0:T(8,128)(2,1)S(1)}, bf16[512,384]{1,0:T(8,128)(2,1)S(1)}, u32[]{:S(2)}, u32[]{:S(2)}) collective-permute-start(bf16[512,384]{1,0:T(8,128)(2,1)S(1)} %collective-permute-done.block), channel_id=1, source_target_pairs={{0,4},{4,8},{8,12},{12,14},{14,10},{10,6},{6,2},{2,0},{5,1},{9,5},... | collective-permute-start | bytes 1179656 | tf_op jit(solution)/shard_map/ppermute | solution.py:305
  16.7 8.4 %collective-permute-start.7 = (bf16[512,384]{1,0:T(8,128)(2,1)S(1)}, bf16[512,384]{1,0:T(8,128)(2,1)S(1)}, u32[]{:S(2)}, u32[]{:S(2)}) collective-permute-start(bf16[512,384]{1,0:T(8,128)(2,1)S(1)} %collective-permute-done.4.block), channel_id=1, source_target_pairs={{0,4},{4,8},{8,12},{12,14},{14,10},{10,6},{6,2},{2,0},{5,1},{9,5},... | collective-permute-start | bytes 1179656 | tf_op jit(solution)/shard_map/ppermute | solution.py:305
  18.8 6.4 %collective-permute-start.8 = (bf16[512,384]{1,0:T(8,128)(2,1)S(1)}, bf16[512,384]{1,0:T(8,128)(2,1)S(1)}, u32[]{:S(2)}, u32[]{:S(2)}) collective-permute-start(bf16[512,384]{1,0:T(8,128)(2,1)S(1)} %collective-permute-done.4.block), channel_id=1, source_target_pairs={{0,1},{1,0},{2,3},{3,2},{4,5},{5,4},{6,7},{7,6},{8,9},{9,8},{10,11... | collective-permute-start | bytes 1179656 | tf_op jit(solution)/shard_map/ppermute | solution.py:308
  20.9 8.4 %collective-permute-start.5 = (bf16[512,384]{1,0:T(8,128)(2,1)S(1)}, bf16[512,384]{1,0:T(8,128)(2,1)S(1)}, u32[]{:S(2)}, u32[]{:S(2)}) collective-permute-start(bf16[512,384]{1,0:T(8,128)(2,1)S(1)} %collective-permute-done.1.block), channel_id=1, source_target_pairs={{0,4},{4,8},{8,12},{12,14},{14,10},{10,6},{6,2},{2,0},{5,1},{9,5},... | collective-permute-start | bytes 1179656 | tf_op jit(solution)/shard_map/ppermute | solution.py:305
  23.0 6.4 %collective-permute-start.6 = (bf16[512,384]{1,0:T(8,128)(2,1)S(1)}, bf16[512,384]{1,0:T(8,128)(2,1)S(1)}, u32[]{:S(2)}, u32[]{:S(2)}) collective-permute-start(bf16[512,384]{1,0:T(8,128)(2,1)S(1)} %collective-permute-done.1.block), channel_id=1, source_target_pairs={{0,1},{1,0},{2,3},{3,2},{4,5},{5,4},{6,7},{7,6},{8,9},{9,8},{10,11... | collective-permute-start | bytes 1179656 | tf_op jit(solution)/shard_map/ppermute | solution.py:308
  25.1 4.8 %collective-permute-start.9 = (bf16[512,384]{1,0:T(8,128)(2,1)S(1)}, bf16[512,384]{1,0:T(8,128)(2,1)S(1)}, u32[]{:S(2)}, u32[]{:S(2)}) collective-permute-start(bf16[512,384]{1,0:T(8,128)(2,1)S(1)} %collective-permute-done.7.block), channel_id=1, source_target_pairs={{0,1},{1,0},{2,3},{3,2},{4,5},{5,4},{6,7},{7,6},{8,9},{9,8},{10,11... | collective-permute-start | bytes 1179656 | tf_op jit(solution)/shard_map/ppermute | solution.py:308
  25.7 8.0 %collective-permute-start.15 = (bf16[512,384]{1,0:T(8,128)(2,1)S(1)}, bf16[512,384]{1,0:T(8,128)(2,1)S(1)}, u32[]{:S(2)}, u32[]{:S(2)}) collective-permute-start(bf16[512,384]{1,0:T(8,128)(2,1)S(1)} %collective-permute-done.7.block), channel_id=1, source_target_pairs={{0,4},{4,8},{8,12},{12,14},{14,10},{10,6},{6,2},{2,0},{5,1},{9,5},... | collective-permute-start | bytes 1179656 | tf_op jit(solution)/shard_map/ppermute | solution.py:305
  29.3 5.5 %collective-permute-start.12 = (bf16[512,384]{1,0:T(8,128)(2,1)S(1)}, bf16[512,384]{1,0:T(8,128)(2,1)S(1)}, u32[]{:S(2)}, u32[]{:S(2)}) collective-permute-start(bf16[512,384]{1,0:T(8,128)(2,1)S(1)} %collective-permute-done.5.block), channel_id=1, source_target_pairs={{0,1},{1,0},{2,3},{3,2},{4,5},{5,4},{6,7},{7,6},{8,9},{9,8},{10,11... | collective-permute-start | bytes 1179656 | tf_op jit(solution)/shard_map/ppermute | solution.py:308
  29.9 5.7 %collective-permute-start.11 = (bf16[256,384]{1,0:T(8,128)(2,1)S(1)}, bf16[256,384]{1,0:T(8,128)(2,1)S(1)}, u32[]{:S(2)}, u32[]{:S(2)}) collective-permute-start(bf16[256,384]{1,0:T(8,128)(2,1)S(1)} %get-tuple-element.51), channel_id=1, source_target_pairs={{0,4},{4,8},{8,12},{12,14},{14,10},{10,6},{6,2},{2,0},{5,1},{9,5},... | collective-permute-start | bytes 589832 | tf_op jit(solution)/shard_map/ppermute | solution.py:314
  32.1 5.7 %collective-permute-start.10 = (bf16[256,384]{1,0:T(8,128)(2,1)S(1)}, bf16[256,384]{1,0:T(8,128)(2,1)S(1)}, u32[]{:S(2)}, u32[]{:S(2)}) collective-permute-start(bf16[256,384]{1,0:T(8,128)(2,1)S(1)} %get-tuple-element.52), channel_id=1, source_target_pairs={{0,4},{4,8},{8,12},{12,14},{14,10},{10,6},{6,2},{2,0},{5,1},{9,5},... | collective-permute-start | bytes 589832 | tf_op jit(solution)/shard_map/ppermute | solution.py:315
  33.7 4.1 %collective-permute-start.16 = (bf16[256,384]{1,0:T(8,128)(2,1)S(1)}, bf16[256,384]{1,0:T(8,128)(2,1)S(1)}, u32[]{:S(2)}, u32[]{:S(2)}) collective-permute-start(bf16[256,384]{1,0:T(8,128)(2,1)S(1)} %get-tuple-element.49), channel_id=1, source_target_pairs={{0,1},{1,0},{2,3},{3,2},{4,5},{5,4},{6,7},{7,6},{8,9},{9,8},{10,11... | collective-permute-start | bytes 589832 | tf_op jit(solution)/shard_map/ppermute | solution.py:311
  33.8 4.0 %collective-permute-start.17 = (bf16[256,384]{1,0:T(8,128)(2,1)S(1)}, bf16[256,384]{1,0:T(8,128)(2,1)S(1)}, u32[]{:S(2)}, u32[]{:S(2)}) collective-permute-start(bf16[256,384]{1,0:T(8,128)(2,1)S(1)} %get-tuple-element.50), channel_id=1, source_target_pairs={{0,1},{1,0},{2,3},{3,2},{4,5},{5,4},{6,7},{7,6},{8,9},{9,8},{10,11... | collective-permute-start | bytes 589832 | tf_op jit(solution)/shard_map/ppermute | solution.py:311
  35.7 2.7 %collective-permute-start.14 = (bf16[256,384]{1,0:T(8,128)(2,1)S(1)}, bf16[256,384]{1,0:T(8,128)(2,1)S(1)}, u32[]{:S(2)}, u32[]{:S(2)}) collective-permute-start(bf16[256,384]{1,0:T(8,128)(2,1)S(1)} %collective-permute-done.11.last_a), channel_id=1, source_target_pairs={{0,1},{1,0},{2,3},{3,2},{4,5},{5,4},{6,7},{7,6},{8,9},{9,8},{10,11... | collective-permute-start | bytes 589832 | tf_op jit(solution)/shard_map/ppermute | solution.py:320
  37.8 1.4 %collective-permute-start.13 = (bf16[256,384]{1,0:T(8,128)(2,1)S(1)}, bf16[256,384]{1,0:T(8,128)(2,1)S(1)}, u32[]{:S(2)}, u32[]{:S(2)}) collective-permute-start(bf16[256,384]{1,0:T(8,128)(2,1)S(1)} %collective-permute-done.10.last_b), channel_id=1, source_target_pairs={{0,1},{1,0},{2,3},{3,2},{4,5},{5,4},{6,7},{7,6},{8,9},{9,8},{10,11... | collective-permute-start | bytes 589832 | tf_op jit(solution)/shard_map/ppermute | solution.py:322
